TPU v7x, 32 devices: a whole 2x2x4 slice. The times are simulated.
32 devices in a mesh: seq: 8 (over z, x), batch: 4 (over y, core).
Axes of the slice: x: 2, y: 2, z: 4, core: 2. Of those that a mesh axis runs over, the one named last changes fastest.
Arguments:
- sequence_input: bfloat16 [8192, 1536], P(('batch', 'seq')), parts along dimension 0, may hold values from -6 to 6
- conv_first: bfloat16 [5, 1536, 768], replicated, may hold values from -0.0625 to 0.0625
- conv_second: bfloat16 [5, 768, 768], replicated, may hold values from -0.09375 to 0.09375
- qkv_weight: bfloat16 [768, 1536], replicated, may hold values from -0.21875 to 0.21875
- out_weight: bfloat16 [512, 768], replicated, may hold values from -0.25 to 0.25
- logit_scale: float32 [4], replicated, may hold values from 2.5 to 30, as said below
Outputs:
- block_output: bfloat16 [8192, 768], P(('batch', 'seq')), parts along dimension 0
There are 4 independent parts, one for each index of `batch`. A program takes and returns all parts, laid end to end along the dimension named above; an argument that names none is the same for every part. Nothing has to cross between parts.
Inputs may be any that keep to these rules, and one draw needn't show every extreme that they name: `logit_scale`: one positive scale a head.
All inputs are finite; a program needn't handle non-finite values.
Results may differ from a plain program's by a relative error of at most 0.023.
Values may be sent and summed in bfloat16 or wider, within the bound.
No kernel may reach another device: no remote copies, remote signals or barrier semaphores. Data moves between devices by JAX's collectives and lax.ppermute only.
A program may use at most 256 MiB of HBM per device.

v0:
```python
import math

import jax
import jax.numpy as jnp
from jax import lax
from jax.sharding import PartitionSpec as P


def padded_2(block, sides, width):
    for axis, dim in sides:
        count = lax.axis_size(axis)
        forward = [(i, i + 1) for i in range(count - 1)]
        backward = [(target, source) for source, target in forward]
        low = lax.ppermute(
            lax.slice_in_dim(block, block.shape[dim] - width, None, axis=dim), axis, forward
        )
        high = lax.ppermute(lax.slice_in_dim(block, 0, width, axis=dim), axis, backward)
        block = jnp.concatenate([low, block, high], axis=dim)
    return block


def convolve(padded, weight, row_count):
    conv_sum = jnp.dot(padded[0:row_count], weight[0], preferred_element_type=jnp.float32)
    for offset in range(1, weight.shape[0]):
        conv_sum = conv_sum + jnp.dot(
            padded[offset : offset + row_count], weight[offset], preferred_element_type=jnp.float32
        )
    return conv_sum


def head_rms(tensor):
    return tensor * lax.rsqrt(jnp.mean(tensor * tensor, axis=-1, keepdims=True) + 1e-06)


def attend_block(state_now, queries, key_block, value_block):
    running_max, running_sum, running_out = state_now
    scores = jnp.einsum("thd,shd->hts", queries, key_block, preferred_element_type=jnp.float32)
    new_max = jnp.maximum(running_max, jnp.max(scores, axis=2))
    weights = jnp.exp(scores - new_max[:, :, None])
    running_sum = jnp.sum(weights, axis=2)
    running_out = jnp.einsum(
        "hts,shd->htd",
        weights.astype(jnp.bfloat16),
        value_block,
        preferred_element_type=jnp.float32,
    )
    return (new_max, running_sum, running_out)


def body(sequence_input, conv_first, conv_second, qkv_weight, out_weight, logit_scale):
    row_count = sequence_input.shape[0]
    padded_input = padded_2(sequence_input, (("seq", 0),), 2)
    first_out = jax.nn.gelu(convolve(padded_input, conv_first, row_count)).astype(jnp.bfloat16)
    padded_first = padded_2(first_out, (("seq", 0),), 2)
    second = convolve(padded_first, conv_second, row_count)
    hidden = (first_out.astype(jnp.float32) + second).astype(jnp.bfloat16)
    head_count = logit_scale.shape[0]
    width_all = qkv_weight.shape[1] // 3
    head_size = width_all // head_count
    query_part = jnp.dot(hidden, qkv_weight[:, :width_all], preferred_element_type=jnp.float32)
    query_part = query_part.reshape(row_count, head_count, head_size)
    queries = (head_rms(query_part) * (logit_scale / math.sqrt(head_size))[None, :, None]).astype(
        jnp.bfloat16
    )
    kv_weight = qkv_weight[:, width_all:]
    start_state = (
        jnp.full((head_count, row_count), -1e30, jnp.float32),
        jnp.zeros((head_count, row_count), jnp.float32),
        jnp.zeros((head_count, row_count, head_size), jnp.float32),
    )
    piece_rows = hidden.shape[0]
    paired = jnp.dot(hidden, kv_weight, preferred_element_type=jnp.float32)
    key_block = head_rms(paired[:, :width_all].reshape(piece_rows, head_count, head_size)).astype(
        jnp.bfloat16
    )
    value_block = (
        paired[:, width_all:].reshape(piece_rows, head_count, head_size).astype(jnp.bfloat16)
    )
    own_keys = key_block
    own_values = value_block
    flat_keys = own_keys.reshape(row_count, width_all)
    flat_values = own_values.reshape(row_count, width_all)
    piece_pair = (
        lax.all_gather(flat_keys, "seq", axis=0, tiled=True),
        lax.all_gather(flat_values, "seq", axis=0, tiled=True),
    )
    piece_rows = piece_pair[0].shape[0]
    key_block = piece_pair[0].reshape(piece_rows, head_count, head_size)
    value_block = piece_pair[1].reshape(piece_rows, head_count, head_size)
    final_state = attend_block(start_state, queries, key_block, value_block)
    running_max, running_sum, running_out = final_state
    attended = (
        (running_out / running_sum[:, :, None])
        .transpose(1, 0, 2)
        .reshape(row_count, width_all)
        .astype(jnp.bfloat16)
    )
    return (
        hidden.astype(jnp.float32)
        + jnp.dot(attended, out_weight, preferred_element_type=jnp.float32)
    ).astype(jnp.bfloat16)


def solution(mesh):
    in_specs = (P(("batch", "seq"), None), P(), P(), P(), P(), P())
    out_specs = P(("batch", "seq"), None)
    return jax.shard_map(body, mesh=mesh, in_specs=in_specs, out_specs=out_specs, check_vma=False)
```

profile of v0, /device:TPU:1, one launch (start us, length us, event | category | flops | bytes accessed | tf_op | source)
XLA Modules:
  0.0 157.2 jit_solution(1832271157804132736)
XLA Ops:
  6.5 0.8 fusion.101
  7.4 1.3 collective-permute-start.1
  8.7 4.7 %collective-permute-start = (bf16[2,1536]{1,0:T(2,128)(2,1)S(1)}, bf16[2,1536]{1,0:T(2,128)(2,1)S(1)}, u32[]{:S(2)}, u32[]{:S(2)}) collective-permute-start(bf16[2,1536]{1,0:T(2,128)(2,1)S(1)} %get-tuple-element.5), channel_id=1, source_target_pairs={{0,4},{4,8},{8,12},{12,16},{16,20},{20,24},{24,28},{1,5},{5,9},{9,... | collective-permute-start | bytes 18440 | tf_op jit(solution)/shard_map/ppermute | solution.py:14
  13.4 2.7 %fusion.9 = f32[256,768]{1,0:T(8,128)S(1)} fusion(bf16[256,1536]{1,0:T(8,128)(2,1)} %param.6, bf16[5,1536,768]{2,1,0:T(8,128)(2,1)} %param.7), kind=kOutput, calls=%fused_computation.9 | convolution fusion | flops 603979776 | bytes 3932160 | tf_op jit(solution)/shard_map/dot_general | solution.py:25
  16.2 2.5 %fusion.5 = f32[256,768]{1,0:T(8,128)S(1)} fusion(bf16[5,1536,768]{2,1,0:T(8,128)(2,1)} %param.7, bf16[258,1536]{1,0:T(8,128)(2,1)S(1)} %constant_dynamic-update-slice_fusion), kind=kOutput, calls=%fused_computation.5 | convolution fusion | flops 603979776 | bytes 3932160 | tf_op jit(solution)/shard_map/dot_general | solution.py:25
  18.7 2.5 %fusion.7 = f32[256,768]{1,0:T(8,128)S(1)} fusion(bf16[5,1536,768]{2,1,0:T(8,128)(2,1)} %param.7, bf16[258,1536]{1,0:T(8,128)(2,1)S(1)} %constant_dynamic-update-slice_fusion), kind=kOutput, calls=%fused_computation.7 | convolution fusion | flops 603979776 | bytes 3932160 | tf_op jit(solution)/shard_map/dot_general | solution.py:25
  21.2 2.6 %fusion.11 = f32[256,768]{1,0:T(8,128)S(1)} fusion(bf16[5,1536,768]{2,1,0:T(8,128)(2,1)} %param.7, bf16[256,1536]{1,0:T(8,128)(2,1)S(1)} %copy-done.3, bf16[2,1536]{1,0:T(2,128)(2,1)S(1)} %collective-permute-done), kind=kOutput, calls=%fused_computation.11 | convolution fusion | flops 605552640 | bytes 3938304 | tf_op jit(solution)/shard_map/dot_general | solution.py:25
  23.8 2.8 %fusion.77 = bf16[256,768]{1,0:T(8,128)(2,1)S(1)} fusion(f32[256,768]{1,0:T(8,128)S(1)} %fusion.5, f32[256,768]{1,0:T(8,128)S(1)} %fusion.7, f32[256,768]{1,0:T(8,128)S(1)} %fusion.9, f32[256,768]{1,0:T(8,128)S(1)} %fusion.11, bf16[5,1536,768]{2,1,0:T(8,128)(2,1)} %param.7, bf16[2,1536]{1,0:T(2,128)(2,1)S(1)} %collective-permute-done, ...), kind=kOutput, calls=%fused_computation.64 | convolution fusion | flops 608108544 | bytes 6690816 | tf_op jit(solution)/shard_map/dot_general | solution.py:23
  26.6 4.3 %collective-permute-start.2 = (bf16[2,768]{1,0:T(2,128)(2,1)S(1)}, bf16[2,768]{1,0:T(2,128)(2,1)S(1)}, u32[]{:S(2)}, u32[]{:S(2)}) collective-permute-start(bf16[2,768]{1,0:T(2,128)(2,1)S(1)} %get-tuple-element.7), channel_id=1, source_target_pairs={{0,4},{4,8},{8,12},{12,16},{16,20},{20,24},{24,28},{1,5},{5,9},{9,... | collective-permute-start | bytes 9224 | tf_op jit(solution)/shard_map/ppermute | solution.py:14
  30.9 0.5 fusion.48
  31.4 1.3 collective-permute-start.3
  32.7 0.5 fusion.50
  33.2 2.5 %collective-permute-done.3 = bf16[2,768]{1,0:T(2,128)(2,1)S(1)} collective-permute-done((bf16[2,768]{1,0:T(2,128)(2,1)S(1)}, bf16[2,768]{1,0:T(2,128)(2,1)S(1)}, u32[]{:S(2)}, u32[]{:S(2)}) %collective-permute-start.3) | collective-permute-done | bytes 3104 | tf_op jit(solution)/shard_map/ppermute | solution.py:17
  35.7 0.5 fusion.45
  36.2 0.5 fusion.33
  36.7 0.5 fusion.40
  37.2 1.1 copy-done.2
  38.4 0.6 fusion.23
  39.2 0.3 reduce_sum.28
  39.9 0.8 fusion.87
  40.9 0.7 slice.220
  41.7 1.5 fusion.85
  43.4 0.3 multiply_reduce_fusion
  43.8 0.3 multiply_convert_fusion
  44.1 47.2 %all-gather.3.cloned.1.call-done = bf16[2048,512]{1,0:T(8,128)(2,1)} async-done(((bf16[256,512]{1,0:T(8,128)(2,1)}), bf16[2048,512]{1,0:T(8,128)(2,1)}) %all-gather.3.cloned.1.call-update) | async-done | bytes 2097168 | tf_op jit(solution)/shard_map/all_gather | solution.py:84
  91.3 2.9 %fusion.103 = (f32[4,256]{1,0:T(4,128)S(1)}, f32[4,256,2048]{2,1,0:T(8,128)S(1)}) fusion(bf16[256,4,128]{2,1,0:T(4,128)(2,1)S(1)} %multiply_convert_fusion, bf16[2048,512]{1,0:T(8,128)(2,1)} %all-gather.3.cloned.1.call-done), kind=kOutput, calls=%fused_computation.102 | convolution fusion | flops 538967040 | bytes 10752000 | tf_op jit(solution)/shard_map/thd,shd->hts/dot_general | solution.py:37
  94.3 3.2 %copy-done.1 = f32[4,256,2048]{2,1,0:T(8,128)} copy-done((f32[4,256,2048]{2,1,0:T(8,128)}, f32[4,256,2048]{2,1,0:T(8,128)S(1)}, u32[]{:S(2)}) %copy-start.1) | copy-done | bytes 8388632
  97.5 1.3 fusion
  98.8 42.5 %all-gather.5.cloned.1.call-done = bf16[2048,512]{1,0:T(8,128)(2,1)} async-done(((bf16[256,512]{1,0:T(8,128)(2,1)}), bf16[2048,512]{1,0:T(8,128)(2,1)}) %all-gather.5.cloned.1.call-update) | async-done | bytes 2097168 | tf_op jit(solution)/shard_map/all_gather | solution.py:85
  141.3 2.9 %copy.21 = bf16[2048,512]{0,1:T(8,128)(2,1)S(1)} copy(bf16[2048,512]{1,0:T(8,128)(2,1)} %all-gather.5.cloned.1.call-done) | data formatting | bytes 4194304 | tf_op jit(solution)/shard_map/reshape | solution.py:89
  144.2 5.0 %fusion.61 = bf16[256,4,128]{0,2,1:T(8,128)(2,1)S(1)} fusion(bf16[2048,4,128]{0,2,1:T(8,128)(2,1)S(1)} %bitcast.72, f32[4,256,2048]{2,1,0:T(8,128)} %copy-done.1, f32[4,256]{1,0:T(4,128)S(1)} %broadcast_maximum_fusion, f32[256,4]{0,1:T(4,128)S(1)} %bitcast.77), kind=kOutput, calls=%fused_computation.53 | convolution fusion | flops 541327360 | bytes 10756096 | tf_op jit(solution)/shard_map/hts,shd->htd/dot_general | solution.py:41
  149.2 1.1 fusion.41
  (31 shorter events, 1.2 us)
Async XLA Ops:
  6.5 142.7 %copy-start = (bf16[512,768]{1,0:T(8,128)(2,1)S(1)}, bf16[512,768]{1,0:T(8,128)(2,1)}, u32[]{:S(2)}) copy-start(bf16[512,768]{1,0:T(8,128)(2,1)} %param.10) | copy-start | bytes 2359300
  6.5 84.8 %all-gather.3.cloned.1.call-start = ((), (), s32[]{:S(2)}) async-start(), calls=%async_computation | async-start | bytes 2359296 | tf_op jit(solution)/shard_map/all_gather | solution.py:84
  7.4 8.8 %collective-permute-start.1 = (bf16[2,1536]{1,0:T(2,128)(2,1)S(1)}, bf16[2,1536]{1,0:T(2,128)(2,1)S(1)}, u32[]{:S(2)}, u32[]{:S(2)}) collective-permute-start(bf16[2,1536]{1,0:T(2,128)(2,1)S(1)} %get-tuple-element.6), channel_id=1, source_target_pairs={{4,0},{8,4},{12,8},{16,12},{20,16},{24,20},{28,24},{5,1},{9,5},{13... | collective-permute-start | bytes 18440 | tf_op jit(solution)/shard_map/ppermute | solution.py:17
  8.7 7.4 %copy-start.3 = (bf16[256,1536]{1,0:T(8,128)(2,1)S(1)}, bf16[256,1536]{1,0:T(8,128)(2,1)}, u32[]{:S(2)}) copy-start(bf16[256,1536]{1,0:T(8,128)(2,1)} %param.6) | copy-start | bytes 2359300
  8.7 12.4 %collective-permute-start = (bf16[2,1536]{1,0:T(2,128)(2,1)S(1)}, bf16[2,1536]{1,0:T(2,128)(2,1)S(1)}, u32[]{:S(2)}, u32[]{:S(2)}) collective-permute-start(bf16[2,1536]{1,0:T(2,128)(2,1)S(1)} %get-tuple-element.5), channel_id=1, source_target_pairs={{0,4},{4,8},{8,12},{12,16},{16,20},{20,24},{24,28},{1,5},{5,9},{9,... | collective-permute-start | bytes 18440 | tf_op jit(solution)/shard_map/ppermute | solution.py:14
  21.1 9.7 %slice-start = ((s8[5898240]{0:T(1024)(128)(4,1)}), s8[4194304]{0:T(1024)(128)(4,1)S(1)}, s32[]{:S(2)}) async-start(s8[5898240]{0:T(1024)(128)(4,1)} %bitcast.73), calls=%async_computation.2 | async-start | bytes 8388608
  23.8 7.1 %slice-start.1 = ((s8[5898240]{0:T(1024)(128)(4,1)}), s8[1703936]{0:T(1024)(128)(4,1)S(1)}, s32[]{:S(2)}) async-start(s8[5898240]{0:T(1024)(128)(4,1)} %bitcast.73), calls=%async_computation.3 | async-start | bytes 3407872
  26.6 6.1 %collective-permute-start.2 = (bf16[2,768]{1,0:T(2,128)(2,1)S(1)}, bf16[2,768]{1,0:T(2,128)(2,1)S(1)}, u32[]{:S(2)}, u32[]{:S(2)}) collective-permute-start(bf16[2,768]{1,0:T(2,128)(2,1)S(1)} %get-tuple-element.7), channel_id=1, source_target_pairs={{0,4},{4,8},{8,12},{12,16},{16,20},{20,24},{24,28},{1,5},{5,9},{9,... | collective-permute-start | bytes 9224 | tf_op jit(solution)/shard_map/ppermute | solution.py:14
  31.4 4.3 %collective-permute-start.3 = (bf16[2,768]{1,0:T(2,128)(2,1)S(1)}, bf16[2,768]{1,0:T(2,128)(2,1)S(1)}, u32[]{:S(2)}, u32[]{:S(2)}) collective-permute-start(bf16[2,768]{1,0:T(2,128)(2,1)S(1)} %get-tuple-element.8), channel_id=1, source_target_pairs={{4,0},{8,4},{12,8},{16,12},{20,16},{24,20},{28,24},{5,1},{9,5},{13... | collective-permute-start | bytes 9224 | tf_op jit(solution)/shard_map/ppermute | solution.py:17
  36.7 1.7 %copy-start.2 = (bf16[768,1536]{1,0:T(8,128)(2,1)S(1)}, bf16[768,1536]{1,0:T(8,128)(2,1)}, u32[]{:S(2)}) copy-start(bf16[768,1536]{1,0:T(8,128)(2,1)} %param.9) | copy-start | bytes 7077892
  39.0 2.7 %copy-start.4 = (f32[4]{0:T(128)S(1)}, f32[4]{0:T(128)}, u32[]{:S(2)}) copy-start(f32[4]{0:T(128)} %param.11) | copy-start | bytes 52
  40.7 100.6 %all-gather.5.cloned.1.call-start = ((), (), s32[]{:S(2)}) async-start(), calls=%async_computation.1 | async-start | bytes 2359296 | tf_op jit(solution)/shard_map/all_gather | solution.py:85
  94.3 3.2 %copy-start.1 = (f32[4,256,2048]{2,1,0:T(8,128)}, f32[4,256,2048]{2,1,0:T(8,128)S(1)}, u32[]{:S(2)}) copy-start(f32[4,256,2048]{2,1,0:T(8,128)S(1)} %get-tuple-element.10) | copy-start | bytes 25165828
Sparse Core Ops, SparseCore 0:
  40.8 50.4 all-gather.2
  93.5 47.7 all-gather.4
where the time goes:
time: 159 us; the launch traced here: 157 us
  waiting for transfers between devices  92.2 us (58%)
  matrix products  26.6 us (17%)
  between operations  13.8 us (9%)
  starting transfers between devices  11.8 us (7%)
  local copies, waits for them, and re-layouts  9.65 us (6%)
  other arithmetic  3.2 us (2%)
    all_gather x1, waiting for transfers between devices, body(): lax.all_gather(flat_keys, 'seq', axis=0, tiled=True)  47.2 us
    all_gather x1, waiting for transfers between devices, body(): lax.all_gather(flat_values, 'seq', axis=0, tiled=True)  42.5 us
    dot_general x8, matrix products, convolve(): jnp.dot(padded[offset:offset + row_count], weight[offset], preferred_elem...  12.2 us
    ppermute x2, starting transfers between devices, padded_2(): lax.ppermute(lax.slice_in_dim(block, block.shape[dim] - width, None, axis...  8.97 us
    dot_general x1, matrix products, attend_block(): jnp.einsum('hts,shd->htd', weights.astype(jnp.bfloat16), value_block, pre...  5.01 us
    unnamed x15, local copies, waits for them, and re-layouts  4.43 us
    dot_general x2, matrix products, convolve(): jnp.dot(padded[0:row_count], weight[0], preferred_element_type=jnp.float32)  3.26 us
  transfers between devices with their start and end apart: 6, of which 3 were waited for; matrix products, arithmetic and copies ran while one was open for 10% of the time, Pallas kernels for 0%

commit v1 on v0

v1 whole, which is shorter than its diff:
```python
import functools
import math

import jax
import jax.numpy as jnp
from jax import lax
from jax.experimental import pallas as pl
from jax.experimental.pallas import tpu as pltpu
from jax.sharding import PartitionSpec as P

F32 = jnp.float32
BF16 = jnp.bfloat16
EDGE = 8
TAPS = 5
MIB = 1 << 20


def head_rms(tensor):
    return tensor * lax.rsqrt(jnp.mean(tensor * tensor, axis=-1, keepdims=True) + 1e-06)


def edge_rows(block):
    count = lax.axis_size("seq")
    forward = [(i, i + 1) for i in range(count - 1)]
    backward = [(target, source) for source, target in forward]
    before = lax.ppermute(block[block.shape[0] - EDGE :], "seq", forward)
    after = lax.ppermute(block[:EDGE], "seq", backward)
    return after, before


def stem_kernel(
    place, x_ref, after_ref, before_ref, w1_hbm, w2_hbm, wqkv_hbm, scale_ref, *rest, heads, head
):
    hidden_ref, units = rest[0], rest[1 : 1 + heads]
    w1, w2, wqkv, xp, fp, total, projected, sems = rest[1 + heads :]
    rows = x_ref.shape[0]
    circle = rows + 2 * EDGE
    width = heads * head
    copies = []
    for j in range(TAPS):
        copies.append(pltpu.make_async_copy(w1_hbm.at[j], w1.at[j], sems.at[j]))
    for j in range(TAPS):
        copies.append(pltpu.make_async_copy(w2_hbm.at[j], w2.at[j], sems.at[TAPS + j]))
    copies.append(pltpu.make_async_copy(wqkv_hbm, wqkv, sems.at[2 * TAPS]))
    for copy in copies:
        copy.start()

    def rolled(product, j):
        shift = (TAPS // 2 - j) % circle
        return product if shift == 0 else pltpu.roll(product, shift, 0)

    xp[0:rows] = x_ref[...]
    xp[rows:circle] = jnp.concatenate(
        [after_ref[...].astype(F32), before_ref[...].astype(F32)], axis=0
    ).astype(BF16)
    for j in range(TAPS):
        copies[j].wait()
        product = rolled(jnp.dot(xp[...], w1[j], preferred_element_type=F32), j)
        if j == 0:
            total[...] = product
        else:
            total[...] += product
    fp[0:rows] = jax.nn.gelu(total[0:rows]).astype(BF16)
    has_before = place[0].astype(F32)
    has_after = place[1].astype(F32)
    fp[rows:circle] = jnp.concatenate(
        [
            jax.nn.gelu(total[rows : rows + EDGE]) * has_after,
            jax.nn.gelu(total[rows + EDGE : circle]) * has_before,
        ],
        axis=0,
    ).astype(BF16)
    for j in range(TAPS):
        copies[TAPS + j].wait()
        product = rolled(jnp.dot(fp[...], w2[j], preferred_element_type=F32), j)
        if j == 0:
            total[...] = product
        else:
            total[...] += product
    hidden = (fp[0:rows].astype(F32) + total[0:rows]).astype(BF16)
    hidden_ref[...] = hidden
    copies[2 * TAPS].wait()
    projected[...] = jnp.dot(hidden, wqkv[...], preferred_element_type=F32)
    for r in range(heads):
        h = place[2 + r]
        at = pl.multiple_of(h * head, head)
        q = head_rms(projected[:, pl.ds(at, head)]) * (scale_ref[h] / math.sqrt(head))
        k = head_rms(projected[:, pl.ds(width + at, head)])
        units[r][:, 0:head] = q.astype(BF16)
        units[r][:, head : 2 * head] = k.astype(BF16)
        units[r][:, 2 * head :] = projected[:, pl.ds(2 * width + at, head)].astype(BF16)


def stem(place, block, after, before, conv_first, conv_second, qkv_weight, logit_scale):
    rows, channels = block.shape
    width = conv_first.shape[2]
    heads = logit_scale.shape[0]
    head = qkv_weight.shape[1] // 3 // heads
    circle = rows + 2 * EDGE
    vmem = pl.BlockSpec(memory_space=pltpu.VMEM)
    smem = pl.BlockSpec(memory_space=pltpu.SMEM)
    hbm = pl.BlockSpec(memory_space=pl.ANY)
    return pl.pallas_call(
        functools.partial(stem_kernel, heads=heads, head=head),
        out_shape=[jax.ShapeDtypeStruct((rows, width), BF16)]
        + [jax.ShapeDtypeStruct((rows, 3 * head), BF16)] * heads,
        in_specs=[smem, vmem, vmem, vmem, hbm, hbm, hbm, smem],
        out_specs=[vmem] * (1 + heads),
        scratch_shapes=[
            pltpu.VMEM(conv_first.shape, BF16),
            pltpu.VMEM(conv_second.shape, BF16),
            pltpu.VMEM(qkv_weight.shape, BF16),
            pltpu.VMEM((circle, channels), BF16),
            pltpu.VMEM((circle, width), BF16),
            pltpu.VMEM((circle, width), F32),
            pltpu.VMEM((rows, qkv_weight.shape[1]), F32),
            pltpu.SemaphoreType.DMA((2 * TAPS + 1,)),
        ],
        compiler_params=pltpu.CompilerParams(vmem_limit_bytes=48 * MIB),
        name="stem",
    )(place, block, after, before, conv_first, conv_second, qkv_weight, logit_scale)


def attend_kernel(*refs, head, count):
    own, other, outs = refs[:count], refs[count : 2 * count], refs[2 * count : 3 * count]
    keys, values = refs[3 * count :]
    rows = own[0].shape[0]
    for i in range(count):
        keys[i * rows : (i + 1) * rows] = own[i][:, head : 2 * head]
        values[i * rows : (i + 1) * rows] = own[i][:, 2 * head :]
        keys[(count + i) * rows : (count + i + 1) * rows] = other[i][:, head : 2 * head]
        values[(count + i) * rows : (count + i + 1) * rows] = other[i][:, 2 * head :]
    for i in range(count):
        scores = lax.dot_general(
            own[i][:, 0:head],
            keys[...],
            (((1,), (1,)), ((), ())),
            preferred_element_type=F32,
        )
        weights = jnp.exp(scores - jnp.max(scores, axis=1, keepdims=True))
        denominators = jnp.sum(weights, axis=1, keepdims=True)
        mixed = jnp.dot(weights.astype(BF16), values[...], preferred_element_type=F32)
        outs[i][...] = (mixed / denominators).astype(BF16)


def attend(own, other):
    count = len(own)
    rows, wide = own[0].shape
    head = wide // 3
    vmem = pl.BlockSpec(memory_space=pltpu.VMEM)
    return pl.pallas_call(
        functools.partial(attend_kernel, head=head, count=count),
        out_shape=[jax.ShapeDtypeStruct((rows, head), BF16)] * count,
        in_specs=[vmem] * (2 * count),
        out_specs=[vmem] * count,
        scratch_shapes=[
            pltpu.VMEM((2 * count * rows, head), BF16),
            pltpu.VMEM((2 * count * rows, head), BF16),
        ],
        compiler_params=pltpu.CompilerParams(vmem_limit_bytes=32 * MIB),
        name="attend",
    )(*own, *other)


def finish_kernel(place, hidden_ref, weight_ref, *rest):
    mixed, out_ref = rest[:-1], rest[-1]
    head = mixed[0].shape[1]
    total = hidden_ref[...].astype(F32)
    for r in range(len(mixed)):
        at = pl.multiple_of(place[2 + r] * head, head)
        total += jnp.dot(
            mixed[r][...], weight_ref[pl.ds(at, head), :], preferred_element_type=F32
        )
    out_ref[...] = total.astype(out_ref.dtype)


def finish(place, hidden, out_weight, mixed):
    vmem = pl.BlockSpec(memory_space=pltpu.VMEM)
    smem = pl.BlockSpec(memory_space=pltpu.SMEM)
    return pl.pallas_call(
        finish_kernel,
        out_shape=jax.ShapeDtypeStruct(hidden.shape, BF16),
        in_specs=[smem] + [vmem] * (2 + len(mixed)),
        out_specs=vmem,
        compiler_params=pltpu.CompilerParams(vmem_limit_bytes=32 * MIB),
        name="finish",
    )(place, hidden, out_weight, *mixed)


def routes(seq_count, batch_count, heads):
    rounds = []
    for r in range(heads):
        pairs = []
        for g in range(seq_count):
            for b in range(batch_count):
                chip = heads * (b % 2) + (r ^ (g % heads))
                target = chip * batch_count + b - b % 2 + g // heads
                pairs.append((g * batch_count + b, target))
        rounds.append(pairs)
    return rounds


def by_heads(sequence_input, conv_first, conv_second, qkv_weight, out_weight, logit_scale):
    heads = logit_scale.shape[0]
    count = lax.axis_size("seq")
    batch_count = lax.axis_size("batch")
    g = lax.axis_index("seq")
    place = jnp.stack(
        [(g > 0).astype(jnp.int32), (g < count - 1).astype(jnp.int32)]
        + [(r ^ (g % heads)).astype(jnp.int32) for r in range(heads)]
    )
    after, before = edge_rows(sequence_input)
    hidden, *units = stem(
        place, sequence_input, after, before, conv_first, conv_second, qkv_weight, logit_scale
    )
    both = ("seq", "batch")
    rounds = routes(count, batch_count, heads)
    own = [lax.ppermute(unit, both, pairs) for unit, pairs in zip(units, rounds)]
    cores = [(b, b ^ 1) for b in range(batch_count)]
    other = [lax.ppermute(unit, "batch", cores) for unit in own]
    outs = attend(own, other)
    mixed = [
        lax.ppermute(out, both, [(target, source) for source, target in pairs])
        for out, pairs in zip(outs, rounds)
    ]
    return finish(place, hidden, out_weight, mixed)


def by_gather(sequence_input, conv_first, conv_second, qkv_weight, out_weight, logit_scale):
    heads = logit_scale.shape[0]
    count = lax.axis_size("seq")
    g = lax.axis_index("seq")
    place = jnp.stack(
        [(g > 0).astype(jnp.int32), (g < count - 1).astype(jnp.int32)]
        + [jnp.int32(r) for r in range(heads)]
    )
    after, before = edge_rows(sequence_input)
    hidden, *units = stem(
        place, sequence_input, after, before, conv_first, conv_second, qkv_weight, logit_scale
    )
    head = units[0].shape[1] // 3
    pairs = jnp.concatenate([unit[:, head:] for unit in units], axis=1)
    everywhere = lax.all_gather(pairs, "seq", axis=0, tiled=True)
    mixed = []
    for h in range(heads):
        at = 2 * h * head
        scores = lax.dot_general(
            units[h][:, :head],
            everywhere[:, at : at + head],
            (((1,), (1,)), ((), ())),
            preferred_element_type=F32,
        )
        weights = jnp.exp(scores - jnp.max(scores, axis=1, keepdims=True))
        denominators = jnp.sum(weights, axis=1, keepdims=True)
        out = jnp.dot(
            weights.astype(BF16),
            everywhere[:, at + head : at + 2 * head],
            preferred_element_type=F32,
        )
        mixed.append((out / denominators).astype(BF16))
    return finish(place, hidden, out_weight, mixed)


def solution(mesh):
    def body(*args):
        heads = args[-1].shape[0]
        fits = mesh.shape["seq"] == 2 * heads and mesh.shape["batch"] % 2 == 0
        return (by_heads if fits and heads & (heads - 1) == 0 else by_gather)(*args)

    in_specs = (P(("batch", "seq"), None), P(), P(), P(), P(), P())
    out_specs = P(("batch", "seq"), None)
    return jax.shard_map(body, mesh=mesh, in_specs=in_specs, out_specs=out_specs, check_vma=False)
```

time: 159 us -> 68.8 us (0.43)
  waiting for transfers between devices: 92.2 us -> 18.1 us
  matrix products: 26.6 us -> 0 us
  Pallas kernels: 0 us -> 17.2 us
  starting transfers between devices: 11.8 us -> 28.8 us
  between operations: 13.8 us -> 0.08 us
  local copies, waits for them, and re-layouts: 9.65 us -> 4.3 us
  other arithmetic: 3.2 us -> 0 us
    all_gather x2 -> x0, waiting for transfers between devices: 89.7 us -> none  [the longest x1 47.2 us: body(): lax.all_gather(flat_keys, 'seq', axis=0, tiled=True)]
    dot_general x15 -> x0, matrix products: 26.6 us -> none  [the longest x8 12.2 us: convolve(): jnp.dot(padded[offset:offset + row_count], weight[offset], preferred_elem...]
    pallas_call x0 -> x3, Pallas kernels: none -> 17.2 us  [the longest x1 12 us: stem(): pl.pallas_call(functools.partial(stem_kernel, heads=heads, head=head), ou...]
    ppermute x4 -> x14, starting transfers between devices: 11.6 us -> 28.8 us  [the longest x4 11.8 us: by_heads(): lax.ppermute(unit, both, pairs)]
    ppermute x4 -> x14, waiting for transfers between devices: 2.54 us -> 18.1 us  [the longest x4 9.9 us: by_heads(): lax.ppermute(unit, both, pairs)]
    reshape x2 -> x0, local copies, waits for them, and re-layouts: 3.11 us -> none  [the longest x1 2.93 us: body(): value_block = piece_pair[1].reshape(piece_rows, head_count, head_size)]
    reduce_sum x3 -> x0, other arithmetic: 1.98 us -> none  [the longest x1 1.3 us: attend_block(): running_sum = jnp.sum(weights, axis=2)]
    unnamed x15 -> x8, local copies, waits for them, and re-layouts: 4.43 us -> 3.46 us
  transfers between devices with their start and end apart: 6 -> 14, of which waited for: 3 -> 8; matrix products, arithmetic and copies ran while one was open for 10% -> 0% of each run, Pallas kernels for 0% -> 0%
where the time goes in v1:
time: 68.8 us; the launch traced here: 68.5 us
  starting transfers between devices  28.8 us (42%)
  waiting for transfers between devices  18.1 us (26%)
  Pallas kernels  17.2 us (25%)
  local copies, waits for them, and re-layouts  4.3 us (6%)
    pallas_call x1, Pallas kernels, stem(): pl.pallas_call(functools.partial(stem_kernel, heads=heads, head=head), ou...  12 us
    ppermute x4, starting transfers between devices, by_heads(): lax.ppermute(unit, both, pairs)  11.8 us
    ppermute x4, starting transfers between devices, by_heads(): lax.ppermute(out, both, [(target, source) for source, target in pairs])  11.2 us
    ppermute x4, waiting for transfers between devices, by_heads(): lax.ppermute(unit, both, pairs)  9.9 us
    ppermute x1, starting transfers between devices, edge_rows(): before = lax.ppermute(block[block.shape[0] - EDGE:], 'seq', forward)  3.93 us
    ppermute x4, waiting for transfers between devices, by_heads(): lax.ppermute(out, both, [(target, source) for source, target in pairs])  3.6 us
    unnamed x8, local copies, waits for them, and re-layouts  3.46 us
    pallas_call x1, Pallas kernels, attend(): pl.pallas_call(functools.partial(attend_kernel, head=head, count=count),...  3.37 us
  transfers between devices with their start and end apart: 14, of which 8 were waited for; matrix products, arithmetic and copies ran while one was open for 0% of the time, Pallas kernels for 0%

profile of v1, /device:TPU:1, one launch (start us, length us, event | category | flops | bytes accessed | tf_op | source)
XLA Modules:
  0.0 68.5 jit_solution(10866604411786390681)
XLA Ops:
  0.0 0.8 %fusion = (bf16[8,1536]{1,0:T(8,128)(2,1)S(1)}, bf16[8,1536]{1,0:T(8,128)(2,1)S(1)}) fusion(bf16[256,1536]{1,0:T(8,128)(2,1)} %x_ref.1), kind=kLoop, calls=%fused_computation | loop fusion | bytes 98304 | tf_op jit(solution)/shard_map/slice | solution.py:26
  0.8 3.9 %collective-permute-start.1 = (bf16[8,1536]{1,0:T(8,128)(2,1)S(1)}, bf16[8,1536]{1,0:T(8,128)(2,1)S(1)}, u32[]{:S(2)}, u32[]{:S(2)}) collective-permute-start(bf16[8,1536]{1,0:T(8,128)(2,1)S(1)} %get-tuple-element.23), channel_id=1, source_target_pairs={{0,4},{4,8},{8,12},{12,16},{16,20},{20,24},{24,28},{1,5},{5,9},{9,... | collective-permute-start | bytes 73736 | tf_op jit(solution)/shard_map/ppermute | solution.py:26
  4.7 1.3 %collective-permute-start = (bf16[8,1536]{1,0:T(8,128)(2,1)S(1)}, bf16[8,1536]{1,0:T(8,128)(2,1)S(1)}, u32[]{:S(2)}, u32[]{:S(2)}) collective-permute-start(bf16[8,1536]{1,0:T(8,128)(2,1)S(1)} %get-tuple-element.24), channel_id=1, source_target_pairs={{4,0},{8,4},{12,8},{16,12},{20,16},{24,20},{28,24},{5,1},{9,5},{13... | collective-permute-start | bytes 73736 | tf_op jit(solution)/shard_map/ppermute | solution.py:27
  6.0 0.1 stack.35.place
  6.1 3.2 %collective-permute-done.after_ref = bf16[8,1536]{1,0:T(8,128)(2,1)S(1)} collective-permute-done((bf16[8,1536]{1,0:T(8,128)(2,1)S(1)}, bf16[8,1536]{1,0:T(8,128)(2,1)S(1)}, u32[]{:S(2)}, u32[]{:S(2)}) %collective-permute-start) | collective-permute-done | bytes 24608 | tf_op jit(solution)/shard_map/ppermute | solution.py:27
  9.3 1.7 %copy-done = bf16[768,1536]{1,0:T(8,128)(2,1)S(1)} copy-done((bf16[768,1536]{1,0:T(8,128)(2,1)S(1)}, bf16[768,1536]{1,0:T(8,128)(2,1)}, u32[]{:S(2)}) %copy-start) | copy-done | bytes 2359320
  10.9 1.1 %copy-done.1 = bf16[256,1536]{1,0:T(8,128)(2,1)S(1)} copy-done((bf16[256,1536]{1,0:T(8,128)(2,1)S(1)}, bf16[256,1536]{1,0:T(8,128)(2,1)}, u32[]{:S(2)}) %copy-start.1) | copy-done | bytes 786456
  12.1 0.7 copy-done.3
  12.7 12.0 %stem.1 = (bf16[256,768]{1,0:T(8,128)(2,1)S(1)}, bf16[256,384]{1,0:T(8,128)(2,1)S(1)}, bf16[256,384]{1,0:T(8,128)(2,1)S(1)}, bf16[256,384]{1,0:T(8,128)(2,1)S(1)}, bf16[256,384]{1,0:T(8,128)(2,1)S(1)}) custom-call(s32[6]{0:T(128)S(1)} %stack.35.place, bf16[256,1536]{1,0:T(8,128)(2,1)S(1)} %copy-done.1, bf16[8,1536]{1,0:T(8,128)(2,1)S(1)} %collective-permute-done.after_ref, ...), custom_call_target="tpu_custom_call" | custom-call | tf_op jit(solution)/shard_map/stem/pallas_call | solution.py:103
  24.8 6.2 %collective-permute-start.2 = (bf16[256,384]{1,0:T(8,128)(2,1)S(1)}, bf16[256,384]{1,0:T(8,128)(2,1)S(1)}, u32[]{:S(2)}, u32[]{:S(2)}) collective-permute-start(bf16[256,384]{1,0:T(8,128)(2,1)S(1)} %get-tuple-element.15), channel_id=1, source_target_pairs={{0,0},{1,16},{2,2},{3,18},{4,4},{5,20},{6,6},{7,22},{8,8},{9,24},{... | collective-permute-start | bytes 589832 | tf_op jit(solution)/shard_map/ppermute | solution.py:218
  31.0 2.0 %collective-permute-start.3 = (bf16[256,384]{1,0:T(8,128)(2,1)S(1)}, bf16[256,384]{1,0:T(8,128)(2,1)S(1)}, u32[]{:S(2)}, u32[]{:S(2)}) collective-permute-start(bf16[256,384]{1,0:T(8,128)(2,1)S(1)} %get-tuple-element.16), channel_id=1, source_target_pairs={{0,4},{1,20},{2,6},{3,22},{4,0},{5,16},{6,2},{7,18},{8,12},{9,28},... | collective-permute-start | bytes 589832 | tf_op jit(solution)/shard_map/ppermute | solution.py:218
  32.9 0.9 %collective-permute-start.4 = (bf16[256,384]{1,0:T(8,128)(2,1)S(1)}, bf16[256,384]{1,0:T(8,128)(2,1)S(1)}, u32[]{:S(2)}, u32[]{:S(2)}) collective-permute-start(bf16[256,384]{1,0:T(8,128)(2,1)S(1)} %get-tuple-element.17), channel_id=1, source_target_pairs={{0,8},{1,24},{2,10},{3,26},{4,12},{5,28},{6,14},{7,30},{8,0},{9,16... | collective-permute-start | bytes 589832 | tf_op jit(solution)/shard_map/ppermute | solution.py:218
  33.8 2.7 %collective-permute-start.5 = (bf16[256,384]{1,0:T(8,128)(2,1)S(1)}, bf16[256,384]{1,0:T(8,128)(2,1)S(1)}, u32[]{:S(2)}, u32[]{:S(2)}) collective-permute-start(bf16[256,384]{1,0:T(8,128)(2,1)S(1)} %get-tuple-element.18), channel_id=1, source_target_pairs={{0,12},{1,28},{2,14},{3,30},{4,8},{5,24},{6,10},{7,26},{8,4},{9,20... | collective-permute-start | bytes 589832 | tf_op jit(solution)/shard_map/ppermute | solution.py:218
  36.5 0.0 collective-permute-done.2.refs_0_
  36.5 0.0 collective-permute-start.6
  36.5 9.9 %collective-permute-done.3.refs_1_ = bf16[256,384]{1,0:T(8,128)(2,1)S(1)} collective-permute-done((bf16[256,384]{1,0:T(8,128)(2,1)S(1)}, bf16[256,384]{1,0:T(8,128)(2,1)S(1)}, u32[]{:S(2)}, u32[]{:S(2)}) %collective-permute-start.3) | collective-permute-done | bytes 196640 | tf_op jit(solution)/shard_map/ppermute | solution.py:218
  46.4 0.0 collective-permute-done.4.refs_2_
  46.4 0.5 collective-permute-start.8
  46.9 0.0 collective-permute-done.5.refs_3_
  46.9 0.1 collective-permute-start.9
  47.0 0.9 %collective-permute-done.7.refs_5_ = bf16[256,384]{1,0:T(8,128)(2,1)S(1)} collective-permute-done((bf16[256,384]{1,0:T(8,128)(2,1)S(1)}, bf16[256,384]{1,0:T(8,128)(2,1)S(1)}, u32[]{:S(2)}, u32[]{:S(2)}) %collective-permute-start.7) | collective-permute-done | bytes 196640 | tf_op jit(solution)/shard_map/ppermute | solution.py:220
  47.9 0.3 collective-permute-done.8.refs_6_
  48.2 0.3 collective-permute-done.9.refs_7_
  48.4 3.4 %attend.1 = (bf16[256,128]{1,0:T(8,128)(2,1)S(1)}, bf16[256,128]{1,0:T(8,128)(2,1)S(1)}, bf16[256,128]{1,0:T(8,128)(2,1)S(1)}, bf16[256,128]{1,0:T(8,128)(2,1)S(1)}) custom-call(bf16[256,384]{1,0:T(8,128)(2,1)S(1)} %collective-permute-done.2.refs_0_, bf16[256,384]{1,0:T(8,128)(2,1)S(1)} %collective-permute-done.3.refs_1_, ...), custom_call_target="tpu_custom_call" | custom-call | tf_op jit(solution)/shard_map/attend/pallas_call | solution.py:151
  51.8 5.9 %collective-permute-start.10 = (bf16[256,128]{1,0:T(8,128)(2,1)S(1)}, bf16[256,128]{1,0:T(8,128)(2,1)S(1)}, u32[]{:S(2)}, u32[]{:S(2)}) collective-permute-start(bf16[256,128]{1,0:T(8,128)(2,1)S(1)} %get-tuple-element.19), channel_id=1, source_target_pairs={{0,0},{16,1},{2,2},{18,3},{4,4},{20,5},{6,6},{22,7},{8,8},{24,9},{... | collective-permute-start | bytes 196616 | tf_op jit(solution)/shard_map/ppermute | solution.py:223
  57.7 1.7 %collective-permute-start.11 = (bf16[256,128]{1,0:T(8,128)(2,1)S(1)}, bf16[256,128]{1,0:T(8,128)(2,1)S(1)}, u32[]{:S(2)}, u32[]{:S(2)}) collective-permute-start(bf16[256,128]{1,0:T(8,128)(2,1)S(1)} %get-tuple-element.20), channel_id=1, source_target_pairs={{4,0},{20,1},{6,2},{22,3},{0,4},{16,5},{2,6},{18,7},{12,8},{28,9},... | collective-permute-start | bytes 196616 | tf_op jit(solution)/shard_map/ppermute | solution.py:223
  59.4 0.8 %collective-permute-start.12 = (bf16[256,128]{1,0:T(8,128)(2,1)S(1)}, bf16[256,128]{1,0:T(8,128)(2,1)S(1)}, u32[]{:S(2)}, u32[]{:S(2)}) collective-permute-start(bf16[256,128]{1,0:T(8,128)(2,1)S(1)} %get-tuple-element.21), channel_id=1, source_target_pairs={{8,0},{24,1},{10,2},{26,3},{12,4},{28,5},{14,6},{30,7},{0,8},{16,9... | collective-permute-start | bytes 196616 | tf_op jit(solution)/shard_map/ppermute | solution.py:223
  60.2 2.8 %collective-permute-start.13 = (bf16[256,128]{1,0:T(8,128)(2,1)S(1)}, bf16[256,128]{1,0:T(8,128)(2,1)S(1)}, u32[]{:S(2)}, u32[]{:S(2)}) collective-permute-start(bf16[256,128]{1,0:T(8,128)(2,1)S(1)} %get-tuple-element.22), channel_id=1, source_target_pairs={{12,0},{28,1},{14,2},{30,3},{8,4},{24,5},{10,6},{26,7},{4,8},{20,9... | collective-permute-start | bytes 196616 | tf_op jit(solution)/shard_map/ppermute | solution.py:223
  63.0 1.0 %collective-permute-done.11.rest_1_ = bf16[256,128]{1,0:T(8,128)(2,1)S(1)} collective-permute-done((bf16[256,128]{1,0:T(8,128)(2,1)S(1)}, bf16[256,128]{1,0:T(8,128)(2,1)S(1)}, u32[]{:S(2)}, u32[]{:S(2)}) %collective-permute-start.11) | collective-permute-done | bytes 65568 | tf_op jit(solution)/shard_map/ppermute | solution.py:223
  64.0 1.0 %collective-permute-done.12.rest_2_ = bf16[256,128]{1,0:T(8,128)(2,1)S(1)} collective-permute-done((bf16[256,128]{1,0:T(8,128)(2,1)S(1)}, bf16[256,128]{1,0:T(8,128)(2,1)S(1)}, u32[]{:S(2)}, u32[]{:S(2)}) %collective-permute-start.12) | collective-permute-done | bytes 65568 | tf_op jit(solution)/shard_map/ppermute | solution.py:223
  65.0 1.6 %collective-permute-done.13.rest_3_ = bf16[256,128]{1,0:T(8,128)(2,1)S(1)} collective-permute-done((bf16[256,128]{1,0:T(8,128)(2,1)S(1)}, bf16[256,128]{1,0:T(8,128)(2,1)S(1)}, u32[]{:S(2)}, u32[]{:S(2)}) %collective-permute-start.13) | collective-permute-done | bytes 65568 | tf_op jit(solution)/shard_map/ppermute | solution.py:223
  66.6 1.9 %finish.1 = bf16[256,768]{1,0:T(8,128)(2,1)} custom-call(s32[6]{0:T(128)S(1)} %stack.35.place, bf16[256,768]{1,0:T(8,128)(2,1)S(1)} %get-tuple-element.14.hidden_ref, bf16[512,768]{1,0:T(8,128)(2,1)S(1)} %copy-done.2, bf16[256,128]{1,0:T(8,128)(2,1)S(1)} %collective-permute-done.10.rest_0_, bf16[256,128]{1,0:T(8,128)(2,1)S(1)} %collective-permute-done.11.rest_1_, ...), custom_call_target="tpu_custom_call" | custom-call | tf_op jit(solution)/shard_map/finish/pallas_call | solution.py:180
  (9 shorter events, 0.0 us)
Async XLA Ops:
  0.8 5.3 %collective-permute-start.1 = (bf16[8,1536]{1,0:T(8,128)(2,1)S(1)}, bf16[8,1536]{1,0:T(8,128)(2,1)S(1)}, u32[]{:S(2)}, u32[]{:S(2)}) collective-permute-start(bf16[8,1536]{1,0:T(8,128)(2,1)S(1)} %get-tuple-element.23), channel_id=1, source_target_pairs={{0,4},{4,8},{8,12},{12,16},{16,20},{20,24},{24,28},{1,5},{5,9},{9,... | collective-permute-start | bytes 73736 | tf_op jit(solution)/shard_map/ppermute | solution.py:26
  4.7 4.6 %collective-permute-start = (bf16[8,1536]{1,0:T(8,128)(2,1)S(1)}, bf16[8,1536]{1,0:T(8,128)(2,1)S(1)}, u32[]{:S(2)}, u32[]{:S(2)}) collective-permute-start(bf16[8,1536]{1,0:T(8,128)(2,1)S(1)} %get-tuple-element.24), channel_id=1, source_target_pairs={{4,0},{8,4},{12,8},{16,12},{20,16},{24,20},{28,24},{5,1},{9,5},{13... | collective-permute-start | bytes 73736 | tf_op jit(solution)/shard_map/ppermute | solution.py:27
  9.3 1.7 %copy-start = (bf16[768,1536]{1,0:T(8,128)(2,1)S(1)}, bf16[768,1536]{1,0:T(8,128)(2,1)}, u32[]{:S(2)}) copy-start(bf16[768,1536]{1,0:T(8,128)(2,1)} %wqkv_hbm.1) | copy-start | bytes 7077892
  10.9 1.1 %copy-start.1 = (bf16[256,1536]{1,0:T(8,128)(2,1)S(1)}, bf16[256,1536]{1,0:T(8,128)(2,1)}, u32[]{:S(2)}) copy-start(bf16[256,1536]{1,0:T(8,128)(2,1)} %x_ref.1) | copy-start | bytes 2359300
  12.1 0.7 copy-start.3
  12.7 53.9 %copy-start.2 = (bf16[512,768]{1,0:T(8,128)(2,1)S(1)}, bf16[512,768]{1,0:T(8,128)(2,1)}, u32[]{:S(2)}) copy-start(bf16[512,768]{1,0:T(8,128)(2,1)} %weight_ref.1) | copy-start | bytes 2359300
  24.8 11.8 %collective-permute-start.2 = (bf16[256,384]{1,0:T(8,128)(2,1)S(1)}, bf16[256,384]{1,0:T(8,128)(2,1)S(1)}, u32[]{:S(2)}, u32[]{:S(2)}) collective-permute-start(bf16[256,384]{1,0:T(8,128)(2,1)S(1)} %get-tuple-element.15), channel_id=1, source_target_pairs={{0,0},{1,16},{2,2},{3,18},{4,4},{5,20},{6,6},{7,22},{8,8},{9,24},{... | collective-permute-start | bytes 589832 | tf_op jit(solution)/shard_map/ppermute | solution.py:218
  31.0 15.5 %collective-permute-start.3 = (bf16[256,384]{1,0:T(8,128)(2,1)S(1)}, bf16[256,384]{1,0:T(8,128)(2,1)S(1)}, u32[]{:S(2)}, u32[]{:S(2)}) collective-permute-start(bf16[256,384]{1,0:T(8,128)(2,1)S(1)} %get-tuple-element.16), channel_id=1, source_target_pairs={{0,4},{1,20},{2,6},{3,22},{4,0},{5,16},{6,2},{7,18},{8,12},{9,28},... | collective-permute-start | bytes 589832 | tf_op jit(solution)/shard_map/ppermute | solution.py:218
  32.9 13.5 %collective-permute-start.4 = (bf16[256,384]{1,0:T(8,128)(2,1)S(1)}, bf16[256,384]{1,0:T(8,128)(2,1)S(1)}, u32[]{:S(2)}, u32[]{:S(2)}) collective-permute-start(bf16[256,384]{1,0:T(8,128)(2,1)S(1)} %get-tuple-element.17), channel_id=1, source_target_pairs={{0,8},{1,24},{2,10},{3,26},{4,12},{5,28},{6,14},{7,30},{8,0},{9,16... | collective-permute-start | bytes 589832 | tf_op jit(solution)/shard_map/ppermute | solution.py:218
  33.8 13.1 %collective-permute-start.5 = (bf16[256,384]{1,0:T(8,128)(2,1)S(1)}, bf16[256,384]{1,0:T(8,128)(2,1)S(1)}, u32[]{:S(2)}, u32[]{:S(2)}) collective-permute-start(bf16[256,384]{1,0:T(8,128)(2,1)S(1)} %get-tuple-element.18), channel_id=1, source_target_pairs={{0,12},{1,28},{2,14},{3,30},{4,8},{5,24},{6,10},{7,26},{8,4},{9,20... | collective-permute-start | bytes 589832 | tf_op jit(solution)/shard_map/ppermute | solution.py:218
  36.5 10.5 %collective-permute-start.6 = (bf16[256,384]{1,0:T(8,128)(2,1)S(1)}, bf16[256,384]{1,0:T(8,128)(2,1)S(1)}, u32[]{:S(2)}, u32[]{:S(2)}) collective-permute-start(bf16[256,384]{1,0:T(8,128)(2,1)S(1)} %collective-permute-done.2.refs_0_), channel_id=1, source_target_pairs={{0,1},{1,0},{2,3},{3,2},{4,5},{5,4},{6,7},{7,6},{8,9},{9,8},{10,11... | collective-permute-start | bytes 589832 | tf_op jit(solution)/shard_map/ppermute | solution.py:220
  46.4 1.4 %collective-permute-start.7 = (bf16[256,384]{1,0:T(8,128)(2,1)S(1)}, bf16[256,384]{1,0:T(8,128)(2,1)S(1)}, u32[]{:S(2)}, u32[]{:S(2)}) collective-permute-start(bf16[256,384]{1,0:T(8,128)(2,1)S(1)} %collective-permute-done.3.refs_1_), channel_id=1, source_target_pairs={{0,1},{1,0},{2,3},{3,2},{4,5},{5,4},{6,7},{7,6},{8,9},{9,8},{10,11... | collective-permute-start | bytes 589832 | tf_op jit(solution)/shard_map/ppermute | solution.py:220
  46.4 1.7 %collective-permute-start.8 = (bf16[256,384]{1,0:T(8,128)(2,1)S(1)}, bf16[256,384]{1,0:T(8,128)(2,1)S(1)}, u32[]{:S(2)}, u32[]{:S(2)}) collective-permute-start(bf16[256,384]{1,0:T(8,128)(2,1)S(1)} %collective-permute-done.4.refs_2_), channel_id=1, source_target_pairs={{0,1},{1,0},{2,3},{3,2},{4,5},{5,4},{6,7},{7,6},{8,9},{9,8},{10,11... | collective-permute-start | bytes 589832 | tf_op jit(solution)/shard_map/ppermute | solution.py:220
  46.9 1.5 %collective-permute-start.9 = (bf16[256,384]{1,0:T(8,128)(2,1)S(1)}, bf16[256,384]{1,0:T(8,128)(2,1)S(1)}, u32[]{:S(2)}, u32[]{:S(2)}) collective-permute-start(bf16[256,384]{1,0:T(8,128)(2,1)S(1)} %collective-permute-done.5.refs_3_), channel_id=1, source_target_pairs={{0,1},{1,0},{2,3},{3,2},{4,5},{5,4},{6,7},{7,6},{8,9},{9,8},{10,11... | collective-permute-start | bytes 589832 | tf_op jit(solution)/shard_map/ppermute | solution.py:220
  51.8 11.2 %collective-permute-start.10 = (bf16[256,128]{1,0:T(8,128)(2,1)S(1)}, bf16[256,128]{1,0:T(8,128)(2,1)S(1)}, u32[]{:S(2)}, u32[]{:S(2)}) collective-permute-start(bf16[256,128]{1,0:T(8,128)(2,1)S(1)} %get-tuple-element.19), channel_id=1, source_target_pairs={{0,0},{16,1},{2,2},{18,3},{4,4},{20,5},{6,6},{22,7},{8,8},{24,9},{... | collective-permute-start | bytes 196616 | tf_op jit(solution)/shard_map/ppermute | solution.py:223
  57.7 6.3 %collective-permute-start.11 = (bf16[256,128]{1,0:T(8,128)(2,1)S(1)}, bf16[256,128]{1,0:T(8,128)(2,1)S(1)}, u32[]{:S(2)}, u32[]{:S(2)}) collective-permute-start(bf16[256,128]{1,0:T(8,128)(2,1)S(1)} %get-tuple-element.20), channel_id=1, source_target_pairs={{4,0},{20,1},{6,2},{22,3},{0,4},{16,5},{2,6},{18,7},{12,8},{28,9},... | collective-permute-start | bytes 196616 | tf_op jit(solution)/shard_map/ppermute | solution.py:223
  59.4 5.6 %collective-permute-start.12 = (bf16[256,128]{1,0:T(8,128)(2,1)S(1)}, bf16[256,128]{1,0:T(8,128)(2,1)S(1)}, u32[]{:S(2)}, u32[]{:S(2)}) collective-permute-start(bf16[256,128]{1,0:T(8,128)(2,1)S(1)} %get-tuple-element.21), channel_id=1, source_target_pairs={{8,0},{24,1},{10,2},{26,3},{12,4},{28,5},{14,6},{30,7},{0,8},{16,9... | collective-permute-start | bytes 196616 | tf_op jit(solution)/shard_map/ppermute | solution.py:223
  60.2 6.5 %collective-permute-start.13 = (bf16[256,128]{1,0:T(8,128)(2,1)S(1)}, bf16[256,128]{1,0:T(8,128)(2,1)S(1)}, u32[]{:S(2)}, u32[]{:S(2)}) collective-permute-start(bf16[256,128]{1,0:T(8,128)(2,1)S(1)} %get-tuple-element.22), channel_id=1, source_target_pairs={{12,0},{28,1},{14,2},{30,3},{8,4},{24,5},{10,6},{26,7},{4,8},{20,9... | collective-permute-start | bytes 196616 | tf_op jit(solution)/shard_map/ppermute | solution.py:223

commit v2 on v1

v2 whole, which is shorter than its diff:
```python
import functools
import math

import jax
import jax.numpy as jnp
from jax import lax
from jax.experimental import pallas as pl
from jax.experimental.pallas import tpu as pltpu
from jax.sharding import PartitionSpec as P

F32 = jnp.float32
BF16 = jnp.bfloat16
EDGE = 8
TAPS = 5
MIB = 1 << 20


def head_rms(tensor):
    return tensor * lax.rsqrt(jnp.mean(tensor * tensor, axis=-1, keepdims=True) + 1e-06)


def first_kernel(x_hbm, w1_hbm, total_ref, to_pair_ref, to_other_ref, x, w1, sems):
    rows = x.shape[0]
    circle = total_ref.shape[0]
    copies = [pltpu.make_async_copy(x_hbm, x, sems.at[TAPS])]
    copies += [pltpu.make_async_copy(w1_hbm.at[j], w1.at[j], sems.at[j]) for j in range(TAPS)]
    for copy in copies:
        copy.start()
    copies[0].wait()
    for j in range(TAPS):
        copies[1 + j].wait()
        product = jnp.dot(x[...], w1[j], preferred_element_type=F32)
        product = on_circle(product, j)
        if j == 0:
            total_ref[...] = product
        else:
            total_ref[...] += product
    near = EDGE // 2
    begin = jnp.concatenate([total_ref[circle - near : circle], total_ref[0:near]], axis=0)
    end = total_ref[rows - near : rows + near]
    even = lax.axis_index("seq") % 2 == 0
    to_pair_ref[...] = jnp.where(even, end, begin)
    to_other_ref[...] = jnp.where(even, begin, end)


def on_circle(product, j):
    spare = jnp.zeros((2 * EDGE, product.shape[1]), F32)
    circle = product.shape[0] + 2 * EDGE
    shift = (TAPS // 2 - j) % circle
    product = jnp.concatenate([product, spare], axis=0)
    return product if shift == 0 else pltpu.roll(product, shift, 0)


def second_kernel(total_ref, w2, first_ref, second_ref, total):
    rows = first_ref.shape[0]
    row = lax.broadcasted_iota(jnp.int32, first_ref.shape, 0)
    reach = TAPS // 2
    inner = (row >= reach) & (row < rows - reach)
    first_ref[...] = jnp.where(inner, jax.nn.gelu(total_ref[0:rows]), 0.0).astype(BF16)
    for j in range(TAPS):
        product = jnp.dot(first_ref[...], w2[j], preferred_element_type=F32)
        product = on_circle(product, j)
        if j == 0:
            total[...] = product
        else:
            total[...] += product
    second_ref[...] = total[0:rows]


def third_kernel(
    total_ref, pair_ref, other_ref, first_ref, second_ref, w2, wqkv, scale_hbm, *rest,
    heads, head, count, spread
):
    hidden_ref, rest_units, (scale_ref, sem) = rest[0], rest[1:-2], rest[-2:]
    scale_copy = pltpu.make_async_copy(scale_hbm, scale_ref, sem)
    scale_copy.start()
    g = lax.axis_index("seq")
    has_before = (g > 0).astype(jnp.int32)
    has_after = (g < count - 1).astype(jnp.int32)
    rows = first_ref.shape[0]
    circle = total_ref.shape[0]
    near, reach = EDGE // 2, TAPS // 2
    row = lax.broadcasted_iota(jnp.int32, pair_ref.shape, 0)
    even = g % 2 == 0
    before = jnp.where(even, other_ref[...], pair_ref[...]) * has_before.astype(F32)
    after = jnp.where(even, pair_ref[...], other_ref[...]) * has_after.astype(F32)
    begin = jnp.concatenate([total_ref[circle - near : circle], total_ref[0:near]], axis=0)
    begin = jax.nn.gelu(begin + before)
    keep = (row >= near - reach * has_before) & (row < near + reach)
    begin = jnp.where(keep, begin, 0.0)
    end = jax.nn.gelu(total_ref[rows - near : rows + near] + after)
    keep = (row >= near - reach) & (row < near + reach * has_after)
    end = jnp.where(keep, end, 0.0)
    edges = jnp.concatenate([begin, end], axis=0).astype(BF16)
    sums = [jnp.zeros(before.shape, F32)] * 2
    for j in range(TAPS):
        product = jnp.dot(edges, w2[j], preferred_element_type=F32)
        shift = (reach - j) % EDGE
        for i in range(2):
            part = product[i * EDGE : (i + 1) * EDGE]
            sums[i] = sums[i] + (part if shift == 0 else pltpu.roll(part, shift, 0))
    pad = jnp.zeros((EDGE - near, first_ref.shape[1]), F32)
    rounded = edges.astype(F32)
    second_ref_rows = second_ref[0:EDGE] + jnp.concatenate(
        [sums[0][near:] + rounded[near:EDGE], pad], axis=0
    )
    last_rows = second_ref[rows - EDGE : rows] + jnp.concatenate(
        [pad, sums[1][:near] + rounded[EDGE : EDGE + near]], axis=0
    )
    hidden = first_ref[...].astype(F32) + jnp.concatenate(
        [second_ref_rows, second_ref[EDGE : rows - EDGE], last_rows], axis=0
    )
    hidden_ref[...] = hidden.astype(BF16)
    scale_copy.wait()
    project(hidden_ref, wqkv, scale_ref, rest_units, g, range(len(rest_units)), heads, head, spread)


def project(hidden_ref, wqkv, scale_ref, units, g, rounds, heads, head, spread):
    width = heads * head
    hidden = hidden_ref[...]
    for unit, r in zip(units, rounds):
        h = head_of(r, g, heads) if spread else r
        at = pl.multiple_of(h * head, head)
        weight = jnp.concatenate(
            [wqkv[:, pl.ds(part * width + at, head)] for part in range(3)], axis=1
        )
        projected = jnp.dot(hidden, weight, preferred_element_type=F32)
        q = head_rms(projected[:, :head]) * (scale_ref[h] / math.sqrt(head))
        unit[:, 0:head] = q.astype(BF16)
        unit[:, head : 2 * head] = head_rms(projected[:, head : 2 * head]).astype(BF16)
        unit[:, 2 * head :] = projected[:, 2 * head :].astype(BF16)


def fourth_kernel(hidden_ref, wqkv, scale_hbm, *rest, heads, head, spread):
    units, (scale_ref, sem) = rest[:-2], rest[-2:]
    scale_copy = pltpu.make_async_copy(scale_hbm, scale_ref, sem)
    scale_copy.start()
    scale_copy.wait()
    g = lax.axis_index("seq")
    rounds = range(heads - len(units), heads)
    project(hidden_ref, wqkv, scale_ref, units, g, rounds, heads, head, spread)


def head_of(r, g, heads):
    half = heads // 2
    side = g // heads
    return half * (side ^ 1 ^ (r // half)) + ((r % half) ^ (g % half))


def swaps(offset):
    count, batch_count = lax.axis_size("seq"), lax.axis_size("batch")
    pairs = []
    for g in range(count):
        for b in range(batch_count):
            to = ((g + offset) ^ 1) - offset
            target = (to, b) if 0 <= to < count else (g, b ^ 1 if b ^ 1 < batch_count else b)
            pairs.append((g * batch_count + b, target[0] * batch_count + target[1]))
    return pairs


def stem(block, conv_first, conv_second, qkv_weight, logit_scale, spread):
    rows, channels = block.shape
    width = conv_first.shape[2]
    heads = logit_scale.shape[0]
    head = qkv_weight.shape[1] // 3 // heads
    circle = rows + 2 * EDGE
    vmem = pl.BlockSpec(memory_space=pltpu.VMEM)
    hbm = pl.BlockSpec(memory_space=pltpu.HBM)
    shape = jax.ShapeDtypeStruct
    total, to_pair, to_other = pl.pallas_call(
        first_kernel,
        out_shape=[shape((circle, width), F32)] + [shape((EDGE, width), F32)] * 2,
        in_specs=[hbm, hbm],
        out_specs=[vmem] * 3,
        scratch_shapes=[
            pltpu.VMEM(block.shape, BF16),
            pltpu.VMEM(conv_first.shape, BF16),
            pltpu.SemaphoreType.DMA((TAPS + 1,)),
        ],
        compiler_params=pltpu.CompilerParams(vmem_limit_bytes=24 * MIB),
        name="first",
    )(
        pltpu.with_memory_space_constraint(block, pltpu.HBM),
        pltpu.with_memory_space_constraint(conv_first, pltpu.HBM),
    )
    total, to_pair, to_other, conv_second, qkv_weight = lax.optimization_barrier(
        (total, to_pair, to_other, conv_second, qkv_weight)
    )
    pair = lax.ppermute(to_pair, ("seq", "batch"), swaps(0))
    other = lax.ppermute(to_other, ("seq", "batch"), swaps(1))
    first, second = pl.pallas_call(
        second_kernel,
        out_shape=[shape((rows, width), BF16), shape((rows, width), F32)],
        in_specs=[vmem] * 2,
        out_specs=[vmem] * 2,
        scratch_shapes=[pltpu.VMEM((circle, width), F32)],
        compiler_params=pltpu.CompilerParams(vmem_limit_bytes=24 * MIB),
        name="second",
    )(total, conv_second)
    half = heads // 2
    fixed = dict(heads=heads, head=head, spread=spread)
    unit = shape((rows, 3 * head), BF16)
    scale_scratch = [pltpu.SMEM(logit_scale.shape, F32), pltpu.SemaphoreType.DMA]
    hidden, *units = pl.pallas_call(
        functools.partial(third_kernel, count=lax.axis_size("seq"), **fixed),
        out_shape=[shape((rows, width), BF16)] + [unit] * half,
        in_specs=[vmem] * 7 + [hbm],
        out_specs=[vmem] * (1 + half),
        scratch_shapes=scale_scratch,
        compiler_params=pltpu.CompilerParams(vmem_limit_bytes=24 * MIB),
        name="third",
    )(total, pair, other, first, second, conv_second, qkv_weight, logit_scale)
    units += pl.pallas_call(
        functools.partial(fourth_kernel, **fixed),
        out_shape=[unit] * (heads - half),
        in_specs=[vmem] * 2 + [hbm],
        out_specs=[vmem] * (heads - half),
        scratch_shapes=scale_scratch,
        compiler_params=pltpu.CompilerParams(vmem_limit_bytes=24 * MIB),
        name="fourth",
    )(hidden, qkv_weight, logit_scale)
    return [hidden, *units]


def scores_of(queries, keys):
    return lax.dot_general(
        queries, keys, (((1,), (1,)), ((), ())), preferred_element_type=F32
    )


def stack_keys(units, keys, values):
    rows = units[0].shape[0]
    head = keys.shape[1]
    for i, unit in enumerate(units):
        keys[i * rows : (i + 1) * rows] = unit[:, head : 2 * head]
        values[i * rows : (i + 1) * rows] = unit[:, 2 * head :]


def attend_kernel(*refs, head, count):
    units, outs, (keys, values) = refs[: -2 - count], refs[-2 - count : -2], refs[-2:]
    stack_keys(units, keys, values)
    for i in range(count):
        scores = scores_of(units[i][:, 0:head], keys[...])
        weights = jnp.exp(scores - jnp.max(scores, axis=1, keepdims=True))
        denominators = jnp.sum(weights, axis=1, keepdims=True)
        mixed = jnp.dot(weights.astype(BF16), values[...], preferred_element_type=F32)
        outs[i][...] = (mixed / denominators).astype(BF16)


def attend(units, count, name):
    rows, wide = units[0].shape
    head = wide // 3
    vmem = pl.BlockSpec(memory_space=pltpu.VMEM)
    return pl.pallas_call(
        functools.partial(attend_kernel, head=head, count=count),
        out_shape=[jax.ShapeDtypeStruct((rows, head), BF16)] * count,
        in_specs=[vmem] * len(units),
        out_specs=[vmem] * count,
        scratch_shapes=[pltpu.VMEM((len(units) * rows, head), BF16)] * 2,
        compiler_params=pltpu.CompilerParams(vmem_limit_bytes=24 * MIB),
        name=name,
    )(*units)


def finish_kernel(hidden_ref, weight_ref, *rest, spread):
    mixed, out_ref = rest[:-1], rest[-1]
    g = lax.axis_index("seq")
    head = mixed[0].shape[1]
    total = hidden_ref[...].astype(F32)
    for r in range(len(mixed)):
        h = head_of(r, g, len(mixed)) if spread else r
        at = pl.multiple_of(h * head, head)
        total += jnp.dot(
            mixed[r][...], weight_ref[pl.ds(at, head), :], preferred_element_type=F32
        )
    out_ref[...] = total.astype(out_ref.dtype)


def finish(hidden, out_weight, mixed, spread):
    vmem = pl.BlockSpec(memory_space=pltpu.VMEM)
    return pl.pallas_call(
        functools.partial(finish_kernel, spread=spread),
        out_shape=jax.ShapeDtypeStruct(hidden.shape, BF16),
        in_specs=[vmem] * (2 + len(mixed)),
        out_specs=vmem,
        compiler_params=pltpu.CompilerParams(vmem_limit_bytes=32 * MIB),
        name="finish",
    )(hidden, out_weight, *mixed)


def routes(seq_count, batch_count, heads):
    half = heads // 2
    rounds = []
    for r in range(heads):
        pairs = []
        for g in range(seq_count):
            for b in range(batch_count):
                h = head_of(r, g, heads)
                chip = heads * (h // half) + half * (b % 2) + h % half
                core = (g // half + r // half) % 2
                target = chip * batch_count + b - b % 2 + core
                pairs.append((g * batch_count + b, target))
        rounds.append(pairs)
    return rounds


def by_heads(sequence_input, conv_first, conv_second, qkv_weight, out_weight, logit_scale):
    heads = logit_scale.shape[0]
    count = lax.axis_size("seq")
    batch_count = lax.axis_size("batch")
    hidden, *units = stem(
        sequence_input, conv_first, conv_second, qkv_weight, logit_scale, True
    )
    both = ("seq", "batch")
    rounds = routes(count, batch_count, heads)
    own = [lax.ppermute(unit, both, pairs) for unit, pairs in zip(units, rounds)]
    cores = [(b, b ^ 1) for b in range(batch_count)]
    other = [lax.ppermute(unit, "batch", cores) for unit in own]
    half = heads // 2
    far, near = own[:half], own[half:]
    outs = attend([*far, *near, *other], half, "far")
    outs, near = lax.optimization_barrier((outs, near))
    outs = outs + attend([*near, *far, *other], heads - half, "near")
    mixed = [
        lax.ppermute(out, both, [(target, source) for source, target in pairs])
        for out, pairs in zip(outs, rounds)
    ]
    return finish(hidden, out_weight, mixed, True)


def by_gather(sequence_input, conv_first, conv_second, qkv_weight, out_weight, logit_scale):
    heads = logit_scale.shape[0]
    count = lax.axis_size("seq")
    hidden, *units = stem(
        sequence_input, conv_first, conv_second, qkv_weight, logit_scale, False
    )
    head = units[0].shape[1] // 3
    pairs = jnp.concatenate([unit[:, head:] for unit in units], axis=1)
    everywhere = lax.all_gather(pairs, "seq", axis=0, tiled=True)
    mixed = []
    for h in range(heads):
        at = 2 * h * head
        scores = lax.dot_general(
            units[h][:, :head],
            everywhere[:, at : at + head],
            (((1,), (1,)), ((), ())),
            preferred_element_type=F32,
        )
        weights = jnp.exp(scores - jnp.max(scores, axis=1, keepdims=True))
        denominators = jnp.sum(weights, axis=1, keepdims=True)
        out = jnp.dot(
            weights.astype(BF16),
            everywhere[:, at + head : at + 2 * head],
            preferred_element_type=F32,
        )
        mixed.append((out / denominators).astype(BF16))
    return finish(hidden, out_weight, mixed, False)


def solution(mesh):
    def body(*args):
        heads = args[-1].shape[0]
        fits = heads == 4 and mesh.shape["seq"] == 2 * heads and mesh.shape["batch"] % 2 == 0
        return (by_heads if fits else by_gather)(*args)

    in_specs = (P(("batch", "seq"), None), P(), P(), P(), P(), P())
    out_specs = P(("batch", "seq"), None)
    return jax.shard_map(body, mesh=mesh, in_specs=in_specs, out_specs=out_specs, check_vma=False)
```

time: 68.8 us -> 52.6 us (0.76)
  waiting for transfers between devices: 18.1 us -> 8.69 us
  local copies, waits for them, and re-layouts: 4.3 us -> 0.02 us
  starting transfers between devices: 28.8 us -> 26.5 us
    ppermute x4, starting transfers between devices: 0.58 us -> 12.2 us  [by_heads(): other = [lax.ppermute(unit, 'batch', cores) for unit in own]]
    ppermute x4, starting transfers between devices: 11.2 us -> 4.46 us  [by_heads(): lax.ppermute(out, both, [(target, source) for source, target in pairs])]
    ppermute x4, waiting for transfers between devices: 9.9 us -> 3.53 us  [by_heads(): lax.ppermute(unit, both, pairs)]
    ppermute x4, starting transfers between devices: 11.8 us -> 6.81 us  [by_heads(): lax.ppermute(unit, both, pairs)]
    unnamed x8, local copies, waits for them, and re-layouts: 3.46 us -> 0.02 us
    ppermute x2, waiting for transfers between devices: 3.17 us -> 0.01 us  [the longest x1 0.01 us: stem(): other = lax.ppermute(to_other, ('seq', 'batch'), swaps(1))]
    ppermute x2, starting transfers between devices: 5.23 us -> 3.06 us  [the longest x1 2.1 us: stem(): pair = lax.ppermute(to_pair, ('seq', 'batch'), swaps(0))]
    slice x1 -> x0, local copies, waits for them, and re-layouts: 0.76 us -> none  [edge_rows(): before = lax.ppermute(block[block.shape[0] - EDGE:], 'seq', forward)]
  transfers between devices with their start and end apart: 14 -> 14, of which waited for: 8 -> 7; matrix products, arithmetic and copies ran while one was open for 0% -> 0% of each run, Pallas kernels for 0% -> 10%
where the time goes in v2:
time: 52.6 us; the launch traced here: 52.4 us
  starting transfers between devices  26.5 us (50%)
  Pallas kernels  17.1 us (33%)
  waiting for transfers between devices  8.69 us (17%)
    ppermute x4, starting transfers between devices, by_heads(): other = [lax.ppermute(unit, 'batch', cores) for unit in own]  12.2 us
    pallas_call x1, Pallas kernels, stem(): pl.pallas_call(first_kernel, out_shape=[shape((circle, width), F32)] + [s...  6.83 us
    ppermute x4, starting transfers between devices, by_heads(): lax.ppermute(unit, both, pairs)  6.81 us
    ppermute x4, starting transfers between devices, by_heads(): lax.ppermute(out, both, [(target, source) for source, target in pairs])  4.46 us
    ppermute x4, waiting for transfers between devices, by_heads(): lax.ppermute(out, both, [(target, source) for source, target in pairs])  3.95 us
    pallas_call x2, Pallas kernels, attend(): pl.pallas_call(functools.partial(attend_kernel, head=head, count=count),...  3.74 us
    ppermute x4, waiting for transfers between devices, by_heads(): lax.ppermute(unit, both, pairs)  3.53 us
    ppermute x1, starting transfers between devices, stem(): pair = lax.ppermute(to_pair, ('seq', 'batch'), swaps(0))  2.1 us
  transfers between devices with their start and end apart: 14, of which 7 were waited for; matrix products, arithmetic and copies ran while one was open for 0% of the time, Pallas kernels for 10%

profile of v2, /device:TPU:1, one launch (start us, length us, event | category | flops | bytes accessed | tf_op | source)
XLA Modules:
  0.0 52.4 jit_solution(9714358641452259975)
XLA Ops:
  0.0 6.8 %first.1 = (f32[272,768]{1,0:T(8,128)S(1)}, f32[8,768]{1,0:T(8,128)S(1)}, f32[8,768]{1,0:T(8,128)S(1)}) custom-call(bf16[256,1536]{1,0:T(8,128)(2,1)} %x_hbm.1, bf16[5,1536,768]{2,1,0:T(8,128)(2,1)} %w1_hbm.1), custom_call_target="tpu_custom_call" | custom-call | tf_op jit(solution)/shard_map/first/pallas_call | solution.py:170
  6.8 0.0 copy-start.1
  6.8 0.0 copy-start.3
  6.9 2.1 %collective-permute-start = (f32[8,768]{1,0:T(8,128)S(1)}, f32[8,768]{1,0:T(8,128)S(1)}, u32[]{:S(2)}, u32[]{:S(2)}) collective-permute-start(f32[8,768]{1,0:T(8,128)S(1)} %get-tuple-element.32), channel_id=1, source_target_pairs={{0,4},{1,5},{2,6},{3,7},{4,0},{5,1},{6,2},{7,3},{8,12},{9,13},{10,... | collective-permute-start | bytes 73736 | tf_op jit(solution)/shard_map/ppermute | solution.py:189
  9.0 1.0 %collective-permute-start.1 = (f32[8,768]{1,0:T(8,128)S(1)}, f32[8,768]{1,0:T(8,128)S(1)}, u32[]{:S(2)}, u32[]{:S(2)}) collective-permute-start(f32[8,768]{1,0:T(8,128)S(1)} %get-tuple-element.33), channel_id=1, source_target_pairs={{0,1},{1,0},{2,3},{3,2},{4,8},{5,9},{6,10},{7,11},{8,4},{9,5},{10,... | collective-permute-start | bytes 73736 | tf_op jit(solution)/shard_map/ppermute | solution.py:190
  9.9 1.9 %second.1 = (bf16[256,768]{1,0:T(8,128)(2,1)S(1)}, f32[256,768]{1,0:T(8,128)S(1)}) custom-call(f32[272,768]{1,0:T(8,128)S(1)} %get-tuple-element.31.total_ref, bf16[5,768,768]{2,1,0:T(8,128)(2,1)S(1)} %copy-done), custom_call_target="tpu_custom_call" | custom-call | tf_op jit(solution)/shard_map/second/pallas_call | solution.py:191
  11.9 0.0 collective-permute-done.1.other_ref
  11.9 0.0 copy-start.2
  11.9 2.1 %third.1 = (bf16[256,768]{1,0:T(8,128)(2,1)S(1)}, bf16[256,384]{1,0:T(8,128)(2,1)S(1)}, bf16[256,384]{1,0:T(8,128)(2,1)S(1)}) custom-call(f32[272,768]{1,0:T(8,128)S(1)} %get-tuple-element.31.total_ref, f32[8,768]{1,0:T(8,128)S(1)} %collective-permute-done.pair_ref, f32[8,768]{1,0:T(8,128)S(1)} %collective-permute-done.1.other_ref, ...), custom_call_target="tpu_custom_call" | custom-call | tf_op jit(solution)/shard_map/third/pallas_call | solution.py:204
  14.0 6.0 %collective-permute-start.2 = (bf16[256,384]{1,0:T(8,128)(2,1)S(1)}, bf16[256,384]{1,0:T(8,128)(2,1)S(1)}, u32[]{:S(2)}, u32[]{:S(2)}) collective-permute-start(bf16[256,384]{1,0:T(8,128)(2,1)S(1)} %get-tuple-element.39), channel_id=1, source_target_pairs={{0,16},{1,24},{2,18},{3,26},{4,20},{5,28},{6,22},{7,30},{8,17},{9,... | collective-permute-start | bytes 589832 | tf_op jit(solution)/shard_map/ppermute | solution.py:316
  20.0 1.2 %fourth.1 = (bf16[256,384]{1,0:T(8,128)(2,1)S(1)}, bf16[256,384]{1,0:T(8,128)(2,1)S(1)}) custom-call(bf16[256,768]{1,0:T(8,128)(2,1)S(1)} %get-tuple-element.38.hidden_ref, bf16[768,1536]{1,0:T(8,128)(2,1)S(1)} %copy-done.1, f32[4]{0:T(128)S(1)} %copy-done.3), custom_call_target="tpu_custom_call" | custom-call | tf_op jit(solution)/shard_map/fourth/pallas_call | solution.py:213
  21.2 0.1 collective-permute-start.4
  21.3 0.7 %collective-permute-start.5 = (bf16[256,384]{1,0:T(8,128)(2,1)S(1)}, bf16[256,384]{1,0:T(8,128)(2,1)S(1)}, u32[]{:S(2)}, u32[]{:S(2)}) collective-permute-start(bf16[256,384]{1,0:T(8,128)(2,1)S(1)} %get-tuple-element.42), channel_id=1, source_target_pairs={{0,5},{1,13},{2,7},{3,15},{4,1},{5,9},{6,3},{7,11},{8,4},{9,12},{1... | collective-permute-start | bytes 589832 | tf_op jit(solution)/shard_map/ppermute | solution.py:316
  22.0 3.5 %collective-permute-done.2.refs_0_.refs_2_ = bf16[256,384]{1,0:T(8,128)(2,1)S(1)} collective-permute-done((bf16[256,384]{1,0:T(8,128)(2,1)S(1)}, bf16[256,384]{1,0:T(8,128)(2,1)S(1)}, u32[]{:S(2)}, u32[]{:S(2)}) %collective-permute-start.2) | collective-permute-done | bytes 196640 | tf_op jit(solution)/shard_map/ppermute | solution.py:316
  25.5 6.9 %collective-permute-start.6 = (bf16[256,384]{1,0:T(8,128)(2,1)S(1)}, bf16[256,384]{1,0:T(8,128)(2,1)S(1)}, u32[]{:S(2)}, u32[]{:S(2)}) collective-permute-start(bf16[256,384]{1,0:T(8,128)(2,1)S(1)} %collective-permute-done.2.refs_0_.refs_2_), channel_id=1, source_target_pairs={{0,1},{1,0},{2,3},{3,2},{4,5},{5,4},{6,7},{7,6},{8,9},{9,8},{10,11... | collective-permute-start | bytes 589832 | tf_op jit(solution)/shard_map/ppermute | solution.py:318
  32.5 0.0 collective-permute-done.3.refs_1_.refs_3_
  32.5 4.7 %collective-permute-start.7 = (bf16[256,384]{1,0:T(8,128)(2,1)S(1)}, bf16[256,384]{1,0:T(8,128)(2,1)S(1)}, u32[]{:S(2)}, u32[]{:S(2)}) collective-permute-start(bf16[256,384]{1,0:T(8,128)(2,1)S(1)} %collective-permute-done.3.refs_1_.refs_3_), channel_id=1, source_target_pairs={{0,1},{1,0},{2,3},{3,2},{4,5},{5,4},{6,7},{7,6},{8,9},{9,8},{10,11... | collective-permute-start | bytes 589832 | tf_op jit(solution)/shard_map/ppermute | solution.py:318
  37.2 0.0 collective-permute-start.8
  37.2 0.5 collective-permute-start.9
  37.7 0.5 %collective-permute-done.7.refs_5_ = bf16[256,384]{1,0:T(8,128)(2,1)S(1)} collective-permute-done((bf16[256,384]{1,0:T(8,128)(2,1)S(1)}, bf16[256,384]{1,0:T(8,128)(2,1)S(1)}, u32[]{:S(2)}, u32[]{:S(2)}) %collective-permute-start.7) | collective-permute-done | bytes 196640 | tf_op jit(solution)/shard_map/ppermute | solution.py:318
  38.3 0.4 collective-permute-done.8.refs_6_
  38.6 0.3 collective-permute-done.9.refs_7_
  38.9 1.9 %far.1 = (bf16[256,128]{1,0:T(8,128)(2,1)S(1)}, bf16[256,128]{1,0:T(8,128)(2,1)S(1)}) custom-call(bf16[256,384]{1,0:T(8,128)(2,1)S(1)} %collective-permute-done.2.refs_0_.refs_2_, bf16[256,384]{1,0:T(8,128)(2,1)S(1)} %collective-permute-done.3.refs_1_.refs_3_, bf16[256,384]{1,0:T(8,128)(2,1)S(1)} %collective-permute-done.4.refs_2_.refs_0_, ...), custom_call_target="tpu_custom_call" | custom-call | tf_op jit(solution)/shard_map/far/pallas_call | solution.py:254
  40.8 0.1 collective-permute-start.10
  40.9 3.9 %collective-permute-start.11 = (bf16[256,128]{1,0:T(8,128)(2,1)S(1)}, bf16[256,128]{1,0:T(8,128)(2,1)S(1)}, u32[]{:S(2)}, u32[]{:S(2)}) collective-permute-start(bf16[256,128]{1,0:T(8,128)(2,1)S(1)} %get-tuple-element.46), channel_id=1, source_target_pairs={{20,0},{28,1},{22,2},{30,3},{16,4},{24,5},{18,6},{26,7},{21,8},{29... | collective-permute-start | bytes 196616 | tf_op jit(solution)/shard_map/ppermute | solution.py:325
  44.8 1.9 %near.1 = (bf16[256,128]{1,0:T(8,128)(2,1)S(1)}, bf16[256,128]{1,0:T(8,128)(2,1)S(1)}) custom-call(bf16[256,384]{1,0:T(8,128)(2,1)S(1)} %collective-permute-done.4.refs_2_.refs_0_, bf16[256,384]{1,0:T(8,128)(2,1)S(1)} %collective-permute-done.5.refs_3_.refs_1_, bf16[256,384]{1,0:T(8,128)(2,1)S(1)} %collective-permute-done.2.refs_0_.refs_2_, ...), custom_call_target="tpu_custom_call" | custom-call | tf_op jit(solution)/shard_map/near/pallas_call | solution.py:254
  46.7 0.1 collective-permute-start.12
  46.7 0.4 collective-permute-start.13
  47.2 0.6 %collective-permute-done.11.rest_1_ = bf16[256,128]{1,0:T(8,128)(2,1)S(1)} collective-permute-done((bf16[256,128]{1,0:T(8,128)(2,1)S(1)}, bf16[256,128]{1,0:T(8,128)(2,1)S(1)}, u32[]{:S(2)}, u32[]{:S(2)}) %collective-permute-start.11) | collective-permute-done | bytes 65568 | tf_op jit(solution)/shard_map/ppermute | solution.py:325
  47.7 2.4 %collective-permute-done.12.rest_2_ = bf16[256,128]{1,0:T(8,128)(2,1)S(1)} collective-permute-done((bf16[256,128]{1,0:T(8,128)(2,1)S(1)}, bf16[256,128]{1,0:T(8,128)(2,1)S(1)}, u32[]{:S(2)}, u32[]{:S(2)}) %collective-permute-start.12) | collective-permute-done | bytes 65568 | tf_op jit(solution)/shard_map/ppermute | solution.py:325
  50.1 1.0 %collective-permute-done.13.rest_3_ = bf16[256,128]{1,0:T(8,128)(2,1)S(1)} collective-permute-done((bf16[256,128]{1,0:T(8,128)(2,1)S(1)}, bf16[256,128]{1,0:T(8,128)(2,1)S(1)}, u32[]{:S(2)}, u32[]{:S(2)}) %collective-permute-start.13) | collective-permute-done | bytes 65568 | tf_op jit(solution)/shard_map/ppermute | solution.py:325
  51.1 1.3 %finish.1 = bf16[256,768]{1,0:T(8,128)(2,1)} custom-call(bf16[256,768]{1,0:T(8,128)(2,1)S(1)} %get-tuple-element.38.hidden_ref, bf16[512,768]{1,0:T(8,128)(2,1)S(1)} %copy-done.2, bf16[256,128]{1,0:T(8,128)(2,1)S(1)} %collective-permute-done.10.rest_0_, bf16[256,128]{1,0:T(8,128)(2,1)S(1)} %collective-permute-done.11.rest_1_, ...), custom_call_target="tpu_custom_call" | custom-call | tf_op jit(solution)/shard_map/finish/pallas_call | solution.py:281
  (11 shorter events, 0.0 us)
Async XLA Ops:
  0.0 9.9 %copy-start = (bf16[5,768,768]{2,1,0:T(8,128)(2,1)S(1)}, bf16[5,768,768]{2,1,0:T(8,128)(2,1)}, u32[]{:S(2)}) copy-start(bf16[5,768,768]{2,1,0:T(8,128)(2,1)} %w2.1) | copy-start | bytes 17694724
  6.8 5.0 %copy-start.1 = (bf16[768,1536]{1,0:T(8,128)(2,1)S(1)}, bf16[768,1536]{1,0:T(8,128)(2,1)}, u32[]{:S(2)}) copy-start(bf16[768,1536]{1,0:T(8,128)(2,1)} %wqkv.1) | copy-start | bytes 7077892
  6.8 5.0 %copy-start.3 = (f32[4]{0:T(128)S(1)}, f32[4]{0:T(128)}, u32[]{:S(2)}) copy-start(f32[4]{0:T(128)} %scale_hbm.3) | copy-start | bytes 52
  6.9 5.0 %collective-permute-start = (f32[8,768]{1,0:T(8,128)S(1)}, f32[8,768]{1,0:T(8,128)S(1)}, u32[]{:S(2)}, u32[]{:S(2)}) collective-permute-start(f32[8,768]{1,0:T(8,128)S(1)} %get-tuple-element.32), channel_id=1, source_target_pairs={{0,4},{1,5},{2,6},{3,7},{4,0},{5,1},{6,2},{7,3},{8,12},{9,13},{10,... | collective-permute-start | bytes 73736 | tf_op jit(solution)/shard_map/ppermute | solution.py:189
  9.0 2.9 %collective-permute-start.1 = (f32[8,768]{1,0:T(8,128)S(1)}, f32[8,768]{1,0:T(8,128)S(1)}, u32[]{:S(2)}, u32[]{:S(2)}) collective-permute-start(f32[8,768]{1,0:T(8,128)S(1)} %get-tuple-element.33), channel_id=1, source_target_pairs={{0,1},{1,0},{2,3},{3,2},{4,8},{5,9},{6,10},{7,11},{8,4},{9,5},{10,... | collective-permute-start | bytes 73736 | tf_op jit(solution)/shard_map/ppermute | solution.py:190
  11.9 39.2 %copy-start.2 = (bf16[512,768]{1,0:T(8,128)(2,1)S(1)}, bf16[512,768]{1,0:T(8,128)(2,1)}, u32[]{:S(2)}) copy-start(bf16[512,768]{1,0:T(8,128)(2,1)} %weight_ref.1) | copy-start | bytes 2359300
  14.0 11.6 %collective-permute-start.2 = (bf16[256,384]{1,0:T(8,128)(2,1)S(1)}, bf16[256,384]{1,0:T(8,128)(2,1)S(1)}, u32[]{:S(2)}, u32[]{:S(2)}) collective-permute-start(bf16[256,384]{1,0:T(8,128)(2,1)S(1)} %get-tuple-element.39), channel_id=1, source_target_pairs={{0,16},{1,24},{2,18},{3,26},{4,20},{5,28},{6,22},{7,30},{8,17},{9,... | collective-permute-start | bytes 589832 | tf_op jit(solution)/shard_map/ppermute | solution.py:316
  20.0 12.4 %collective-permute-start.3 = (bf16[256,384]{1,0:T(8,128)(2,1)S(1)}, bf16[256,384]{1,0:T(8,128)(2,1)S(1)}, u32[]{:S(2)}, u32[]{:S(2)}) collective-permute-start(bf16[256,384]{1,0:T(8,128)(2,1)S(1)} %get-tuple-element.40), channel_id=1, source_target_pairs={{0,20},{1,28},{2,22},{3,30},{4,16},{5,24},{6,18},{7,26},{8,21},{9,... | collective-permute-start | bytes 589832 | tf_op jit(solution)/shard_map/ppermute | solution.py:316
  21.2 16.0 %collective-permute-start.4 = (bf16[256,384]{1,0:T(8,128)(2,1)S(1)}, bf16[256,384]{1,0:T(8,128)(2,1)S(1)}, u32[]{:S(2)}, u32[]{:S(2)}) collective-permute-start(bf16[256,384]{1,0:T(8,128)(2,1)S(1)} %get-tuple-element.41), channel_id=1, source_target_pairs={{0,1},{1,9},{2,3},{3,11},{4,5},{5,13},{6,7},{7,15},{8,0},{9,8},{10... | collective-permute-start | bytes 589832 | tf_op jit(solution)/shard_map/ppermute | solution.py:316
  21.3 15.9 %collective-permute-start.5 = (bf16[256,384]{1,0:T(8,128)(2,1)S(1)}, bf16[256,384]{1,0:T(8,128)(2,1)S(1)}, u32[]{:S(2)}, u32[]{:S(2)}) collective-permute-start(bf16[256,384]{1,0:T(8,128)(2,1)S(1)} %get-tuple-element.42), channel_id=1, source_target_pairs={{0,5},{1,13},{2,7},{3,15},{4,1},{5,9},{6,3},{7,11},{8,4},{9,12},{1... | collective-permute-start | bytes 589832 | tf_op jit(solution)/shard_map/ppermute | solution.py:316
  25.5 12.2 %collective-permute-start.6 = (bf16[256,384]{1,0:T(8,128)(2,1)S(1)}, bf16[256,384]{1,0:T(8,128)(2,1)S(1)}, u32[]{:S(2)}, u32[]{:S(2)}) collective-permute-start(bf16[256,384]{1,0:T(8,128)(2,1)S(1)} %collective-permute-done.2.refs_0_.refs_2_), channel_id=1, source_target_pairs={{0,1},{1,0},{2,3},{3,2},{4,5},{5,4},{6,7},{7,6},{8,9},{9,8},{10,11... | collective-permute-start | bytes 589832 | tf_op jit(solution)/shard_map/ppermute | solution.py:318
  32.5 5.8 %collective-permute-start.7 = (bf16[256,384]{1,0:T(8,128)(2,1)S(1)}, bf16[256,384]{1,0:T(8,128)(2,1)S(1)}, u32[]{:S(2)}, u32[]{:S(2)}) collective-permute-start(bf16[256,384]{1,0:T(8,128)(2,1)S(1)} %collective-permute-done.3.refs_1_.refs_3_), channel_id=1, source_target_pairs={{0,1},{1,0},{2,3},{3,2},{4,5},{5,4},{6,7},{7,6},{8,9},{9,8},{10,11... | collective-permute-start | bytes 589832 | tf_op jit(solution)/shard_map/ppermute | solution.py:318
  37.2 1.4 %collective-permute-start.8 = (bf16[256,384]{1,0:T(8,128)(2,1)S(1)}, bf16[256,384]{1,0:T(8,128)(2,1)S(1)}, u32[]{:S(2)}, u32[]{:S(2)}) collective-permute-start(bf16[256,384]{1,0:T(8,128)(2,1)S(1)} %collective-permute-done.4.refs_2_.refs_0_), channel_id=1, source_target_pairs={{0,1},{1,0},{2,3},{3,2},{4,5},{5,4},{6,7},{7,6},{8,9},{9,8},{10,11... | collective-permute-start | bytes 589832 | tf_op jit(solution)/shard_map/ppermute | solution.py:318
  37.2 1.7 %collective-permute-start.9 = (bf16[256,384]{1,0:T(8,128)(2,1)S(1)}, bf16[256,384]{1,0:T(8,128)(2,1)S(1)}, u32[]{:S(2)}, u32[]{:S(2)}) collective-permute-start(bf16[256,384]{1,0:T(8,128)(2,1)S(1)} %collective-permute-done.5.refs_3_.refs_1_), channel_id=1, source_target_pairs={{0,1},{1,0},{2,3},{3,2},{4,5},{5,4},{6,7},{7,6},{8,9},{9,8},{10,11... | collective-permute-start | bytes 589832 | tf_op jit(solution)/shard_map/ppermute | solution.py:318
  40.8 6.4 %collective-permute-start.10 = (bf16[256,128]{1,0:T(8,128)(2,1)S(1)}, bf16[256,128]{1,0:T(8,128)(2,1)S(1)}, u32[]{:S(2)}, u32[]{:S(2)}) collective-permute-start(bf16[256,128]{1,0:T(8,128)(2,1)S(1)} %get-tuple-element.45), channel_id=1, source_target_pairs={{16,0},{24,1},{18,2},{26,3},{20,4},{28,5},{22,6},{30,7},{17,8},{25... | collective-permute-start | bytes 196616 | tf_op jit(solution)/shard_map/ppermute | solution.py:325
  40.9 6.9 %collective-permute-start.11 = (bf16[256,128]{1,0:T(8,128)(2,1)S(1)}, bf16[256,128]{1,0:T(8,128)(2,1)S(1)}, u32[]{:S(2)}, u32[]{:S(2)}) collective-permute-start(bf16[256,128]{1,0:T(8,128)(2,1)S(1)} %get-tuple-element.46), channel_id=1, source_target_pairs={{20,0},{28,1},{22,2},{30,3},{16,4},{24,5},{18,6},{26,7},{21,8},{29... | collective-permute-start | bytes 196616 | tf_op jit(solution)/shard_map/ppermute | solution.py:325
  46.7 3.5 %collective-permute-start.12 = (bf16[256,128]{1,0:T(8,128)(2,1)S(1)}, bf16[256,128]{1,0:T(8,128)(2,1)S(1)}, u32[]{:S(2)}, u32[]{:S(2)}) collective-permute-start(bf16[256,128]{1,0:T(8,128)(2,1)S(1)} %get-tuple-element.49), channel_id=1, source_target_pairs={{1,0},{9,1},{3,2},{11,3},{5,4},{13,5},{7,6},{15,7},{0,8},{8,9},{2,... | collective-permute-start | bytes 196616 | tf_op jit(solution)/shard_map/ppermute | solution.py:325
  46.7 4.4 %collective-permute-start.13 = (bf16[256,128]{1,0:T(8,128)(2,1)S(1)}, bf16[256,128]{1,0:T(8,128)(2,1)S(1)}, u32[]{:S(2)}, u32[]{:S(2)}) collective-permute-start(bf16[256,128]{1,0:T(8,128)(2,1)S(1)} %get-tuple-element.50), channel_id=1, source_target_pairs={{5,0},{13,1},{7,2},{15,3},{1,4},{9,5},{3,6},{11,7},{4,8},{12,9},{6... | collective-permute-start | bytes 196616 | tf_op jit(solution)/shard_map/ppermute | solution.py:325

commit v3 on v2

v3 whole, which is shorter than its diff:
```python
import functools
import math

import jax
import jax.numpy as jnp
from jax import lax
from jax.experimental import pallas as pl
from jax.experimental.pallas import tpu as pltpu
from jax.sharding import PartitionSpec as P

F32 = jnp.float32
BF16 = jnp.bfloat16
EDGE = 8
TILE = 16
TAPS = 5
MIB = 1 << 20


def head_rms(tensor):
    return tensor * lax.rsqrt(jnp.mean(tensor * tensor, axis=-1, keepdims=True) + 1e-06)


def edges_kernel(x_hbm, w1_hbm, to_pair, to_other, first, last, sems):
    rows = x_hbm.shape[0]
    copies = [
        pltpu.make_async_copy(x_hbm.at[pl.ds(0, TILE)], first, sems.at[0]),
        pltpu.make_async_copy(x_hbm.at[pl.ds(rows - TILE, TILE)], last, sems.at[1]),
    ]
    for copy in copies:
        copy.start()
    for copy in copies:
        copy.wait()
    even = lax.axis_index("seq") % 2 == 0
    begin = first[...].astype(F32)[:EDGE]
    end = last[...].astype(F32)[TILE - EDGE :]
    to_pair[...] = jnp.where(even, end, begin).astype(BF16)
    to_other[...] = jnp.where(even, begin, end).astype(BF16)


def rolled(product, j):
    shift = (TAPS // 2 - j) % product.shape[0]
    return product if shift == 0 else pltpu.roll(product, shift, 0)


def first_kernel(x_ref, pair_ref, other_ref, w1, first_ref, x, total, *, count):
    rows = x_ref.shape[0]
    g = lax.axis_index("seq")
    even = g % 2 == 0
    has_before = (g > 0).astype(F32)
    has_after = (g < count - 1).astype(F32)
    pair, other = pair_ref[...].astype(F32), other_ref[...].astype(F32)
    after = jnp.where(even, pair, other) * has_after
    before = jnp.where(even, other, pair) * has_before
    x[0:rows] = x_ref[...]
    x[rows:] = jnp.concatenate([after, before], axis=0).astype(BF16)
    for j in range(TAPS):
        product = rolled(jnp.dot(x[...], w1[j], preferred_element_type=F32), j)
        if j == 0:
            total[...] = product
        else:
            total[...] += product
    first_ref[0:rows] = jax.nn.gelu(total[0:rows]).astype(BF16)
    after = jax.nn.gelu(total[rows : rows + EDGE]) * has_after
    before = jax.nn.gelu(total[rows + EDGE :]) * has_before
    first_ref[rows:] = jnp.concatenate([after, before], axis=0).astype(BF16)


def second_kernel(first_ref, w2, wqkv, scale_hbm, *rest, heads, head, spread):
    hidden_ref, units, (total, scale_ref, sem) = rest[0], rest[1:-3], rest[-3:]
    scale_copy = pltpu.make_async_copy(scale_hbm, scale_ref, sem)
    scale_copy.start()
    rows = hidden_ref.shape[0]
    for j in range(TAPS):
        product = rolled(jnp.dot(first_ref[...], w2[j], preferred_element_type=F32), j)
        if j == 0:
            total[...] = product
        else:
            total[...] += product
    hidden_ref[...] = (first_ref[0:rows].astype(F32) + total[0:rows]).astype(BF16)
    scale_copy.wait()
    g = lax.axis_index("seq")
    project(hidden_ref, wqkv, scale_ref, units, g, range(len(units)), heads, head, spread)


def project(hidden_ref, wqkv, scale_ref, units, g, rounds, heads, head, spread):
    width = heads * head
    hidden = hidden_ref[...]
    for unit, r in zip(units, rounds):
        h = head_of(r, g, heads) if spread else r
        at = pl.multiple_of(h * head, head)
        weight = jnp.concatenate(
            [wqkv[:, pl.ds(part * width + at, head)] for part in range(3)], axis=1
        )
        projected = jnp.dot(hidden, weight, preferred_element_type=F32)
        q = head_rms(projected[:, :head]) * (scale_ref[h] / math.sqrt(head))
        unit[:, 0:head] = q.astype(BF16)
        unit[:, head : 2 * head] = head_rms(projected[:, head : 2 * head]).astype(BF16)
        unit[:, 2 * head :] = projected[:, 2 * head :].astype(BF16)


def third_kernel(hidden_ref, wqkv, scale_hbm, *rest, heads, head, spread):
    units, (scale_ref, sem) = rest[:-2], rest[-2:]
    scale_copy = pltpu.make_async_copy(scale_hbm, scale_ref, sem)
    scale_copy.start()
    scale_copy.wait()
    g = lax.axis_index("seq")
    rounds = range(heads - len(units), heads)
    project(hidden_ref, wqkv, scale_ref, units, g, rounds, heads, head, spread)


def head_of(r, g, heads):
    half = heads // 2
    side = g // heads
    return half * (side ^ 1 ^ (r // half)) + ((r % half) ^ (g % half))


def swaps(offset):
    count, batch_count = lax.axis_size("seq"), lax.axis_size("batch")
    pairs = []
    for g in range(count):
        for b in range(batch_count):
            to = ((g + offset) ^ 1) - offset
            target = (to, b) if 0 <= to < count else (g, b ^ 1 if b ^ 1 < batch_count else b)
            pairs.append((g * batch_count + b, target[0] * batch_count + target[1]))
    return pairs


def stem(block, conv_first, conv_second, qkv_weight, logit_scale, spread):
    rows, channels = block.shape
    width = conv_first.shape[2]
    heads = logit_scale.shape[0]
    head = qkv_weight.shape[1] // 3 // heads
    circle = rows + 2 * EDGE
    vmem = pl.BlockSpec(memory_space=pltpu.VMEM)
    hbm = pl.BlockSpec(memory_space=pltpu.HBM)
    shape = jax.ShapeDtypeStruct
    params = pltpu.CompilerParams(vmem_limit_bytes=24 * MIB)
    edge = shape((EDGE, channels), BF16)
    to_pair, to_other = pl.pallas_call(
        edges_kernel,
        out_shape=[edge, edge],
        in_specs=[hbm] * 2,
        out_specs=[vmem] * 2,
        scratch_shapes=[pltpu.VMEM((TILE, channels), BF16)] * 2
        + [pltpu.SemaphoreType.DMA((2,))],
        compiler_params=params,
        name="edges",
    )(
        pltpu.with_memory_space_constraint(block, pltpu.HBM),
        pltpu.with_memory_space_constraint(conv_first, pltpu.HBM),
    )
    pair = lax.ppermute(to_pair, ("seq", "batch"), swaps(0))
    other = lax.ppermute(to_other, ("seq", "batch"), swaps(1))
    first = pl.pallas_call(
        functools.partial(first_kernel, count=lax.axis_size("seq")),
        out_shape=shape((circle, width), BF16),
        in_specs=[vmem] * 4,
        out_specs=vmem,
        scratch_shapes=[pltpu.VMEM((circle, channels), BF16), pltpu.VMEM((circle, width), F32)],
        compiler_params=params,
        name="first",
    )(block, pair, other, conv_first)
    half = heads // 2
    fixed = dict(heads=heads, head=head, spread=spread)
    unit = shape((rows, 3 * head), BF16)
    scale_scratch = [pltpu.SMEM(logit_scale.shape, F32), pltpu.SemaphoreType.DMA]
    hidden, *units = pl.pallas_call(
        functools.partial(second_kernel, **fixed),
        out_shape=[shape((rows, width), BF16)] + [unit] * half,
        in_specs=[vmem] * 3 + [hbm],
        out_specs=[vmem] * (1 + half),
        scratch_shapes=[pltpu.VMEM((circle, width), F32)] + scale_scratch,
        compiler_params=params,
        name="second",
    )(first, conv_second, qkv_weight, logit_scale)
    units += pl.pallas_call(
        functools.partial(third_kernel, **fixed),
        out_shape=[unit] * (heads - half),
        in_specs=[vmem] * 2 + [hbm],
        out_specs=[vmem] * (heads - half),
        scratch_shapes=scale_scratch,
        compiler_params=pltpu.CompilerParams(vmem_limit_bytes=24 * MIB),
        name="third",
    )(hidden, qkv_weight, logit_scale)
    return [hidden, *units]


def scores_of(queries, keys):
    return lax.dot_general(
        queries, keys, (((1,), (1,)), ((), ())), preferred_element_type=F32
    )


def attend_units(queries, units, wide_sums=False):
    head = queries.shape[1]
    scores = [scores_of(queries, unit[:, head : 2 * head]) for unit in units]
    top = functools.reduce(jnp.maximum, [jnp.max(s, axis=1, keepdims=True) for s in scores])
    weights = [jnp.exp(s - top) for s in scores]
    values = jnp.concatenate([unit[:, 2 * head :] for unit in units], axis=0)
    if wide_sums:
        values = jnp.concatenate([values, jnp.ones_like(values)], axis=1)
    else:
        total = functools.reduce(jnp.add, [jnp.sum(w, axis=1, keepdims=True) for w in weights])
    weights = jnp.concatenate([w.astype(BF16) for w in weights], axis=1)
    mixed = jnp.dot(weights, values, preferred_element_type=F32)
    return (top, mixed[:, head:], mixed[:, :head]) if wide_sums else (top, total, mixed)


def attend_all_kernel(*refs, head, count):
    units, outs = refs[:-count], refs[-count:]
    for i in range(count):
        _, total, mixed = attend_units(units[i][:, 0:head], units)
        outs[i][...] = (mixed / total).astype(BF16)


def attend_some_kernel(*refs, head, count):
    units, (tops, totals, sums) = refs[:-3], refs[-3:]
    rows = units[0].shape[0]
    for i in range(count):
        part = slice(i * rows, (i + 1) * rows)
        top, total, sums[part] = attend_units(units[i][:, 0:head], units)
        tops[part] = jnp.broadcast_to(top, (rows, head))
        totals[part] = jnp.broadcast_to(total, (rows, head))


def attend_rest_kernel(*refs, head, count):
    units, (tops, totals, sums), outs = refs[: -3 - count], refs[-3 - count : -count], refs[-count:]
    rows = units[0].shape[0]
    for i in range(count):
        part = slice(i * rows, (i + 1) * rows)
        top, total, mixed = attend_units(units[i][:, 0:head], units[count:], wide_sums=True)
        top = jnp.broadcast_to(top, (rows, head))
        new_top = jnp.maximum(top, tops[part])
        old, new = jnp.exp(tops[part] - new_top), jnp.exp(top - new_top)
        total = totals[part] * old + total * new
        outs[i][...] = ((sums[part] * old + mixed * new) / total).astype(BF16)


def attend(kernel, count, out_shape, operands, name):
    vmem = pl.BlockSpec(memory_space=pltpu.VMEM)
    head = operands[0].shape[1] // 3
    return pl.pallas_call(
        functools.partial(kernel, head=head, count=count),
        out_shape=out_shape,
        in_specs=[vmem] * len(operands),
        out_specs=[vmem] * len(out_shape),
        compiler_params=pltpu.CompilerParams(vmem_limit_bytes=24 * MIB),
        name=name,
    )(*operands)


def attention(own, swap):
    half = len(own) // 2
    rows, wide = own[0].shape
    shape = jax.ShapeDtypeStruct
    result = [shape((rows, wide // 3), BF16)] * half
    partial = [shape((half * rows, wide // 3), F32)] * 3
    far, near = own[:half], own[half:]
    other = [swap(unit) for unit in own]
    last = other[half - 1]
    most = [*far, *near, *other[: half - 1], *other[half:]]
    part = attend(attend_some_kernel, half, partial, most, "most")
    far_outs = attend(attend_rest_kernel, half, result, [*far, last, *part], "last")
    far_outs, near = lax.optimization_barrier((far_outs, near))
    near_outs = attend(attend_all_kernel, half, result, [*near, *far, *other], "near")
    return [*far_outs, *near_outs]


def finish_kernel(hidden_ref, weight_ref, *rest, spread):
    mixed, out_ref = rest[:-1], rest[-1]
    g = lax.axis_index("seq")
    head = mixed[0].shape[1]
    total = hidden_ref[...].astype(F32)
    for r in range(len(mixed)):
        h = head_of(r, g, len(mixed)) if spread else r
        at = pl.multiple_of(h * head, head)
        total += jnp.dot(
            mixed[r][...], weight_ref[pl.ds(at, head), :], preferred_element_type=F32
        )
    out_ref[...] = total.astype(out_ref.dtype)


def finish(hidden, out_weight, mixed, spread):
    vmem = pl.BlockSpec(memory_space=pltpu.VMEM)
    return pl.pallas_call(
        functools.partial(finish_kernel, spread=spread),
        out_shape=jax.ShapeDtypeStruct(hidden.shape, BF16),
        in_specs=[vmem] * (2 + len(mixed)),
        out_specs=vmem,
        compiler_params=pltpu.CompilerParams(vmem_limit_bytes=32 * MIB),
        name="finish",
    )(hidden, out_weight, *mixed)


def routes(seq_count, batch_count, heads):
    half = heads // 2
    rounds = []
    for r in range(heads):
        pairs = []
        for g in range(seq_count):
            for b in range(batch_count):
                h = head_of(r, g, heads)
                chip = heads * (h // half) + half * (b % 2) + h % half
                core = (g // half + r // half) % 2
                target = chip * batch_count + b - b % 2 + core
                pairs.append((g * batch_count + b, target))
        rounds.append(pairs)
    return rounds


def by_heads(sequence_input, conv_first, conv_second, qkv_weight, out_weight, logit_scale):
    heads = logit_scale.shape[0]
    count = lax.axis_size("seq")
    batch_count = lax.axis_size("batch")
    hidden, *units = stem(
        sequence_input, conv_first, conv_second, qkv_weight, logit_scale, True
    )
    both = ("seq", "batch")
    rounds = routes(count, batch_count, heads)
    own = [lax.ppermute(unit, both, pairs) for unit, pairs in zip(units, rounds)]
    cores = [(b, b ^ 1) for b in range(batch_count)]
    outs = attention(own, lambda unit: lax.ppermute(unit, "batch", cores))
    mixed = [
        lax.ppermute(out, both, [(target, source) for source, target in pairs])
        for out, pairs in zip(outs, rounds)
    ]
    return finish(hidden, out_weight, mixed, True)


def by_gather(sequence_input, conv_first, conv_second, qkv_weight, out_weight, logit_scale):
    heads = logit_scale.shape[0]
    count = lax.axis_size("seq")
    hidden, *units = stem(
        sequence_input, conv_first, conv_second, qkv_weight, logit_scale, False
    )
    head = units[0].shape[1] // 3
    pairs = jnp.concatenate([unit[:, head:] for unit in units], axis=1)
    everywhere = lax.all_gather(pairs, "seq", axis=0, tiled=True)
    mixed = []
    for h in range(heads):
        at = 2 * h * head
        scores = lax.dot_general(
            units[h][:, :head],
            everywhere[:, at : at + head],
            (((1,), (1,)), ((), ())),
            preferred_element_type=F32,
        )
        weights = jnp.exp(scores - jnp.max(scores, axis=1, keepdims=True))
        denominators = jnp.sum(weights, axis=1, keepdims=True)
        out = jnp.dot(
            weights.astype(BF16),
            everywhere[:, at + head : at + 2 * head],
            preferred_element_type=F32,
        )
        mixed.append((out / denominators).astype(BF16))
    return finish(hidden, out_weight, mixed, False)


def solution(mesh):
    def body(*args):
        heads = args[-1].shape[0]
        fits = heads == 4 and mesh.shape["seq"] == 2 * heads and mesh.shape["batch"] % 2 == 0
        return (by_heads if fits else by_gather)(*args)

    in_specs = (P(("batch", "seq"), None), P(), P(), P(), P(), P())
    out_specs = P(("batch", "seq"), None)
    return jax.shard_map(body, mesh=mesh, in_specs=in_specs, out_specs=out_specs, check_vma=False)
```

time: 52.6 us -> 49.2 us (0.935)
  Pallas kernels: 17.1 us -> 13.8 us
    pallas_call x6 -> x7, Pallas kernels: 15.8 us -> 12.5 us  [the longest x3 3.91 us: attend(): pl.pallas_call(functools.partial(kernel, head=head, count=count), out_sha...]
    ppermute x4, starting transfers between devices: 12.2 us -> 9.49 us  [by_heads(): outs = attention(own, lambda unit: lax.ppermute(unit, 'batch', cores))]
    ppermute x4, starting transfers between devices: 6.81 us -> 9.11 us  [by_heads(): lax.ppermute(unit, both, pairs)]
    ppermute x4, waiting for transfers between devices: 1.21 us -> 0.01 us  [by_heads(): outs = attention(own, lambda unit: lax.ppermute(unit, 'batch', cores))]
    ppermute x1, waiting for transfers between devices: 0.01 us -> 0.66 us  [stem(): other = lax.ppermute(to_other, ('seq', 'batch'), swaps(1))]
  transfers between devices with their start and end apart: 14 -> 14, of which waited for: 7 -> 8; matrix products, arithmetic and copies ran while one was open for 0% -> 0% of each run, Pallas kernels for 10% -> 9%
where the time goes in v3:
time: 49.2 us; the launch traced here: 49.1 us
  starting transfers between devices  26.3 us (53%)
  Pallas kernels  13.8 us (28%)
  waiting for transfers between devices  8.79 us (18%)
    ppermute x4, starting transfers between devices, by_heads(): outs = attention(own, lambda unit: lax.ppermute(unit, 'batch', cores))  9.49 us
    ppermute x4, starting transfers between devices, by_heads(): lax.ppermute(unit, both, pairs)  9.11 us
    ppermute x4, starting transfers between devices, by_heads(): lax.ppermute(out, both, [(target, source) for source, target in pairs])  4.57 us
    ppermute x4, waiting for transfers between devices, by_heads(): lax.ppermute(out, both, [(target, source) for source, target in pairs])  3.99 us
    ppermute x4, waiting for transfers between devices, by_heads(): lax.ppermute(unit, both, pairs)  3.94 us
    pallas_call x3, Pallas kernels, attend(): pl.pallas_call(functools.partial(kernel, head=head, count=count), out_sha...  3.91 us
    pallas_call x1, Pallas kernels, stem(): pl.pallas_call(functools.partial(first_kernel, count=lax.axis_size('seq')...  3.6 us
    pallas_call x1, Pallas kernels, stem(): pl.pallas_call(functools.partial(second_kernel, **fixed), out_shape=[shap...  2.75 us
  transfers between devices with their start and end apart: 14, of which 8 were waited for; matrix products, arithmetic and copies ran while one was open for 0% of the time, Pallas kernels for 9%

profile of v3, /device:TPU:1, one launch (start us, length us, event | category | flops | bytes accessed | tf_op | source)
XLA Modules:
  0.0 49.1 jit_solution(8561580813170891617)
XLA Ops:
  0.0 1.0 %edges.1 = (bf16[8,1536]{1,0:T(8,128)(2,1)S(1)}, bf16[8,1536]{1,0:T(8,128)(2,1)S(1)}) custom-call(bf16[256,1536]{1,0:T(8,128)(2,1)} %x_ref.1, bf16[5,1536,768]{2,1,0:T(8,128)(2,1)} %w1.1), custom_call_target="tpu_custom_call" | custom-call | tf_op jit(solution)/shard_map/edges/pallas_call | solution.py:139
  1.0 2.1 %collective-permute-start = (bf16[8,1536]{1,0:T(8,128)(2,1)S(1)}, bf16[8,1536]{1,0:T(8,128)(2,1)S(1)}, u32[]{:S(2)}, u32[]{:S(2)}) collective-permute-start(bf16[8,1536]{1,0:T(8,128)(2,1)S(1)} %get-tuple-element.23), channel_id=1, source_target_pairs={{0,4},{1,5},{2,6},{3,7},{4,0},{5,1},{6,2},{7,3},{8,12},{9,13},{10,... | collective-permute-start | bytes 73736 | tf_op jit(solution)/shard_map/ppermute | solution.py:152
  3.1 1.0 %collective-permute-start.1 = (bf16[8,1536]{1,0:T(8,128)(2,1)S(1)}, bf16[8,1536]{1,0:T(8,128)(2,1)S(1)}, u32[]{:S(2)}, u32[]{:S(2)}) collective-permute-start(bf16[8,1536]{1,0:T(8,128)(2,1)S(1)} %get-tuple-element.24), channel_id=1, source_target_pairs={{0,1},{1,0},{2,3},{3,2},{4,8},{5,9},{6,10},{7,11},{8,4},{9,5},{10,... | collective-permute-start | bytes 73736 | tf_op jit(solution)/shard_map/ppermute | solution.py:153
  4.1 0.2 collective-permute-done.pair_ref
  4.3 0.7 %collective-permute-done.1.other_ref = bf16[8,1536]{1,0:T(8,128)(2,1)S(1)} collective-permute-done((bf16[8,1536]{1,0:T(8,128)(2,1)S(1)}, bf16[8,1536]{1,0:T(8,128)(2,1)S(1)}, u32[]{:S(2)}, u32[]{:S(2)}) %collective-permute-start.1) | collective-permute-done | bytes 24608 | tf_op jit(solution)/shard_map/ppermute | solution.py:153
  5.0 3.6 %first.1.first_ref = bf16[272,768]{1,0:T(8,128)(2,1)S(1)} custom-call(bf16[256,1536]{1,0:T(8,128)(2,1)S(1)} %copy-done.2, bf16[8,1536]{1,0:T(8,128)(2,1)S(1)} %collective-permute-done.pair_ref, bf16[8,1536]{1,0:T(8,128)(2,1)S(1)} %collective-permute-done.1.other_ref, bf16[5,1536,768]{2,1,0:T(8,128)(2,1)S(1)} %copy-done), custom_call_target="tpu_custom_call" | custom-call | tf_op jit(solution)/shard_map/first/pallas_call | solution.py:154
  8.7 0.0 copy-start.3
  8.7 2.8 %second.1 = (bf16[256,768]{1,0:T(8,128)(2,1)S(1)}, bf16[256,384]{1,0:T(8,128)(2,1)S(1)}, bf16[256,384]{1,0:T(8,128)(2,1)S(1)}) custom-call(bf16[272,768]{1,0:T(8,128)(2,1)S(1)} %first.1.first_ref, bf16[5,768,768]{2,1,0:T(8,128)(2,1)S(1)} %bitcast.1, bf16[768,1536]{1,0:T(8,128)(2,1)S(1)} %copy-done.1, f32[4]{0:T(128)S(1)} %copy-done.4), custom_call_target="tpu_custom_call" | custom-call | tf_op jit(solution)/shard_map/second/pallas_call | solution.py:167
  11.4 7.1 %collective-permute-start.2 = (bf16[256,384]{1,0:T(8,128)(2,1)S(1)}, bf16[256,384]{1,0:T(8,128)(2,1)S(1)}, u32[]{:S(2)}, u32[]{:S(2)}) collective-permute-start(bf16[256,384]{1,0:T(8,128)(2,1)S(1)} %get-tuple-element.26), channel_id=1, source_target_pairs={{0,16},{1,24},{2,18},{3,26},{4,20},{5,28},{6,22},{7,30},{8,17},{9,... | collective-permute-start | bytes 589832 | tf_op jit(solution)/shard_map/ppermute | solution.py:320
  18.6 1.2 %third.1 = (bf16[256,384]{1,0:T(8,128)(2,1)S(1)}, bf16[256,384]{1,0:T(8,128)(2,1)S(1)}) custom-call(bf16[256,768]{1,0:T(8,128)(2,1)S(1)} %get-tuple-element.25.hidden_ref, bf16[768,1536]{1,0:T(8,128)(2,1)S(1)} %copy-done.1, f32[4]{0:T(128)S(1)} %copy-done.4), custom_call_target="tpu_custom_call" | custom-call | tf_op jit(solution)/shard_map/third/pallas_call | solution.py:176
  19.8 0.1 collective-permute-start.5
  19.9 0.1 collective-permute-start.6
  19.9 1.8 %collective-permute-start.3 = (bf16[256,384]{1,0:T(8,128)(2,1)S(1)}, bf16[256,384]{1,0:T(8,128)(2,1)S(1)}, u32[]{:S(2)}, u32[]{:S(2)}) collective-permute-start(bf16[256,384]{1,0:T(8,128)(2,1)S(1)} %get-tuple-element.27), channel_id=1, source_target_pairs={{0,20},{1,28},{2,22},{3,30},{4,16},{5,24},{6,18},{7,26},{8,21},{9,... | collective-permute-start | bytes 589832 | tf_op jit(solution)/shard_map/ppermute | solution.py:320
  21.8 1.5 %collective-permute-done.2.refs_0_.refs_2_ = bf16[256,384]{1,0:T(8,128)(2,1)S(1)} collective-permute-done((bf16[256,384]{1,0:T(8,128)(2,1)S(1)}, bf16[256,384]{1,0:T(8,128)(2,1)S(1)}, u32[]{:S(2)}, u32[]{:S(2)}) %collective-permute-start.2) | collective-permute-done | bytes 196640 | tf_op jit(solution)/shard_map/ppermute | solution.py:320
  23.3 4.3 %collective-permute-start.7 = (bf16[256,384]{1,0:T(8,128)(2,1)S(1)}, bf16[256,384]{1,0:T(8,128)(2,1)S(1)}, u32[]{:S(2)}, u32[]{:S(2)}) collective-permute-start(bf16[256,384]{1,0:T(8,128)(2,1)S(1)} %collective-permute-done.2.refs_0_.refs_2_), channel_id=1, source_target_pairs={{0,1},{1,0},{2,3},{3,2},{4,5},{5,4},{6,7},{7,6},{8,9},{9,8},{10,11... | collective-permute-start | bytes 589832 | tf_op jit(solution)/shard_map/ppermute | solution.py:322
  27.6 0.0 collective-permute-done.5.refs_2_.refs_0_
  27.6 0.0 collective-permute-start.8
  27.6 2.0 %collective-permute-done.6.refs_3_.refs_1_ = bf16[256,384]{1,0:T(8,128)(2,1)S(1)} collective-permute-done((bf16[256,384]{1,0:T(8,128)(2,1)S(1)}, bf16[256,384]{1,0:T(8,128)(2,1)S(1)}, u32[]{:S(2)}, u32[]{:S(2)}) %collective-permute-start.6) | collective-permute-done | bytes 196640 | tf_op jit(solution)/shard_map/ppermute | solution.py:320
  29.5 1.7 %collective-permute-start.9 = (bf16[256,384]{1,0:T(8,128)(2,1)S(1)}, bf16[256,384]{1,0:T(8,128)(2,1)S(1)}, u32[]{:S(2)}, u32[]{:S(2)}) collective-permute-start(bf16[256,384]{1,0:T(8,128)(2,1)S(1)} %collective-permute-done.6.refs_3_.refs_1_), channel_id=1, source_target_pairs={{0,1},{1,0},{2,3},{3,2},{4,5},{5,4},{6,7},{7,6},{8,9},{9,8},{10,11... | collective-permute-start | bytes 589832 | tf_op jit(solution)/shard_map/ppermute | solution.py:322
  31.2 0.5 %collective-permute-done.3.refs_1_.refs_3_ = bf16[256,384]{1,0:T(8,128)(2,1)S(1)} collective-permute-done((bf16[256,384]{1,0:T(8,128)(2,1)S(1)}, bf16[256,384]{1,0:T(8,128)(2,1)S(1)}, u32[]{:S(2)}, u32[]{:S(2)}) %collective-permute-start.3) | collective-permute-done | bytes 196640 | tf_op jit(solution)/shard_map/ppermute | solution.py:320
  31.7 3.5 %collective-permute-start.4 = (bf16[256,384]{1,0:T(8,128)(2,1)S(1)}, bf16[256,384]{1,0:T(8,128)(2,1)S(1)}, u32[]{:S(2)}, u32[]{:S(2)}) collective-permute-start(bf16[256,384]{1,0:T(8,128)(2,1)S(1)} %collective-permute-done.3.refs_1_.refs_3_), channel_id=1, source_target_pairs={{0,1},{1,0},{2,3},{3,2},{4,5},{5,4},{6,7},{7,6},{8,9},{9,8},{10,11... | collective-permute-start | bytes 589832 | tf_op jit(solution)/shard_map/ppermute | solution.py:322
  35.2 1.7 %most.1 = (f32[512,128]{1,0:T(8,128)S(1)}, f32[512,128]{1,0:T(8,128)S(1)}, f32[512,128]{1,0:T(8,128)S(1)}) custom-call(bf16[256,384]{1,0:T(8,128)(2,1)S(1)} %collective-permute-done.2.refs_0_.refs_2_, bf16[256,384]{1,0:T(8,128)(2,1)S(1)} %collective-permute-done.3.refs_1_.refs_3_, bf16[256,384]{1,0:T(8,128)(2,1)S(1)} %collective-permute-done.5.refs_2_.refs_0_, ...), custom_call_target="tpu_custom_call" | custom-call | tf_op jit(solution)/shard_map/most/pallas_call | solution.py:242
  36.9 0.5 %last.1 = (bf16[256,128]{1,0:T(8,128)(2,1)S(1)}, bf16[256,128]{1,0:T(8,128)(2,1)S(1)}) custom-call(bf16[256,384]{1,0:T(8,128)(2,1)S(1)} %collective-permute-done.2.refs_0_.refs_2_, bf16[256,384]{1,0:T(8,128)(2,1)S(1)} %collective-permute-done.3.refs_1_.refs_3_, bf16[256,384]{1,0:T(8,128)(2,1)S(1)} %collective-permute-done.4.refs_2_.refs_5_, ...), custom_call_target="tpu_custom_call" | custom-call | tf_op jit(solution)/shard_map/last/pallas_call | solution.py:242
  37.4 1.2 %collective-permute-start.10 = (bf16[256,128]{1,0:T(8,128)(2,1)S(1)}, bf16[256,128]{1,0:T(8,128)(2,1)S(1)}, u32[]{:S(2)}, u32[]{:S(2)}) collective-permute-start(bf16[256,128]{1,0:T(8,128)(2,1)S(1)} %get-tuple-element.35), channel_id=1, source_target_pairs={{16,0},{24,1},{18,2},{26,3},{20,4},{28,5},{22,6},{30,7},{17,8},{25... | collective-permute-start | bytes 196616 | tf_op jit(solution)/shard_map/ppermute | solution.py:324
  38.6 3.3 %collective-permute-start.11 = (bf16[256,128]{1,0:T(8,128)(2,1)S(1)}, bf16[256,128]{1,0:T(8,128)(2,1)S(1)}, u32[]{:S(2)}, u32[]{:S(2)}) collective-permute-start(bf16[256,128]{1,0:T(8,128)(2,1)S(1)} %get-tuple-element.36), channel_id=1, source_target_pairs={{20,0},{28,1},{22,2},{30,3},{16,4},{24,5},{18,6},{26,7},{21,8},{29... | collective-permute-start | bytes 196616 | tf_op jit(solution)/shard_map/ppermute | solution.py:324
  41.8 1.7 %near.1 = (bf16[256,128]{1,0:T(8,128)(2,1)S(1)}, bf16[256,128]{1,0:T(8,128)(2,1)S(1)}) custom-call(bf16[256,384]{1,0:T(8,128)(2,1)S(1)} %collective-permute-done.5.refs_2_.refs_0_, bf16[256,384]{1,0:T(8,128)(2,1)S(1)} %collective-permute-done.6.refs_3_.refs_1_, bf16[256,384]{1,0:T(8,128)(2,1)S(1)} %collective-permute-done.2.refs_0_.refs_2_, ...), custom_call_target="tpu_custom_call" | custom-call | tf_op jit(solution)/shard_map/near/pallas_call | solution.py:242
  43.6 0.1 collective-permute-start.12
  43.7 0.1 collective-permute-start.13
  43.8 2.0 %collective-permute-done.11.rest_1_ = bf16[256,128]{1,0:T(8,128)(2,1)S(1)} collective-permute-done((bf16[256,128]{1,0:T(8,128)(2,1)S(1)}, bf16[256,128]{1,0:T(8,128)(2,1)S(1)}, u32[]{:S(2)}, u32[]{:S(2)}) %collective-permute-start.11) | collective-permute-done | bytes 65568 | tf_op jit(solution)/shard_map/ppermute | solution.py:324
  45.8 1.4 %collective-permute-done.12.rest_2_ = bf16[256,128]{1,0:T(8,128)(2,1)S(1)} collective-permute-done((bf16[256,128]{1,0:T(8,128)(2,1)S(1)}, bf16[256,128]{1,0:T(8,128)(2,1)S(1)}, u32[]{:S(2)}, u32[]{:S(2)}) %collective-permute-start.12) | collective-permute-done | bytes 65568 | tf_op jit(solution)/shard_map/ppermute | solution.py:324
  47.2 0.5 %collective-permute-done.13.rest_3_ = bf16[256,128]{1,0:T(8,128)(2,1)S(1)} collective-permute-done((bf16[256,128]{1,0:T(8,128)(2,1)S(1)}, bf16[256,128]{1,0:T(8,128)(2,1)S(1)}, u32[]{:S(2)}, u32[]{:S(2)}) %collective-permute-start.13) | collective-permute-done | bytes 65568 | tf_op jit(solution)/shard_map/ppermute | solution.py:324
  47.8 1.3 %finish.1 = bf16[256,768]{1,0:T(8,128)(2,1)} custom-call(bf16[256,768]{1,0:T(8,128)(2,1)S(1)} %get-tuple-element.25.hidden_ref, bf16[512,768]{1,0:T(8,128)(2,1)S(1)} %copy-done.3, bf16[256,128]{1,0:T(8,128)(2,1)S(1)} %collective-permute-done.10.rest_0_, bf16[256,128]{1,0:T(8,128)(2,1)S(1)} %collective-permute-done.11.rest_1_, ...), custom_call_target="tpu_custom_call" | custom-call | tf_op jit(solution)/shard_map/finish/pallas_call | solution.py:285
  (19 shorter events, 0.0 us)
Async XLA Ops:
  0.0 5.0 %copy-start = (bf16[5,1536,768]{2,1,0:T(8,128)(2,1)S(1)}, bf16[5,1536,768]{2,1,0:T(8,128)(2,1)}, u32[]{:S(2)}) copy-start(bf16[5,1536,768]{2,1,0:T(8,128)(2,1)} %w1.1) | copy-start | bytes 35389444
  0.0 5.0 %copy-start.2 = (bf16[256,1536]{1,0:T(8,128)(2,1)S(1)}, bf16[256,1536]{1,0:T(8,128)(2,1)}, u32[]{:S(2)}) copy-start(bf16[256,1536]{1,0:T(8,128)(2,1)} %x_ref.1) | copy-start | bytes 2359300
  1.0 3.3 %collective-permute-start = (bf16[8,1536]{1,0:T(8,128)(2,1)S(1)}, bf16[8,1536]{1,0:T(8,128)(2,1)S(1)}, u32[]{:S(2)}, u32[]{:S(2)}) collective-permute-start(bf16[8,1536]{1,0:T(8,128)(2,1)S(1)} %get-tuple-element.23), channel_id=1, source_target_pairs={{0,4},{1,5},{2,6},{3,7},{4,0},{5,1},{6,2},{7,3},{8,12},{9,13},{10,... | collective-permute-start | bytes 73736 | tf_op jit(solution)/shard_map/ppermute | solution.py:152
  3.1 5.5 %slice-start = ((s8[5898240]{0:T(1024)(128)(4,1)}), s8[4194304]{0:T(1024)(128)(4,1)S(1)}, s32[]{:S(2)}) async-start(s8[5898240]{0:T(1024)(128)(4,1)} %bitcast), calls=%async_computation | async-start | bytes 8388608
  3.1 5.5 %copy-start.1 = (bf16[768,1536]{1,0:T(8,128)(2,1)S(1)}, bf16[768,1536]{1,0:T(8,128)(2,1)}, u32[]{:S(2)}) copy-start(bf16[768,1536]{1,0:T(8,128)(2,1)} %wqkv.3) | copy-start | bytes 7077892
  3.1 5.5 %slice-start.1 = ((s8[5898240]{0:T(1024)(128)(4,1)}), s8[1703936]{0:T(1024)(128)(4,1)S(1)}, s32[]{:S(2)}) async-start(s8[5898240]{0:T(1024)(128)(4,1)} %bitcast), calls=%async_computation.1 | async-start | bytes 3407872
  3.1 5.5 %copy-start.4 = (f32[4]{0:T(128)S(1)}, f32[4]{0:T(128)}, u32[]{:S(2)}) copy-start(f32[4]{0:T(128)} %scale_hbm.3) | copy-start | bytes 52
  3.1 1.9 %collective-permute-start.1 = (bf16[8,1536]{1,0:T(8,128)(2,1)S(1)}, bf16[8,1536]{1,0:T(8,128)(2,1)S(1)}, u32[]{:S(2)}, u32[]{:S(2)}) collective-permute-start(bf16[8,1536]{1,0:T(8,128)(2,1)S(1)} %get-tuple-element.24), channel_id=1, source_target_pairs={{0,1},{1,0},{2,3},{3,2},{4,8},{5,9},{6,10},{7,11},{8,4},{9,5},{10,... | collective-permute-start | bytes 73736 | tf_op jit(solution)/shard_map/ppermute | solution.py:153
  8.7 39.1 %copy-start.3 = (bf16[512,768]{1,0:T(8,128)(2,1)S(1)}, bf16[512,768]{1,0:T(8,128)(2,1)}, u32[]{:S(2)}) copy-start(bf16[512,768]{1,0:T(8,128)(2,1)} %weight_ref.1) | copy-start | bytes 2359300
  11.4 11.8 %collective-permute-start.2 = (bf16[256,384]{1,0:T(8,128)(2,1)S(1)}, bf16[256,384]{1,0:T(8,128)(2,1)S(1)}, u32[]{:S(2)}, u32[]{:S(2)}) collective-permute-start(bf16[256,384]{1,0:T(8,128)(2,1)S(1)} %get-tuple-element.26), channel_id=1, source_target_pairs={{0,16},{1,24},{2,18},{3,26},{4,20},{5,28},{6,22},{7,30},{8,17},{9,... | collective-permute-start | bytes 589832 | tf_op jit(solution)/shard_map/ppermute | solution.py:320
  19.8 7.8 %collective-permute-start.5 = (bf16[256,384]{1,0:T(8,128)(2,1)S(1)}, bf16[256,384]{1,0:T(8,128)(2,1)S(1)}, u32[]{:S(2)}, u32[]{:S(2)}) collective-permute-start(bf16[256,384]{1,0:T(8,128)(2,1)S(1)} %get-tuple-element.28), channel_id=1, source_target_pairs={{0,1},{1,9},{2,3},{3,11},{4,5},{5,13},{6,7},{7,15},{8,0},{9,8},{10... | collective-permute-start | bytes 589832 | tf_op jit(solution)/shard_map/ppermute | solution.py:320
  19.9 9.7 %collective-permute-start.6 = (bf16[256,384]{1,0:T(8,128)(2,1)S(1)}, bf16[256,384]{1,0:T(8,128)(2,1)S(1)}, u32[]{:S(2)}, u32[]{:S(2)}) collective-permute-start(bf16[256,384]{1,0:T(8,128)(2,1)S(1)} %get-tuple-element.29), channel_id=1, source_target_pairs={{0,5},{1,13},{2,7},{3,15},{4,1},{5,9},{6,3},{7,11},{8,4},{9,12},{1... | collective-permute-start | bytes 589832 | tf_op jit(solution)/shard_map/ppermute | solution.py:320
  19.9 11.7 %collective-permute-start.3 = (bf16[256,384]{1,0:T(8,128)(2,1)S(1)}, bf16[256,384]{1,0:T(8,128)(2,1)S(1)}, u32[]{:S(2)}, u32[]{:S(2)}) collective-permute-start(bf16[256,384]{1,0:T(8,128)(2,1)S(1)} %get-tuple-element.27), channel_id=1, source_target_pairs={{0,20},{1,28},{2,22},{3,30},{4,16},{5,24},{6,18},{7,26},{8,21},{9,... | collective-permute-start | bytes 589832 | tf_op jit(solution)/shard_map/ppermute | solution.py:320
  23.3 12.0 %collective-permute-start.7 = (bf16[256,384]{1,0:T(8,128)(2,1)S(1)}, bf16[256,384]{1,0:T(8,128)(2,1)S(1)}, u32[]{:S(2)}, u32[]{:S(2)}) collective-permute-start(bf16[256,384]{1,0:T(8,128)(2,1)S(1)} %collective-permute-done.2.refs_0_.refs_2_), channel_id=1, source_target_pairs={{0,1},{1,0},{2,3},{3,2},{4,5},{5,4},{6,7},{7,6},{8,9},{9,8},{10,11... | collective-permute-start | bytes 589832 | tf_op jit(solution)/shard_map/ppermute | solution.py:322
  27.6 7.6 %collective-permute-start.8 = (bf16[256,384]{1,0:T(8,128)(2,1)S(1)}, bf16[256,384]{1,0:T(8,128)(2,1)S(1)}, u32[]{:S(2)}, u32[]{:S(2)}) collective-permute-start(bf16[256,384]{1,0:T(8,128)(2,1)S(1)} %collective-permute-done.5.refs_2_.refs_0_), channel_id=1, source_target_pairs={{0,1},{1,0},{2,3},{3,2},{4,5},{5,4},{6,7},{7,6},{8,9},{9,8},{10,11... | collective-permute-start | bytes 589832 | tf_op jit(solution)/shard_map/ppermute | solution.py:322
  29.5 5.7 %collective-permute-start.9 = (bf16[256,384]{1,0:T(8,128)(2,1)S(1)}, bf16[256,384]{1,0:T(8,128)(2,1)S(1)}, u32[]{:S(2)}, u32[]{:S(2)}) collective-permute-start(bf16[256,384]{1,0:T(8,128)(2,1)S(1)} %collective-permute-done.6.refs_3_.refs_1_), channel_id=1, source_target_pairs={{0,1},{1,0},{2,3},{3,2},{4,5},{5,4},{6,7},{7,6},{8,9},{9,8},{10,11... | collective-permute-start | bytes 589832 | tf_op jit(solution)/shard_map/ppermute | solution.py:322
  31.7 5.2 %collective-permute-start.4 = (bf16[256,384]{1,0:T(8,128)(2,1)S(1)}, bf16[256,384]{1,0:T(8,128)(2,1)S(1)}, u32[]{:S(2)}, u32[]{:S(2)}) collective-permute-start(bf16[256,384]{1,0:T(8,128)(2,1)S(1)} %collective-permute-done.3.refs_1_.refs_3_), channel_id=1, source_target_pairs={{0,1},{1,0},{2,3},{3,2},{4,5},{5,4},{6,7},{7,6},{8,9},{9,8},{10,11... | collective-permute-start | bytes 589832 | tf_op jit(solution)/shard_map/ppermute | solution.py:322
  37.4 6.3 %collective-permute-start.10 = (bf16[256,128]{1,0:T(8,128)(2,1)S(1)}, bf16[256,128]{1,0:T(8,128)(2,1)S(1)}, u32[]{:S(2)}, u32[]{:S(2)}) collective-permute-start(bf16[256,128]{1,0:T(8,128)(2,1)S(1)} %get-tuple-element.35), channel_id=1, source_target_pairs={{16,0},{24,1},{18,2},{26,3},{20,4},{28,5},{22,6},{30,7},{17,8},{25... | collective-permute-start | bytes 196616 | tf_op jit(solution)/shard_map/ppermute | solution.py:324
  38.6 7.2 %collective-permute-start.11 = (bf16[256,128]{1,0:T(8,128)(2,1)S(1)}, bf16[256,128]{1,0:T(8,128)(2,1)S(1)}, u32[]{:S(2)}, u32[]{:S(2)}) collective-permute-start(bf16[256,128]{1,0:T(8,128)(2,1)S(1)} %get-tuple-element.36), channel_id=1, source_target_pairs={{20,0},{28,1},{22,2},{30,3},{16,4},{24,5},{18,6},{26,7},{21,8},{29... | collective-permute-start | bytes 196616 | tf_op jit(solution)/shard_map/ppermute | solution.py:324
  43.6 3.6 %collective-permute-start.12 = (bf16[256,128]{1,0:T(8,128)(2,1)S(1)}, bf16[256,128]{1,0:T(8,128)(2,1)S(1)}, u32[]{:S(2)}, u32[]{:S(2)}) collective-permute-start(bf16[256,128]{1,0:T(8,128)(2,1)S(1)} %get-tuple-element.39), channel_id=1, source_target_pairs={{1,0},{9,1},{3,2},{11,3},{5,4},{13,5},{7,6},{15,7},{0,8},{8,9},{2,... | collective-permute-start | bytes 196616 | tf_op jit(solution)/shard_map/ppermute | solution.py:324
  43.7 4.1 %collective-permute-start.13 = (bf16[256,128]{1,0:T(8,128)(2,1)S(1)}, bf16[256,128]{1,0:T(8,128)(2,1)S(1)}, u32[]{:S(2)}, u32[]{:S(2)}) collective-permute-start(bf16[256,128]{1,0:T(8,128)(2,1)S(1)} %get-tuple-element.40), channel_id=1, source_target_pairs={{5,0},{13,1},{7,2},{15,3},{1,4},{9,5},{3,6},{11,7},{4,8},{12,9},{6... | collective-permute-start | bytes 196616 | tf_op jit(solution)/shard_map/ppermute | solution.py:324

commit v4 on v3

--- a/solution.py
+++ b/solution.py
@@ -160,7 +160,7 @@
         compiler_params=params,
         name="first",
     )(block, pair, other, conv_first)
-    half = heads // 2
+    half = 1
     fixed = dict(heads=heads, head=head, spread=spread)
     unit = shape((rows, 3 * head), BF16)
     scale_scratch = [pltpu.SMEM(logit_scale.shape, F32), pltpu.SemaphoreType.DMA]
@@ -250,40 +250,42 @@
 
 
 def attention(own, swap):
-    half = len(own) // 2
     rows, wide = own[0].shape
     shape = jax.ShapeDtypeStruct
-    result = [shape((rows, wide // 3), BF16)] * half
-    partial = [shape((half * rows, wide // 3), F32)] * 3
-    far, near = own[:half], own[half:]
+    steps = [0, 1], [2, 3]
+    result = [shape((rows, wide // 3), BF16)] * len(steps[0])
+    partial = [shape((len(steps[0]) * rows, wide // 3), F32)] * 3
     other = [swap(unit) for unit in own]
-    last = other[half - 1]
-    most = [*far, *near, *other[: half - 1], *other[half:]]
-    part = attend(attend_some_kernel, half, partial, most, "most")
-    far_outs = attend(attend_rest_kernel, half, result, [*far, last, *part], "last")
-    far_outs, near = lax.optimization_barrier((far_outs, near))
-    near_outs = attend(attend_all_kernel, half, result, [*near, *far, *other], "near")
-    return [*far_outs, *near_outs]
-
-
-def finish_kernel(hidden_ref, weight_ref, *rest, spread):
+    last = len(own) // 2 - 1
+    queries = [own[r] for r in steps[0]]
+    most = queries + [own[r] for r in steps[1]] + other[:last] + other[last + 1 :]
+    part = attend(attend_some_kernel, len(queries), partial, most, "most")
+    outs = attend(attend_rest_kernel, len(queries), result, [*queries, other[last], *part], "last")
+    outs, own = lax.optimization_barrier((outs, own))
+    queries = [own[r] for r in steps[1]]
+    keys = queries + [own[r] for r in steps[0]] + other
+    outs = outs + attend(attend_all_kernel, len(queries), result, keys, "near")
+    return outs, steps[0] + steps[1]
+
+
+def finish_kernel(hidden_ref, weight_ref, *rest, rounds, spread):
     mixed, out_ref = rest[:-1], rest[-1]
     g = lax.axis_index("seq")
     head = mixed[0].shape[1]
     total = hidden_ref[...].astype(F32)
-    for r in range(len(mixed)):
+    for r, part in zip(rounds, mixed):
         h = head_of(r, g, len(mixed)) if spread else r
         at = pl.multiple_of(h * head, head)
         total += jnp.dot(
-            mixed[r][...], weight_ref[pl.ds(at, head), :], preferred_element_type=F32
+            part[...], weight_ref[pl.ds(at, head), :], preferred_element_type=F32
         )
     out_ref[...] = total.astype(out_ref.dtype)
 
 
-def finish(hidden, out_weight, mixed, spread):
+def finish(hidden, out_weight, mixed, rounds, spread):
     vmem = pl.BlockSpec(memory_space=pltpu.VMEM)
     return pl.pallas_call(
-        functools.partial(finish_kernel, spread=spread),
+        functools.partial(finish_kernel, rounds=rounds, spread=spread),
         out_shape=jax.ShapeDtypeStruct(hidden.shape, BF16),
         in_specs=[vmem] * (2 + len(mixed)),
         out_specs=vmem,
@@ -319,12 +321,12 @@
     rounds = routes(count, batch_count, heads)
     own = [lax.ppermute(unit, both, pairs) for unit, pairs in zip(units, rounds)]
     cores = [(b, b ^ 1) for b in range(batch_count)]
-    outs = attention(own, lambda unit: lax.ppermute(unit, "batch", cores))
+    outs, order = attention(own, lambda unit: lax.ppermute(unit, "batch", cores))
     mixed = [
-        lax.ppermute(out, both, [(target, source) for source, target in pairs])
-        for out, pairs in zip(outs, rounds)
+        lax.ppermute(out, both, [(target, source) for source, target in rounds[r]])
+        for out, r in zip(outs, order)
     ]
-    return finish(hidden, out_weight, mixed, True)
+    return finish(hidden, out_weight, mixed, order, True)
 
 
 def by_gather(sequence_input, conv_first, conv_second, qkv_weight, out_weight, logit_scale):
@@ -353,7 +355,7 @@
             preferred_element_type=F32,
         )
         mixed.append((out / denominators).astype(BF16))
-    return finish(hidden, out_weight, mixed, False)
+    return finish(hidden, out_weight, mixed, range(heads), False)
 
 
 def solution(mesh):

time: 49.2 us -> 49 us (level)
  transfers between devices with their start and end apart: 14 -> 14, of which waited for: 8 -> 8; matrix products, arithmetic and copies ran while one was open for 0% -> 0% of each run, Pallas kernels for 9% -> 10%
where the time goes in v4:
time: 49 us; the launch traced here: 48.8 us
  starting transfers between devices  26.1 us (53%)
  Pallas kernels  13.8 us (28%)
  waiting for transfers between devices  8.77 us (18%)
    ppermute x4, starting transfers between devices, by_heads(): lax.ppermute(unit, 'batch', cores)  9.31 us
    ppermute x4, starting transfers between devices, by_heads(): lax.ppermute(unit, both, pairs)  9.11 us
    ppermute x4, starting transfers between devices, by_heads(): lax.ppermute(out, both, [(target, source) for source, target in rounds[r]])  4.56 us
    ppermute x4, waiting for transfers between devices, by_heads(): lax.ppermute(out, both, [(target, source) for source, target in rounds[r]])  3.99 us
    ppermute x4, waiting for transfers between devices, by_heads(): lax.ppermute(unit, both, pairs)  3.92 us
    pallas_call x3, Pallas kernels, attend(): pl.pallas_call(functools.partial(kernel, head=head, count=count), out_sha...  3.9 us
    pallas_call x1, Pallas kernels, stem(): pl.pallas_call(functools.partial(first_kernel, count=lax.axis_size('seq')...  3.6 us
    pallas_call x1, Pallas kernels, stem(): pl.pallas_call(functools.partial(second_kernel, **fixed), out_shape=[shap...  2.52 us
  transfers between devices with their start and end apart: 14, of which 8 were waited for; matrix products, arithmetic and copies ran while one was open for 0% of the time, Pallas kernels for 10%

profile of v4, /device:TPU:1, one launch (start us, length us, event | category | flops | bytes accessed | tf_op | source)
XLA Modules:
  0.0 48.8 jit_solution(9478041838288710871)
XLA Ops:
  0.0 1.0 %edges.1 = (bf16[8,1536]{1,0:T(8,128)(2,1)S(1)}, bf16[8,1536]{1,0:T(8,128)(2,1)S(1)}) custom-call(bf16[256,1536]{1,0:T(8,128)(2,1)} %x_ref.1, bf16[5,1536,768]{2,1,0:T(8,128)(2,1)} %w1.1), custom_call_target="tpu_custom_call" | custom-call | tf_op jit(solution)/shard_map/edges/pallas_call | solution.py:139
  1.0 2.1 %collective-permute-start = (bf16[8,1536]{1,0:T(8,128)(2,1)S(1)}, bf16[8,1536]{1,0:T(8,128)(2,1)S(1)}, u32[]{:S(2)}, u32[]{:S(2)}) collective-permute-start(bf16[8,1536]{1,0:T(8,128)(2,1)S(1)} %get-tuple-element.25), channel_id=1, source_target_pairs={{0,4},{1,5},{2,6},{3,7},{4,0},{5,1},{6,2},{7,3},{8,12},{9,13},{10,... | collective-permute-start | bytes 73736 | tf_op jit(solution)/shard_map/ppermute | solution.py:152
  3.1 1.0 %collective-permute-start.1 = (bf16[8,1536]{1,0:T(8,128)(2,1)S(1)}, bf16[8,1536]{1,0:T(8,128)(2,1)S(1)}, u32[]{:S(2)}, u32[]{:S(2)}) collective-permute-start(bf16[8,1536]{1,0:T(8,128)(2,1)S(1)} %get-tuple-element.26), channel_id=1, source_target_pairs={{0,1},{1,0},{2,3},{3,2},{4,8},{5,9},{6,10},{7,11},{8,4},{9,5},{10,... | collective-permute-start | bytes 73736 | tf_op jit(solution)/shard_map/ppermute | solution.py:153
  4.1 0.2 collective-permute-done.pair_ref
  4.3 0.7 %collective-permute-done.1.other_ref = bf16[8,1536]{1,0:T(8,128)(2,1)S(1)} collective-permute-done((bf16[8,1536]{1,0:T(8,128)(2,1)S(1)}, bf16[8,1536]{1,0:T(8,128)(2,1)S(1)}, u32[]{:S(2)}, u32[]{:S(2)}) %collective-permute-start.1) | collective-permute-done | bytes 24608 | tf_op jit(solution)/shard_map/ppermute | solution.py:153
  5.0 3.6 %first.1.first_ref = bf16[272,768]{1,0:T(8,128)(2,1)S(1)} custom-call(bf16[256,1536]{1,0:T(8,128)(2,1)S(1)} %copy-done.2, bf16[8,1536]{1,0:T(8,128)(2,1)S(1)} %collective-permute-done.pair_ref, bf16[8,1536]{1,0:T(8,128)(2,1)S(1)} %collective-permute-done.1.other_ref, bf16[5,1536,768]{2,1,0:T(8,128)(2,1)S(1)} %copy-done), custom_call_target="tpu_custom_call" | custom-call | tf_op jit(solution)/shard_map/first/pallas_call | solution.py:154
  8.7 0.0 copy-start.3
  8.7 2.5 %second.1 = (bf16[256,768]{1,0:T(8,128)(2,1)S(1)}, bf16[256,384]{1,0:T(8,128)(2,1)S(1)}) custom-call(bf16[272,768]{1,0:T(8,128)(2,1)S(1)} %first.1.first_ref, bf16[5,768,768]{2,1,0:T(8,128)(2,1)S(1)} %bitcast.1, bf16[768,1536]{1,0:T(8,128)(2,1)S(1)} %copy-done.1, f32[4]{0:T(128)S(1)} %copy-done.4), custom_call_target="tpu_custom_call" | custom-call | tf_op jit(solution)/shard_map/second/pallas_call | solution.py:167
  11.2 7.1 %collective-permute-start.2 = (bf16[256,384]{1,0:T(8,128)(2,1)S(1)}, bf16[256,384]{1,0:T(8,128)(2,1)S(1)}, u32[]{:S(2)}, u32[]{:S(2)}) collective-permute-start(bf16[256,384]{1,0:T(8,128)(2,1)S(1)} %get-tuple-element.28), channel_id=1, source_target_pairs={{0,16},{1,24},{2,18},{3,26},{4,20},{5,28},{6,22},{7,30},{8,17},{9,... | collective-permute-start | bytes 589832 | tf_op jit(solution)/shard_map/ppermute | solution.py:322
  18.4 1.4 %third.1 = (bf16[256,384]{1,0:T(8,128)(2,1)S(1)}, bf16[256,384]{1,0:T(8,128)(2,1)S(1)}, bf16[256,384]{1,0:T(8,128)(2,1)S(1)}) custom-call(bf16[256,768]{1,0:T(8,128)(2,1)S(1)} %get-tuple-element.27.hidden_ref, bf16[768,1536]{1,0:T(8,128)(2,1)S(1)} %copy-done.1, f32[4]{0:T(128)S(1)} %copy-done.4), custom_call_target="tpu_custom_call" | custom-call | tf_op jit(solution)/shard_map/third/pallas_call | solution.py:176
  19.8 0.1 collective-permute-start.5
  19.9 0.1 collective-permute-start.6
  19.9 1.8 %collective-permute-start.3 = (bf16[256,384]{1,0:T(8,128)(2,1)S(1)}, bf16[256,384]{1,0:T(8,128)(2,1)S(1)}, u32[]{:S(2)}, u32[]{:S(2)}) collective-permute-start(bf16[256,384]{1,0:T(8,128)(2,1)S(1)} %get-tuple-element.29), channel_id=1, source_target_pairs={{0,20},{1,28},{2,22},{3,30},{4,16},{5,24},{6,18},{7,26},{8,21},{9,... | collective-permute-start | bytes 589832 | tf_op jit(solution)/shard_map/ppermute | solution.py:322
  21.8 1.3 %collective-permute-done.2.refs_0_.refs_2_ = bf16[256,384]{1,0:T(8,128)(2,1)S(1)} collective-permute-done((bf16[256,384]{1,0:T(8,128)(2,1)S(1)}, bf16[256,384]{1,0:T(8,128)(2,1)S(1)}, u32[]{:S(2)}, u32[]{:S(2)}) %collective-permute-start.2) | collective-permute-done | bytes 196640 | tf_op jit(solution)/shard_map/ppermute | solution.py:322
  23.0 4.1 %collective-permute-start.7 = (bf16[256,384]{1,0:T(8,128)(2,1)S(1)}, bf16[256,384]{1,0:T(8,128)(2,1)S(1)}, u32[]{:S(2)}, u32[]{:S(2)}) collective-permute-start(bf16[256,384]{1,0:T(8,128)(2,1)S(1)} %collective-permute-done.2.refs_0_.refs_2_), channel_id=1, source_target_pairs={{0,1},{1,0},{2,3},{3,2},{4,5},{5,4},{6,7},{7,6},{8,9},{9,8},{10,11... | collective-permute-start | bytes 589832 | tf_op jit(solution)/shard_map/ppermute | solution.py:324
  27.1 0.0 collective-permute-start.8
  27.2 2.3 %collective-permute-done.6.refs_3_.refs_1_ = bf16[256,384]{1,0:T(8,128)(2,1)S(1)} collective-permute-done((bf16[256,384]{1,0:T(8,128)(2,1)S(1)}, bf16[256,384]{1,0:T(8,128)(2,1)S(1)}, u32[]{:S(2)}, u32[]{:S(2)}) %collective-permute-start.6) | collective-permute-done | bytes 196640 | tf_op jit(solution)/shard_map/ppermute | solution.py:322
  29.4 1.8 %collective-permute-start.9 = (bf16[256,384]{1,0:T(8,128)(2,1)S(1)}, bf16[256,384]{1,0:T(8,128)(2,1)S(1)}, u32[]{:S(2)}, u32[]{:S(2)}) collective-permute-start(bf16[256,384]{1,0:T(8,128)(2,1)S(1)} %collective-permute-done.6.refs_3_.refs_1_), channel_id=1, source_target_pairs={{0,1},{1,0},{2,3},{3,2},{4,5},{5,4},{6,7},{7,6},{8,9},{9,8},{10,11... | collective-permute-start | bytes 589832 | tf_op jit(solution)/shard_map/ppermute | solution.py:324
  31.2 0.4 collective-permute-done.3.refs_1_.refs_3_
  31.6 3.4 %collective-permute-start.4 = (bf16[256,384]{1,0:T(8,128)(2,1)S(1)}, bf16[256,384]{1,0:T(8,128)(2,1)S(1)}, u32[]{:S(2)}, u32[]{:S(2)}) collective-permute-start(bf16[256,384]{1,0:T(8,128)(2,1)S(1)} %collective-permute-done.3.refs_1_.refs_3_), channel_id=1, source_target_pairs={{0,1},{1,0},{2,3},{3,2},{4,5},{5,4},{6,7},{7,6},{8,9},{9,8},{10,11... | collective-permute-start | bytes 589832 | tf_op jit(solution)/shard_map/ppermute | solution.py:324
  35.0 1.7 %most.1 = (f32[512,128]{1,0:T(8,128)S(1)}, f32[512,128]{1,0:T(8,128)S(1)}, f32[512,128]{1,0:T(8,128)S(1)}) custom-call(bf16[256,384]{1,0:T(8,128)(2,1)S(1)} %collective-permute-done.2.refs_0_.refs_2_, bf16[256,384]{1,0:T(8,128)(2,1)S(1)} %collective-permute-done.3.refs_1_.refs_3_, bf16[256,384]{1,0:T(8,128)(2,1)S(1)} %collective-permute-done.5.refs_2_.refs_0_, ...), custom_call_target="tpu_custom_call" | custom-call | tf_op jit(solution)/shard_map/most/pallas_call | solution.py:242
  36.7 0.0 collective-permute-done.4.refs_2_.refs_5_
  36.7 0.5 %last.1 = (bf16[256,128]{1,0:T(8,128)(2,1)S(1)}, bf16[256,128]{1,0:T(8,128)(2,1)S(1)}) custom-call(bf16[256,384]{1,0:T(8,128)(2,1)S(1)} %collective-permute-done.2.refs_0_.refs_2_, bf16[256,384]{1,0:T(8,128)(2,1)S(1)} %collective-permute-done.3.refs_1_.refs_3_, bf16[256,384]{1,0:T(8,128)(2,1)S(1)} %collective-permute-done.4.refs_2_.refs_5_, ...), custom_call_target="tpu_custom_call" | custom-call | tf_op jit(solution)/shard_map/last/pallas_call | solution.py:242
  37.2 1.2 %collective-permute-start.10 = (bf16[256,128]{1,0:T(8,128)(2,1)S(1)}, bf16[256,128]{1,0:T(8,128)(2,1)S(1)}, u32[]{:S(2)}, u32[]{:S(2)}) collective-permute-start(bf16[256,128]{1,0:T(8,128)(2,1)S(1)} %get-tuple-element.37), channel_id=1, source_target_pairs={{16,0},{24,1},{18,2},{26,3},{20,4},{28,5},{22,6},{30,7},{17,8},{25... | collective-permute-start | bytes 196616 | tf_op jit(solution)/shard_map/ppermute | solution.py:326
  38.4 3.2 %collective-permute-start.11 = (bf16[256,128]{1,0:T(8,128)(2,1)S(1)}, bf16[256,128]{1,0:T(8,128)(2,1)S(1)}, u32[]{:S(2)}, u32[]{:S(2)}) collective-permute-start(bf16[256,128]{1,0:T(8,128)(2,1)S(1)} %get-tuple-element.38), channel_id=1, source_target_pairs={{20,0},{28,1},{22,2},{30,3},{16,4},{24,5},{18,6},{26,7},{21,8},{29... | collective-permute-start | bytes 196616 | tf_op jit(solution)/shard_map/ppermute | solution.py:326
  41.6 1.7 %near.1 = (bf16[256,128]{1,0:T(8,128)(2,1)S(1)}, bf16[256,128]{1,0:T(8,128)(2,1)S(1)}) custom-call(bf16[256,384]{1,0:T(8,128)(2,1)S(1)} %collective-permute-done.5.refs_2_.refs_0_, bf16[256,384]{1,0:T(8,128)(2,1)S(1)} %collective-permute-done.6.refs_3_.refs_1_, bf16[256,384]{1,0:T(8,128)(2,1)S(1)} %collective-permute-done.2.refs_0_.refs_2_, ...), custom_call_target="tpu_custom_call" | custom-call | tf_op jit(solution)/shard_map/near/pallas_call | solution.py:242
  43.4 0.1 collective-permute-start.12
  43.4 0.1 collective-permute-start.13
  43.5 2.1 %collective-permute-done.11.rest_1_ = bf16[256,128]{1,0:T(8,128)(2,1)S(1)} collective-permute-done((bf16[256,128]{1,0:T(8,128)(2,1)S(1)}, bf16[256,128]{1,0:T(8,128)(2,1)S(1)}, u32[]{:S(2)}, u32[]{:S(2)}) %collective-permute-start.11) | collective-permute-done | bytes 65568 | tf_op jit(solution)/shard_map/ppermute | solution.py:326
  45.6 1.4 %collective-permute-done.12.rest_2_ = bf16[256,128]{1,0:T(8,128)(2,1)S(1)} collective-permute-done((bf16[256,128]{1,0:T(8,128)(2,1)S(1)}, bf16[256,128]{1,0:T(8,128)(2,1)S(1)}, u32[]{:S(2)}, u32[]{:S(2)}) %collective-permute-start.12) | collective-permute-done | bytes 65568 | tf_op jit(solution)/shard_map/ppermute | solution.py:326
  47.0 0.5 %collective-permute-done.13.rest_3_ = bf16[256,128]{1,0:T(8,128)(2,1)S(1)} collective-permute-done((bf16[256,128]{1,0:T(8,128)(2,1)S(1)}, bf16[256,128]{1,0:T(8,128)(2,1)S(1)}, u32[]{:S(2)}, u32[]{:S(2)}) %collective-permute-start.13) | collective-permute-done | bytes 65568 | tf_op jit(solution)/shard_map/ppermute | solution.py:326
  47.5 1.3 %finish.1 = bf16[256,768]{1,0:T(8,128)(2,1)} custom-call(bf16[256,768]{1,0:T(8,128)(2,1)S(1)} %get-tuple-element.27.hidden_ref, bf16[512,768]{1,0:T(8,128)(2,1)S(1)} %copy-done.3, bf16[256,128]{1,0:T(8,128)(2,1)S(1)} %collective-permute-done.10.rest_0_, bf16[256,128]{1,0:T(8,128)(2,1)S(1)} %collective-permute-done.11.rest_1_, ...), custom_call_target="tpu_custom_call" | custom-call | tf_op jit(solution)/shard_map/finish/pallas_call | solution.py:287
  (19 shorter events, 0.0 us)
Async XLA Ops:
  0.0 5.0 %copy-start = (bf16[5,1536,768]{2,1,0:T(8,128)(2,1)S(1)}, bf16[5,1536,768]{2,1,0:T(8,128)(2,1)}, u32[]{:S(2)}) copy-start(bf16[5,1536,768]{2,1,0:T(8,128)(2,1)} %w1.1) | copy-start | bytes 35389444
  0.0 5.0 %copy-start.2 = (bf16[256,1536]{1,0:T(8,128)(2,1)S(1)}, bf16[256,1536]{1,0:T(8,128)(2,1)}, u32[]{:S(2)}) copy-start(bf16[256,1536]{1,0:T(8,128)(2,1)} %x_ref.1) | copy-start | bytes 2359300
  1.0 3.3 %collective-permute-start = (bf16[8,1536]{1,0:T(8,128)(2,1)S(1)}, bf16[8,1536]{1,0:T(8,128)(2,1)S(1)}, u32[]{:S(2)}, u32[]{:S(2)}) collective-permute-start(bf16[8,1536]{1,0:T(8,128)(2,1)S(1)} %get-tuple-element.25), channel_id=1, source_target_pairs={{0,4},{1,5},{2,6},{3,7},{4,0},{5,1},{6,2},{7,3},{8,12},{9,13},{10,... | collective-permute-start | bytes 73736 | tf_op jit(solution)/shard_map/ppermute | solution.py:152
  3.1 5.5 %slice-start = ((s8[5898240]{0:T(1024)(128)(4,1)}), s8[4194304]{0:T(1024)(128)(4,1)S(1)}, s32[]{:S(2)}) async-start(s8[5898240]{0:T(1024)(128)(4,1)} %bitcast), calls=%async_computation | async-start | bytes 8388608
  3.1 5.5 %copy-start.1 = (bf16[768,1536]{1,0:T(8,128)(2,1)S(1)}, bf16[768,1536]{1,0:T(8,128)(2,1)}, u32[]{:S(2)}) copy-start(bf16[768,1536]{1,0:T(8,128)(2,1)} %wqkv.3) | copy-start | bytes 7077892
  3.1 5.5 %slice-start.1 = ((s8[5898240]{0:T(1024)(128)(4,1)}), s8[1703936]{0:T(1024)(128)(4,1)S(1)}, s32[]{:S(2)}) async-start(s8[5898240]{0:T(1024)(128)(4,1)} %bitcast), calls=%async_computation.1 | async-start | bytes 3407872
  3.1 5.5 %copy-start.4 = (f32[4]{0:T(128)S(1)}, f32[4]{0:T(128)}, u32[]{:S(2)}) copy-start(f32[4]{0:T(128)} %scale_hbm.3) | copy-start | bytes 52
  3.1 1.9 %collective-permute-start.1 = (bf16[8,1536]{1,0:T(8,128)(2,1)S(1)}, bf16[8,1536]{1,0:T(8,128)(2,1)S(1)}, u32[]{:S(2)}, u32[]{:S(2)}) collective-permute-start(bf16[8,1536]{1,0:T(8,128)(2,1)S(1)} %get-tuple-element.26), channel_id=1, source_target_pairs={{0,1},{1,0},{2,3},{3,2},{4,8},{5,9},{6,10},{7,11},{8,4},{9,5},{10,... | collective-permute-start | bytes 73736 | tf_op jit(solution)/shard_map/ppermute | solution.py:153
  8.7 38.9 %copy-start.3 = (bf16[512,768]{1,0:T(8,128)(2,1)S(1)}, bf16[512,768]{1,0:T(8,128)(2,1)}, u32[]{:S(2)}) copy-start(bf16[512,768]{1,0:T(8,128)(2,1)} %weight_ref.1) | copy-start | bytes 2359300
  11.2 11.8 %collective-permute-start.2 = (bf16[256,384]{1,0:T(8,128)(2,1)S(1)}, bf16[256,384]{1,0:T(8,128)(2,1)S(1)}, u32[]{:S(2)}, u32[]{:S(2)}) collective-permute-start(bf16[256,384]{1,0:T(8,128)(2,1)S(1)} %get-tuple-element.28), channel_id=1, source_target_pairs={{0,16},{1,24},{2,18},{3,26},{4,20},{5,28},{6,22},{7,30},{8,17},{9,... | collective-permute-start | bytes 589832 | tf_op jit(solution)/shard_map/ppermute | solution.py:322
  19.8 7.4 %collective-permute-start.5 = (bf16[256,384]{1,0:T(8,128)(2,1)S(1)}, bf16[256,384]{1,0:T(8,128)(2,1)S(1)}, u32[]{:S(2)}, u32[]{:S(2)}) collective-permute-start(bf16[256,384]{1,0:T(8,128)(2,1)S(1)} %get-tuple-element.30), channel_id=1, source_target_pairs={{0,1},{1,9},{2,3},{3,11},{4,5},{5,13},{6,7},{7,15},{8,0},{9,8},{10... | collective-permute-start | bytes 589832 | tf_op jit(solution)/shard_map/ppermute | solution.py:322
  19.9 9.6 %collective-permute-start.6 = (bf16[256,384]{1,0:T(8,128)(2,1)S(1)}, bf16[256,384]{1,0:T(8,128)(2,1)S(1)}, u32[]{:S(2)}, u32[]{:S(2)}) collective-permute-start(bf16[256,384]{1,0:T(8,128)(2,1)S(1)} %get-tuple-element.31), channel_id=1, source_target_pairs={{0,5},{1,13},{2,7},{3,15},{4,1},{5,9},{6,3},{7,11},{8,4},{9,12},{1... | collective-permute-start | bytes 589832 | tf_op jit(solution)/shard_map/ppermute | solution.py:322
  19.9 11.6 %collective-permute-start.3 = (bf16[256,384]{1,0:T(8,128)(2,1)S(1)}, bf16[256,384]{1,0:T(8,128)(2,1)S(1)}, u32[]{:S(2)}, u32[]{:S(2)}) collective-permute-start(bf16[256,384]{1,0:T(8,128)(2,1)S(1)} %get-tuple-element.29), channel_id=1, source_target_pairs={{0,20},{1,28},{2,22},{3,30},{4,16},{5,24},{6,18},{7,26},{8,21},{9,... | collective-permute-start | bytes 589832 | tf_op jit(solution)/shard_map/ppermute | solution.py:322
  23.0 12.0 %collective-permute-start.7 = (bf16[256,384]{1,0:T(8,128)(2,1)S(1)}, bf16[256,384]{1,0:T(8,128)(2,1)S(1)}, u32[]{:S(2)}, u32[]{:S(2)}) collective-permute-start(bf16[256,384]{1,0:T(8,128)(2,1)S(1)} %collective-permute-done.2.refs_0_.refs_2_), channel_id=1, source_target_pairs={{0,1},{1,0},{2,3},{3,2},{4,5},{5,4},{6,7},{7,6},{8,9},{9,8},{10,11... | collective-permute-start | bytes 589832 | tf_op jit(solution)/shard_map/ppermute | solution.py:324
  27.1 7.9 %collective-permute-start.8 = (bf16[256,384]{1,0:T(8,128)(2,1)S(1)}, bf16[256,384]{1,0:T(8,128)(2,1)S(1)}, u32[]{:S(2)}, u32[]{:S(2)}) collective-permute-start(bf16[256,384]{1,0:T(8,128)(2,1)S(1)} %collective-permute-done.5.refs_2_.refs_0_), channel_id=1, source_target_pairs={{0,1},{1,0},{2,3},{3,2},{4,5},{5,4},{6,7},{7,6},{8,9},{9,8},{10,11... | collective-permute-start | bytes 589832 | tf_op jit(solution)/shard_map/ppermute | solution.py:324
  29.4 5.6 %collective-permute-start.9 = (bf16[256,384]{1,0:T(8,128)(2,1)S(1)}, bf16[256,384]{1,0:T(8,128)(2,1)S(1)}, u32[]{:S(2)}, u32[]{:S(2)}) collective-permute-start(bf16[256,384]{1,0:T(8,128)(2,1)S(1)} %collective-permute-done.6.refs_3_.refs_1_), channel_id=1, source_target_pairs={{0,1},{1,0},{2,3},{3,2},{4,5},{5,4},{6,7},{7,6},{8,9},{9,8},{10,11... | collective-permute-start | bytes 589832 | tf_op jit(solution)/shard_map/ppermute | solution.py:324
  31.6 5.1 %collective-permute-start.4 = (bf16[256,384]{1,0:T(8,128)(2,1)S(1)}, bf16[256,384]{1,0:T(8,128)(2,1)S(1)}, u32[]{:S(2)}, u32[]{:S(2)}) collective-permute-start(bf16[256,384]{1,0:T(8,128)(2,1)S(1)} %collective-permute-done.3.refs_1_.refs_3_), channel_id=1, source_target_pairs={{0,1},{1,0},{2,3},{3,2},{4,5},{5,4},{6,7},{7,6},{8,9},{9,8},{10,11... | collective-permute-start | bytes 589832 | tf_op jit(solution)/shard_map/ppermute | solution.py:324
  37.2 6.3 %collective-permute-start.10 = (bf16[256,128]{1,0:T(8,128)(2,1)S(1)}, bf16[256,128]{1,0:T(8,128)(2,1)S(1)}, u32[]{:S(2)}, u32[]{:S(2)}) collective-permute-start(bf16[256,128]{1,0:T(8,128)(2,1)S(1)} %get-tuple-element.37), channel_id=1, source_target_pairs={{16,0},{24,1},{18,2},{26,3},{20,4},{28,5},{22,6},{30,7},{17,8},{25... | collective-permute-start | bytes 196616 | tf_op jit(solution)/shard_map/ppermute | solution.py:326
  38.4 7.2 %collective-permute-start.11 = (bf16[256,128]{1,0:T(8,128)(2,1)S(1)}, bf16[256,128]{1,0:T(8,128)(2,1)S(1)}, u32[]{:S(2)}, u32[]{:S(2)}) collective-permute-start(bf16[256,128]{1,0:T(8,128)(2,1)S(1)} %get-tuple-element.38), channel_id=1, source_target_pairs={{20,0},{28,1},{22,2},{30,3},{16,4},{24,5},{18,6},{26,7},{21,8},{29... | collective-permute-start | bytes 196616 | tf_op jit(solution)/shard_map/ppermute | solution.py:326
  43.4 3.6 %collective-permute-start.12 = (bf16[256,128]{1,0:T(8,128)(2,1)S(1)}, bf16[256,128]{1,0:T(8,128)(2,1)S(1)}, u32[]{:S(2)}, u32[]{:S(2)}) collective-permute-start(bf16[256,128]{1,0:T(8,128)(2,1)S(1)} %get-tuple-element.43), channel_id=1, source_target_pairs={{1,0},{9,1},{3,2},{11,3},{5,4},{13,5},{7,6},{15,7},{0,8},{8,9},{2,... | collective-permute-start | bytes 196616 | tf_op jit(solution)/shard_map/ppermute | solution.py:326
  43.4 4.1 %collective-permute-start.13 = (bf16[256,128]{1,0:T(8,128)(2,1)S(1)}, bf16[256,128]{1,0:T(8,128)(2,1)S(1)}, u32[]{:S(2)}, u32[]{:S(2)}) collective-permute-start(bf16[256,128]{1,0:T(8,128)(2,1)S(1)} %get-tuple-element.44), channel_id=1, source_target_pairs={{5,0},{13,1},{7,2},{15,3},{1,4},{9,5},{3,6},{11,7},{4,8},{12,9},{6... | collective-permute-start | bytes 196616 | tf_op jit(solution)/shard_map/ppermute | solution.py:326

commit v5 on v4

--- a/solution.py
+++ b/solution.py
@@ -42,7 +42,7 @@
     return product if shift == 0 else pltpu.roll(product, shift, 0)
 
 
-def first_kernel(x_ref, pair_ref, other_ref, w1, first_ref, x, total, *, count):
+def first_kernel(x_ref, other_ref, pair_ref, w1, first_ref, x, total, *, count):
     rows = x_ref.shape[0]
     g = lax.axis_index("seq")
     even = g % 2 == 0
@@ -149,8 +149,8 @@
         pltpu.with_memory_space_constraint(block, pltpu.HBM),
         pltpu.with_memory_space_constraint(conv_first, pltpu.HBM),
     )
+    other = lax.ppermute(to_other, ("seq", "batch"), swaps(1))
     pair = lax.ppermute(to_pair, ("seq", "batch"), swaps(0))
-    other = lax.ppermute(to_other, ("seq", "batch"), swaps(1))
     first = pl.pallas_call(
         functools.partial(first_kernel, count=lax.axis_size("seq")),
         out_shape=shape((circle, width), BF16),
@@ -159,7 +159,7 @@
         scratch_shapes=[pltpu.VMEM((circle, channels), BF16), pltpu.VMEM((circle, width), F32)],
         compiler_params=params,
         name="first",
-    )(block, pair, other, conv_first)
+    )(block, other, pair, conv_first)
     half = 1
     fixed = dict(heads=heads, head=head, spread=spread)
     unit = shape((rows, 3 * head), BF16)

time: 49 us -> 48.8 us (level)
    ppermute x4, starting transfers between devices: 9.11 us -> 7.42 us  [by_heads(): lax.ppermute(unit, both, pairs)]
    ppermute x4, starting transfers between devices: 9.31 us -> 10.7 us  [by_heads(): lax.ppermute(unit, 'batch', cores)]
    ppermute x1, starting transfers between devices: 2.11 us -> 3.32 us  [stem(): pair = lax.ppermute(to_pair, ('seq', 'batch'), swaps(0))]
    ppermute x1, waiting for transfers between devices: 0.18 us -> 1.21 us  [stem(): pair = lax.ppermute(to_pair, ('seq', 'batch'), swaps(0))]
    ppermute x1, starting transfers between devices: 1.02 us -> 0.12 us  [stem(): other = lax.ppermute(to_other, ('seq', 'batch'), swaps(1))]
    ppermute x1, waiting for transfers between devices: 0.66 us -> 0.01 us  [stem(): other = lax.ppermute(to_other, ('seq', 'batch'), swaps(1))]
  transfers between devices with their start and end apart: 14 -> 14, of which waited for: 8 -> 7; matrix products, arithmetic and copies ran while one was open for 0% -> 0% of each run, Pallas kernels for 10% -> 10%
where the time goes in v5:
time: 48.8 us; the launch traced here: 48.7 us
  starting transfers between devices  25.8 us (53%)
  Pallas kernels  13.8 us (28%)
  waiting for transfers between devices  8.95 us (18%)
    ppermute x4, starting transfers between devices, by_heads(): lax.ppermute(unit, 'batch', cores)  10.7 us
    ppermute x4, starting transfers between devices, by_heads(): lax.ppermute(unit, both, pairs)  7.42 us
    ppermute x4, starting transfers between devices, by_heads(): lax.ppermute(out, both, [(target, source) for source, target in rounds[r]])  4.19 us
    ppermute x4, waiting for transfers between devices, by_heads(): lax.ppermute(out, both, [(target, source) for source, target in rounds[r]])  4.19 us
    pallas_call x3, Pallas kernels, attend(): pl.pallas_call(functools.partial(kernel, head=head, count=count), out_sha...  3.91 us
    pallas_call x1, Pallas kernels, stem(): pl.pallas_call(functools.partial(first_kernel, count=lax.axis_size('seq')...  3.6 us
    ppermute x4, waiting for transfers between devices, by_heads(): lax.ppermute(unit, both, pairs)  3.54 us
    ppermute x1, starting transfers between devices, stem(): pair = lax.ppermute(to_pair, ('seq', 'batch'), swaps(0))  3.32 us
  transfers between devices with their start and end apart: 14, of which 7 were waited for; matrix products, arithmetic and copies ran while one was open for 0% of the time, Pallas kernels for 10%

profile of v5, /device:TPU:1, one launch (start us, length us, event | category | flops | bytes accessed | tf_op | source)
XLA Modules:
  0.0 48.7 jit_solution(15960120561720014911)
XLA Ops:
  0.0 1.0 %edges.1 = (bf16[8,1536]{1,0:T(8,128)(2,1)S(1)}, bf16[8,1536]{1,0:T(8,128)(2,1)S(1)}) custom-call(bf16[256,1536]{1,0:T(8,128)(2,1)} %x_ref.1, bf16[5,1536,768]{2,1,0:T(8,128)(2,1)} %w1.1), custom_call_target="tpu_custom_call" | custom-call | tf_op jit(solution)/shard_map/edges/pallas_call | solution.py:139
  1.0 0.1 collective-permute-start
  1.1 3.3 %collective-permute-start.1 = (bf16[8,1536]{1,0:T(8,128)(2,1)S(1)}, bf16[8,1536]{1,0:T(8,128)(2,1)S(1)}, u32[]{:S(2)}, u32[]{:S(2)}) collective-permute-start(bf16[8,1536]{1,0:T(8,128)(2,1)S(1)} %get-tuple-element.26), channel_id=1, source_target_pairs={{0,4},{1,5},{2,6},{3,7},{4,0},{5,1},{6,2},{7,3},{8,12},{9,13},{10,... | collective-permute-start | bytes 73736 | tf_op jit(solution)/shard_map/ppermute | solution.py:153
  4.5 1.2 %collective-permute-done.1.pair_ref = bf16[8,1536]{1,0:T(8,128)(2,1)S(1)} collective-permute-done((bf16[8,1536]{1,0:T(8,128)(2,1)S(1)}, bf16[8,1536]{1,0:T(8,128)(2,1)S(1)}, u32[]{:S(2)}, u32[]{:S(2)}) %collective-permute-start.1) | collective-permute-done | bytes 24608 | tf_op jit(solution)/shard_map/ppermute | solution.py:153
  5.7 3.6 %first.1.first_ref = bf16[272,768]{1,0:T(8,128)(2,1)S(1)} custom-call(bf16[256,1536]{1,0:T(8,128)(2,1)S(1)} %copy-done.2, bf16[8,1536]{1,0:T(8,128)(2,1)S(1)} %collective-permute-done.other_ref, bf16[8,1536]{1,0:T(8,128)(2,1)S(1)} %collective-permute-done.1.pair_ref, bf16[5,1536,768]{2,1,0:T(8,128)(2,1)S(1)} %copy-done), custom_call_target="tpu_custom_call" | custom-call | tf_op jit(solution)/shard_map/first/pallas_call | solution.py:154
  9.3 0.0 copy-start.3
  9.4 2.5 %second.1 = (bf16[256,768]{1,0:T(8,128)(2,1)S(1)}, bf16[256,384]{1,0:T(8,128)(2,1)S(1)}) custom-call(bf16[272,768]{1,0:T(8,128)(2,1)S(1)} %first.1.first_ref, bf16[5,768,768]{2,1,0:T(8,128)(2,1)S(1)} %bitcast.1, bf16[768,1536]{1,0:T(8,128)(2,1)S(1)} %copy-done.1, f32[4]{0:T(128)S(1)} %copy-done.4), custom_call_target="tpu_custom_call" | custom-call | tf_op jit(solution)/shard_map/second/pallas_call | solution.py:167
  11.9 5.5 %collective-permute-start.2 = (bf16[256,384]{1,0:T(8,128)(2,1)S(1)}, bf16[256,384]{1,0:T(8,128)(2,1)S(1)}, u32[]{:S(2)}, u32[]{:S(2)}) collective-permute-start(bf16[256,384]{1,0:T(8,128)(2,1)S(1)} %get-tuple-element.28), channel_id=1, source_target_pairs={{0,16},{1,24},{2,18},{3,26},{4,20},{5,28},{6,22},{7,30},{8,17},{9,... | collective-permute-start | bytes 589832 | tf_op jit(solution)/shard_map/ppermute | solution.py:322
  17.3 1.4 %third.1 = (bf16[256,384]{1,0:T(8,128)(2,1)S(1)}, bf16[256,384]{1,0:T(8,128)(2,1)S(1)}, bf16[256,384]{1,0:T(8,128)(2,1)S(1)}) custom-call(bf16[256,768]{1,0:T(8,128)(2,1)S(1)} %get-tuple-element.27.hidden_ref, bf16[768,1536]{1,0:T(8,128)(2,1)S(1)} %copy-done.1, f32[4]{0:T(128)S(1)} %copy-done.4), custom_call_target="tpu_custom_call" | custom-call | tf_op jit(solution)/shard_map/third/pallas_call | solution.py:176
  18.8 0.1 collective-permute-start.5
  18.8 0.1 collective-permute-start.6
  18.9 1.8 %collective-permute-start.3 = (bf16[256,384]{1,0:T(8,128)(2,1)S(1)}, bf16[256,384]{1,0:T(8,128)(2,1)S(1)}, u32[]{:S(2)}, u32[]{:S(2)}) collective-permute-start(bf16[256,384]{1,0:T(8,128)(2,1)S(1)} %get-tuple-element.29), channel_id=1, source_target_pairs={{0,20},{1,28},{2,22},{3,30},{4,16},{5,24},{6,18},{7,26},{8,21},{9,... | collective-permute-start | bytes 589832 | tf_op jit(solution)/shard_map/ppermute | solution.py:322
  20.8 1.3 %collective-permute-done.2.refs_0_.refs_2_ = bf16[256,384]{1,0:T(8,128)(2,1)S(1)} collective-permute-done((bf16[256,384]{1,0:T(8,128)(2,1)S(1)}, bf16[256,384]{1,0:T(8,128)(2,1)S(1)}, u32[]{:S(2)}, u32[]{:S(2)}) %collective-permute-start.2) | collective-permute-done | bytes 196640 | tf_op jit(solution)/shard_map/ppermute | solution.py:322
  22.0 4.1 %collective-permute-start.7 = (bf16[256,384]{1,0:T(8,128)(2,1)S(1)}, bf16[256,384]{1,0:T(8,128)(2,1)S(1)}, u32[]{:S(2)}, u32[]{:S(2)}) collective-permute-start(bf16[256,384]{1,0:T(8,128)(2,1)S(1)} %collective-permute-done.2.refs_0_.refs_2_), channel_id=1, source_target_pairs={{0,1},{1,0},{2,3},{3,2},{4,5},{5,4},{6,7},{7,6},{8,9},{9,8},{10,11... | collective-permute-start | bytes 589832 | tf_op jit(solution)/shard_map/ppermute | solution.py:324
  26.1 0.0 collective-permute-start.8
  26.1 2.3 %collective-permute-done.6.refs_3_.refs_1_ = bf16[256,384]{1,0:T(8,128)(2,1)S(1)} collective-permute-done((bf16[256,384]{1,0:T(8,128)(2,1)S(1)}, bf16[256,384]{1,0:T(8,128)(2,1)S(1)}, u32[]{:S(2)}, u32[]{:S(2)}) %collective-permute-start.6) | collective-permute-done | bytes 196640 | tf_op jit(solution)/shard_map/ppermute | solution.py:322
  28.4 2.9 %collective-permute-start.9 = (bf16[256,384]{1,0:T(8,128)(2,1)S(1)}, bf16[256,384]{1,0:T(8,128)(2,1)S(1)}, u32[]{:S(2)}, u32[]{:S(2)}) collective-permute-start(bf16[256,384]{1,0:T(8,128)(2,1)S(1)} %collective-permute-done.6.refs_3_.refs_1_), channel_id=1, source_target_pairs={{0,1},{1,0},{2,3},{3,2},{4,5},{5,4},{6,7},{7,6},{8,9},{9,8},{10,11... | collective-permute-start | bytes 589832 | tf_op jit(solution)/shard_map/ppermute | solution.py:324
  31.3 0.0 collective-permute-done.3.refs_1_.refs_3_
  31.3 3.7 %collective-permute-start.4 = (bf16[256,384]{1,0:T(8,128)(2,1)S(1)}, bf16[256,384]{1,0:T(8,128)(2,1)S(1)}, u32[]{:S(2)}, u32[]{:S(2)}) collective-permute-start(bf16[256,384]{1,0:T(8,128)(2,1)S(1)} %collective-permute-done.3.refs_1_.refs_3_), channel_id=1, source_target_pairs={{0,1},{1,0},{2,3},{3,2},{4,5},{5,4},{6,7},{7,6},{8,9},{9,8},{10,11... | collective-permute-start | bytes 589832 | tf_op jit(solution)/shard_map/ppermute | solution.py:324
  35.0 0.0 collective-permute-done.7.refs_4_
  35.0 1.7 %most.1 = (f32[512,128]{1,0:T(8,128)S(1)}, f32[512,128]{1,0:T(8,128)S(1)}, f32[512,128]{1,0:T(8,128)S(1)}) custom-call(bf16[256,384]{1,0:T(8,128)(2,1)S(1)} %collective-permute-done.2.refs_0_.refs_2_, bf16[256,384]{1,0:T(8,128)(2,1)S(1)} %collective-permute-done.3.refs_1_.refs_3_, bf16[256,384]{1,0:T(8,128)(2,1)S(1)} %collective-permute-done.5.refs_2_.refs_0_, ...), custom_call_target="tpu_custom_call" | custom-call | tf_op jit(solution)/shard_map/most/pallas_call | solution.py:242
  36.7 0.5 %last.1 = (bf16[256,128]{1,0:T(8,128)(2,1)S(1)}, bf16[256,128]{1,0:T(8,128)(2,1)S(1)}) custom-call(bf16[256,384]{1,0:T(8,128)(2,1)S(1)} %collective-permute-done.2.refs_0_.refs_2_, bf16[256,384]{1,0:T(8,128)(2,1)S(1)} %collective-permute-done.3.refs_1_.refs_3_, bf16[256,384]{1,0:T(8,128)(2,1)S(1)} %collective-permute-done.4.refs_2_.refs_5_, ...), custom_call_target="tpu_custom_call" | custom-call | tf_op jit(solution)/shard_map/last/pallas_call | solution.py:242
  37.2 1.1 %collective-permute-start.10 = (bf16[256,128]{1,0:T(8,128)(2,1)S(1)}, bf16[256,128]{1,0:T(8,128)(2,1)S(1)}, u32[]{:S(2)}, u32[]{:S(2)}) collective-permute-start(bf16[256,128]{1,0:T(8,128)(2,1)S(1)} %get-tuple-element.37), channel_id=1, source_target_pairs={{16,0},{24,1},{18,2},{26,3},{20,4},{28,5},{22,6},{30,7},{17,8},{25... | collective-permute-start | bytes 196616 | tf_op jit(solution)/shard_map/ppermute | solution.py:326
  38.3 2.3 %collective-permute-start.11 = (bf16[256,128]{1,0:T(8,128)(2,1)S(1)}, bf16[256,128]{1,0:T(8,128)(2,1)S(1)}, u32[]{:S(2)}, u32[]{:S(2)}) collective-permute-start(bf16[256,128]{1,0:T(8,128)(2,1)S(1)} %get-tuple-element.38), channel_id=1, source_target_pairs={{20,0},{28,1},{22,2},{30,3},{16,4},{24,5},{18,6},{26,7},{21,8},{29... | collective-permute-start | bytes 196616 | tf_op jit(solution)/shard_map/ppermute | solution.py:326
  40.6 1.7 %near.1 = (bf16[256,128]{1,0:T(8,128)(2,1)S(1)}, bf16[256,128]{1,0:T(8,128)(2,1)S(1)}) custom-call(bf16[256,384]{1,0:T(8,128)(2,1)S(1)} %collective-permute-done.5.refs_2_.refs_0_, bf16[256,384]{1,0:T(8,128)(2,1)S(1)} %collective-permute-done.6.refs_3_.refs_1_, bf16[256,384]{1,0:T(8,128)(2,1)S(1)} %collective-permute-done.2.refs_0_.refs_2_, ...), custom_call_target="tpu_custom_call" | custom-call | tf_op jit(solution)/shard_map/near/pallas_call | solution.py:242
  42.3 0.1 collective-permute-start.12
  42.4 0.7 %collective-permute-start.13 = (bf16[256,128]{1,0:T(8,128)(2,1)S(1)}, bf16[256,128]{1,0:T(8,128)(2,1)S(1)}, u32[]{:S(2)}, u32[]{:S(2)}) collective-permute-start(bf16[256,128]{1,0:T(8,128)(2,1)S(1)} %get-tuple-element.44), channel_id=1, source_target_pairs={{5,0},{13,1},{7,2},{15,3},{1,4},{9,5},{3,6},{11,7},{4,8},{12,9},{6... | collective-permute-start | bytes 196616 | tf_op jit(solution)/shard_map/ppermute | solution.py:326
  43.2 0.3 collective-permute-done.10.rest_0_
  43.5 1.8 %collective-permute-done.11.rest_1_ = bf16[256,128]{1,0:T(8,128)(2,1)S(1)} collective-permute-done((bf16[256,128]{1,0:T(8,128)(2,1)S(1)}, bf16[256,128]{1,0:T(8,128)(2,1)S(1)}, u32[]{:S(2)}, u32[]{:S(2)}) %collective-permute-start.11) | collective-permute-done | bytes 65568 | tf_op jit(solution)/shard_map/ppermute | solution.py:326
  45.3 1.0 %collective-permute-done.12.rest_2_ = bf16[256,128]{1,0:T(8,128)(2,1)S(1)} collective-permute-done((bf16[256,128]{1,0:T(8,128)(2,1)S(1)}, bf16[256,128]{1,0:T(8,128)(2,1)S(1)}, u32[]{:S(2)}, u32[]{:S(2)}) %collective-permute-start.12) | collective-permute-done | bytes 65568 | tf_op jit(solution)/shard_map/ppermute | solution.py:326
  46.3 1.1 %collective-permute-done.13.rest_3_ = bf16[256,128]{1,0:T(8,128)(2,1)S(1)} collective-permute-done((bf16[256,128]{1,0:T(8,128)(2,1)S(1)}, bf16[256,128]{1,0:T(8,128)(2,1)S(1)}, u32[]{:S(2)}, u32[]{:S(2)}) %collective-permute-start.13) | collective-permute-done | bytes 65568 | tf_op jit(solution)/shard_map/ppermute | solution.py:326
  47.3 1.3 %finish.1 = bf16[256,768]{1,0:T(8,128)(2,1)} custom-call(bf16[256,768]{1,0:T(8,128)(2,1)S(1)} %get-tuple-element.27.hidden_ref, bf16[512,768]{1,0:T(8,128)(2,1)S(1)} %copy-done.3, bf16[256,128]{1,0:T(8,128)(2,1)S(1)} %collective-permute-done.10.rest_0_, bf16[256,128]{1,0:T(8,128)(2,1)S(1)} %collective-permute-done.11.rest_1_, ...), custom_call_target="tpu_custom_call" | custom-call | tf_op jit(solution)/shard_map/finish/pallas_call | solution.py:287
  (19 shorter events, 0.0 us)
Async XLA Ops:
  0.0 5.7 %copy-start = (bf16[5,1536,768]{2,1,0:T(8,128)(2,1)S(1)}, bf16[5,1536,768]{2,1,0:T(8,128)(2,1)}, u32[]{:S(2)}) copy-start(bf16[5,1536,768]{2,1,0:T(8,128)(2,1)} %w1.1) | copy-start | bytes 35389444
  0.0 5.7 %copy-start.2 = (bf16[256,1536]{1,0:T(8,128)(2,1)S(1)}, bf16[256,1536]{1,0:T(8,128)(2,1)}, u32[]{:S(2)}) copy-start(bf16[256,1536]{1,0:T(8,128)(2,1)} %x_ref.1) | copy-start | bytes 2359300
  1.0 3.5 %collective-permute-start = (bf16[8,1536]{1,0:T(8,128)(2,1)S(1)}, bf16[8,1536]{1,0:T(8,128)(2,1)S(1)}, u32[]{:S(2)}, u32[]{:S(2)}) collective-permute-start(bf16[8,1536]{1,0:T(8,128)(2,1)S(1)} %get-tuple-element.25), channel_id=1, source_target_pairs={{0,1},{1,0},{2,3},{3,2},{4,8},{5,9},{6,10},{7,11},{8,4},{9,5},{10,... | collective-permute-start | bytes 73736 | tf_op jit(solution)/shard_map/ppermute | solution.py:152
  1.1 8.2 %slice-start = ((s8[5898240]{0:T(1024)(128)(4,1)}), s8[4194304]{0:T(1024)(128)(4,1)S(1)}, s32[]{:S(2)}) async-start(s8[5898240]{0:T(1024)(128)(4,1)} %bitcast), calls=%async_computation | async-start | bytes 8388608
  1.1 8.2 %copy-start.1 = (bf16[768,1536]{1,0:T(8,128)(2,1)S(1)}, bf16[768,1536]{1,0:T(8,128)(2,1)}, u32[]{:S(2)}) copy-start(bf16[768,1536]{1,0:T(8,128)(2,1)} %wqkv.3) | copy-start | bytes 7077892
  1.1 8.2 %slice-start.1 = ((s8[5898240]{0:T(1024)(128)(4,1)}), s8[1703936]{0:T(1024)(128)(4,1)S(1)}, s32[]{:S(2)}) async-start(s8[5898240]{0:T(1024)(128)(4,1)} %bitcast), calls=%async_computation.1 | async-start | bytes 3407872
  1.1 8.2 %copy-start.4 = (f32[4]{0:T(128)S(1)}, f32[4]{0:T(128)}, u32[]{:S(2)}) copy-start(f32[4]{0:T(128)} %scale_hbm.3) | copy-start | bytes 52
  1.1 4.5 %collective-permute-start.1 = (bf16[8,1536]{1,0:T(8,128)(2,1)S(1)}, bf16[8,1536]{1,0:T(8,128)(2,1)S(1)}, u32[]{:S(2)}, u32[]{:S(2)}) collective-permute-start(bf16[8,1536]{1,0:T(8,128)(2,1)S(1)} %get-tuple-element.26), channel_id=1, source_target_pairs={{0,4},{1,5},{2,6},{3,7},{4,0},{5,1},{6,2},{7,3},{8,12},{9,13},{10,... | collective-permute-start | bytes 73736 | tf_op jit(solution)/shard_map/ppermute | solution.py:153
  9.3 38.0 %copy-start.3 = (bf16[512,768]{1,0:T(8,128)(2,1)S(1)}, bf16[512,768]{1,0:T(8,128)(2,1)}, u32[]{:S(2)}) copy-start(bf16[512,768]{1,0:T(8,128)(2,1)} %weight_ref.1) | copy-start | bytes 2359300
  11.9 10.1 %collective-permute-start.2 = (bf16[256,384]{1,0:T(8,128)(2,1)S(1)}, bf16[256,384]{1,0:T(8,128)(2,1)S(1)}, u32[]{:S(2)}, u32[]{:S(2)}) collective-permute-start(bf16[256,384]{1,0:T(8,128)(2,1)S(1)} %get-tuple-element.28), channel_id=1, source_target_pairs={{0,16},{1,24},{2,18},{3,26},{4,20},{5,28},{6,22},{7,30},{8,17},{9,... | collective-permute-start | bytes 589832 | tf_op jit(solution)/shard_map/ppermute | solution.py:322
  18.8 7.4 %collective-permute-start.5 = (bf16[256,384]{1,0:T(8,128)(2,1)S(1)}, bf16[256,384]{1,0:T(8,128)(2,1)S(1)}, u32[]{:S(2)}, u32[]{:S(2)}) collective-permute-start(bf16[256,384]{1,0:T(8,128)(2,1)S(1)} %get-tuple-element.30), channel_id=1, source_target_pairs={{0,1},{1,9},{2,3},{3,11},{4,5},{5,13},{6,7},{7,15},{8,0},{9,8},{10... | collective-permute-start | bytes 589832 | tf_op jit(solution)/shard_map/ppermute | solution.py:322
  18.8 9.6 %collective-permute-start.6 = (bf16[256,384]{1,0:T(8,128)(2,1)S(1)}, bf16[256,384]{1,0:T(8,128)(2,1)S(1)}, u32[]{:S(2)}, u32[]{:S(2)}) collective-permute-start(bf16[256,384]{1,0:T(8,128)(2,1)S(1)} %get-tuple-element.31), channel_id=1, source_target_pairs={{0,5},{1,13},{2,7},{3,15},{4,1},{5,9},{6,3},{7,11},{8,4},{9,12},{1... | collective-permute-start | bytes 589832 | tf_op jit(solution)/shard_map/ppermute | solution.py:322
  18.9 12.4 %collective-permute-start.3 = (bf16[256,384]{1,0:T(8,128)(2,1)S(1)}, bf16[256,384]{1,0:T(8,128)(2,1)S(1)}, u32[]{:S(2)}, u32[]{:S(2)}) collective-permute-start(bf16[256,384]{1,0:T(8,128)(2,1)S(1)} %get-tuple-element.29), channel_id=1, source_target_pairs={{0,20},{1,28},{2,22},{3,30},{4,16},{5,24},{6,18},{7,26},{8,21},{9,... | collective-permute-start | bytes 589832 | tf_op jit(solution)/shard_map/ppermute | solution.py:322
  22.0 13.0 %collective-permute-start.7 = (bf16[256,384]{1,0:T(8,128)(2,1)S(1)}, bf16[256,384]{1,0:T(8,128)(2,1)S(1)}, u32[]{:S(2)}, u32[]{:S(2)}) collective-permute-start(bf16[256,384]{1,0:T(8,128)(2,1)S(1)} %collective-permute-done.2.refs_0_.refs_2_), channel_id=1, source_target_pairs={{0,1},{1,0},{2,3},{3,2},{4,5},{5,4},{6,7},{7,6},{8,9},{9,8},{10,11... | collective-permute-start | bytes 589832 | tf_op jit(solution)/shard_map/ppermute | solution.py:324
  26.1 8.9 %collective-permute-start.8 = (bf16[256,384]{1,0:T(8,128)(2,1)S(1)}, bf16[256,384]{1,0:T(8,128)(2,1)S(1)}, u32[]{:S(2)}, u32[]{:S(2)}) collective-permute-start(bf16[256,384]{1,0:T(8,128)(2,1)S(1)} %collective-permute-done.5.refs_2_.refs_0_), channel_id=1, source_target_pairs={{0,1},{1,0},{2,3},{3,2},{4,5},{5,4},{6,7},{7,6},{8,9},{9,8},{10,11... | collective-permute-start | bytes 589832 | tf_op jit(solution)/shard_map/ppermute | solution.py:324
  28.4 6.6 %collective-permute-start.9 = (bf16[256,384]{1,0:T(8,128)(2,1)S(1)}, bf16[256,384]{1,0:T(8,128)(2,1)S(1)}, u32[]{:S(2)}, u32[]{:S(2)}) collective-permute-start(bf16[256,384]{1,0:T(8,128)(2,1)S(1)} %collective-permute-done.6.refs_3_.refs_1_), channel_id=1, source_target_pairs={{0,1},{1,0},{2,3},{3,2},{4,5},{5,4},{6,7},{7,6},{8,9},{9,8},{10,11... | collective-permute-start | bytes 589832 | tf_op jit(solution)/shard_map/ppermute | solution.py:324
  31.3 5.4 %collective-permute-start.4 = (bf16[256,384]{1,0:T(8,128)(2,1)S(1)}, bf16[256,384]{1,0:T(8,128)(2,1)S(1)}, u32[]{:S(2)}, u32[]{:S(2)}) collective-permute-start(bf16[256,384]{1,0:T(8,128)(2,1)S(1)} %collective-permute-done.3.refs_1_.refs_3_), channel_id=1, source_target_pairs={{0,1},{1,0},{2,3},{3,2},{4,5},{5,4},{6,7},{7,6},{8,9},{9,8},{10,11... | collective-permute-start | bytes 589832 | tf_op jit(solution)/shard_map/ppermute | solution.py:324
  37.2 6.3 %collective-permute-start.10 = (bf16[256,128]{1,0:T(8,128)(2,1)S(1)}, bf16[256,128]{1,0:T(8,128)(2,1)S(1)}, u32[]{:S(2)}, u32[]{:S(2)}) collective-permute-start(bf16[256,128]{1,0:T(8,128)(2,1)S(1)} %get-tuple-element.37), channel_id=1, source_target_pairs={{16,0},{24,1},{18,2},{26,3},{20,4},{28,5},{22,6},{30,7},{17,8},{25... | collective-permute-start | bytes 196616 | tf_op jit(solution)/shard_map/ppermute | solution.py:326
  38.3 7.0 %collective-permute-start.11 = (bf16[256,128]{1,0:T(8,128)(2,1)S(1)}, bf16[256,128]{1,0:T(8,128)(2,1)S(1)}, u32[]{:S(2)}, u32[]{:S(2)}) collective-permute-start(bf16[256,128]{1,0:T(8,128)(2,1)S(1)} %get-tuple-element.38), channel_id=1, source_target_pairs={{20,0},{28,1},{22,2},{30,3},{16,4},{24,5},{18,6},{26,7},{21,8},{29... | collective-permute-start | bytes 196616 | tf_op jit(solution)/shard_map/ppermute | solution.py:326
  42.3 3.9 %collective-permute-start.12 = (bf16[256,128]{1,0:T(8,128)(2,1)S(1)}, bf16[256,128]{1,0:T(8,128)(2,1)S(1)}, u32[]{:S(2)}, u32[]{:S(2)}) collective-permute-start(bf16[256,128]{1,0:T(8,128)(2,1)S(1)} %get-tuple-element.43), channel_id=1, source_target_pairs={{1,0},{9,1},{3,2},{11,3},{5,4},{13,5},{7,6},{15,7},{0,8},{8,9},{2,... | collective-permute-start | bytes 196616 | tf_op jit(solution)/shard_map/ppermute | solution.py:326
  42.4 4.9 %collective-permute-start.13 = (bf16[256,128]{1,0:T(8,128)(2,1)S(1)}, bf16[256,128]{1,0:T(8,128)(2,1)S(1)}, u32[]{:S(2)}, u32[]{:S(2)}) collective-permute-start(bf16[256,128]{1,0:T(8,128)(2,1)S(1)} %get-tuple-element.44), channel_id=1, source_target_pairs={{5,0},{13,1},{7,2},{15,3},{1,4},{9,5},{3,6},{11,7},{4,8},{12,9},{6... | collective-permute-start | bytes 196616 | tf_op jit(solution)/shard_map/ppermute | solution.py:326

commit v6 on v5

--- a/solution.py
+++ b/solution.py
@@ -11,6 +11,7 @@
 F32 = jnp.float32
 BF16 = jnp.bfloat16
 EDGE = 8
+REACH = 4
 TILE = 16
 TAPS = 5
 MIB = 1 << 20
@@ -31,10 +32,19 @@
     for copy in copies:
         copy.wait()
     even = lax.axis_index("seq") % 2 == 0
-    begin = first[...].astype(F32)[:EDGE]
-    end = last[...].astype(F32)[TILE - EDGE :]
+    begin = folded(first[...].astype(F32)[:REACH])
+    end = folded(last[...].astype(F32)[TILE - REACH :])
     to_pair[...] = jnp.where(even, end, begin).astype(BF16)
     to_other[...] = jnp.where(even, begin, end).astype(BF16)
+
+
+def folded(rows):
+    half = rows.shape[1] // 2
+    return jnp.concatenate([rows[:, :half], rows[:, half:]], axis=0)
+
+
+def unfolded(rows):
+    return jnp.concatenate([rows[:REACH], rows[REACH:]], axis=1)
 
 
 def rolled(product, j):
@@ -49,10 +59,11 @@
     has_before = (g > 0).astype(F32)
     has_after = (g < count - 1).astype(F32)
     pair, other = pair_ref[...].astype(F32), other_ref[...].astype(F32)
-    after = jnp.where(even, pair, other) * has_after
-    before = jnp.where(even, other, pair) * has_before
+    rest = jnp.zeros((EDGE - REACH, x.shape[1]), F32)
+    after = unfolded(jnp.where(even, pair, other)) * has_after
+    before = unfolded(jnp.where(even, other, pair)) * has_before
     x[0:rows] = x_ref[...]
-    x[rows:] = jnp.concatenate([after, before], axis=0).astype(BF16)
+    x[rows:] = jnp.concatenate([after, rest, rest, before], axis=0).astype(BF16)
     for j in range(TAPS):
         product = rolled(jnp.dot(x[...], w1[j], preferred_element_type=F32), j)
         if j == 0:
@@ -135,7 +146,7 @@
     hbm = pl.BlockSpec(memory_space=pltpu.HBM)
     shape = jax.ShapeDtypeStruct
     params = pltpu.CompilerParams(vmem_limit_bytes=24 * MIB)
-    edge = shape((EDGE, channels), BF16)
+    edge = shape((EDGE, channels // 2), BF16)
     to_pair, to_other = pl.pallas_call(
         edges_kernel,
         out_shape=[edge, edge],
@@ -272,14 +283,11 @@
     mixed, out_ref = rest[:-1], rest[-1]
     g = lax.axis_index("seq")
     head = mixed[0].shape[1]
-    total = hidden_ref[...].astype(F32)
-    for r, part in zip(rounds, mixed):
-        h = head_of(r, g, len(mixed)) if spread else r
-        at = pl.multiple_of(h * head, head)
-        total += jnp.dot(
-            part[...], weight_ref[pl.ds(at, head), :], preferred_element_type=F32
-        )
-    out_ref[...] = total.astype(out_ref.dtype)
+    heads = [head_of(r, g, len(mixed)) if spread else r for r in rounds]
+    rows = [weight_ref[pl.ds(pl.multiple_of(h * head, head), head), :] for h in heads]
+    attended = jnp.concatenate([part[...] for part in mixed], axis=1)
+    projected = jnp.dot(attended, jnp.concatenate(rows, axis=0), preferred_element_type=F32)
+    out_ref[...] = (hidden_ref[...].astype(F32) + projected).astype(out_ref.dtype)
 
 
 def finish(hidden, out_weight, mixed, rounds, spread):

time: 48.8 us -> 48.4 us (level)
  no operation moved by 1% of the time
where the time goes in v6:
time: 48.4 us; the launch traced here: 48.3 us
  starting transfers between devices  25.8 us (53%)
  Pallas kernels  13.5 us (28%)
  waiting for transfers between devices  8.82 us (18%)
    ppermute x4, starting transfers between devices, by_heads(): lax.ppermute(unit, 'batch', cores)  10.7 us
    ppermute x4, starting transfers between devices, by_heads(): lax.ppermute(unit, both, pairs)  7.42 us
    ppermute x4, starting transfers between devices, by_heads(): lax.ppermute(out, both, [(target, source) for source, target in rounds[r]])  4.19 us
    ppermute x4, waiting for transfers between devices, by_heads(): lax.ppermute(out, both, [(target, source) for source, target in rounds[r]])  4.19 us
    pallas_call x3, Pallas kernels, attend(): pl.pallas_call(functools.partial(kernel, head=head, count=count), out_sha...  3.91 us
    pallas_call x1, Pallas kernels, stem(): pl.pallas_call(functools.partial(first_kernel, count=lax.axis_size('seq')...  3.6 us
    ppermute x4, waiting for transfers between devices, by_heads(): lax.ppermute(unit, both, pairs)  3.54 us
    ppermute x1, starting transfers between devices, stem(): pair = lax.ppermute(to_pair, ('seq', 'batch'), swaps(0))  3.32 us
  transfers between devices with their start and end apart: 14, of which 7 were waited for; matrix products, arithmetic and copies ran while one was open for 0% of the time, Pallas kernels for 10%

profile of v6, /device:TPU:1, one launch (start us, length us, event | category | flops | bytes accessed | tf_op | source)
XLA Modules:
  0.0 48.3 jit_solution(9995440699582430274)
XLA Ops:
  0.0 1.0 %edges.1 = (bf16[8,768]{1,0:T(8,128)(2,1)S(1)}, bf16[8,768]{1,0:T(8,128)(2,1)S(1)}) custom-call(bf16[256,1536]{1,0:T(8,128)(2,1)} %x_ref.1, bf16[5,1536,768]{2,1,0:T(8,128)(2,1)} %w1.1), custom_call_target="tpu_custom_call" | custom-call | tf_op jit(solution)/shard_map/edges/pallas_call | solution.py:150
  1.0 0.1 collective-permute-start
  1.1 3.3 %collective-permute-start.1 = (bf16[8,768]{1,0:T(8,128)(2,1)S(1)}, bf16[8,768]{1,0:T(8,128)(2,1)S(1)}, u32[]{:S(2)}, u32[]{:S(2)}) collective-permute-start(bf16[8,768]{1,0:T(8,128)(2,1)S(1)} %get-tuple-element.26), channel_id=1, source_target_pairs={{0,4},{1,5},{2,6},{3,7},{4,0},{5,1},{6,2},{7,3},{8,12},{9,13},{10,... | collective-permute-start | bytes 36872 | tf_op jit(solution)/shard_map/ppermute | solution.py:164
  4.5 0.0 collective-permute-done.other_ref
  4.5 1.1 %collective-permute-done.1.pair_ref = bf16[8,768]{1,0:T(8,128)(2,1)S(1)} collective-permute-done((bf16[8,768]{1,0:T(8,128)(2,1)S(1)}, bf16[8,768]{1,0:T(8,128)(2,1)S(1)}, u32[]{:S(2)}, u32[]{:S(2)}) %collective-permute-start.1) | collective-permute-done | bytes 12320 | tf_op jit(solution)/shard_map/ppermute | solution.py:164
  5.6 3.6 %first.1.first_ref = bf16[272,768]{1,0:T(8,128)(2,1)S(1)} custom-call(bf16[256,1536]{1,0:T(8,128)(2,1)S(1)} %copy-done.2, bf16[8,768]{1,0:T(8,128)(2,1)S(1)} %collective-permute-done.other_ref, bf16[8,768]{1,0:T(8,128)(2,1)S(1)} %collective-permute-done.1.pair_ref, bf16[5,1536,768]{2,1,0:T(8,128)(2,1)S(1)} %copy-done), custom_call_target="tpu_custom_call" | custom-call | tf_op jit(solution)/shard_map/first/pallas_call | solution.py:165
  9.2 0.0 copy-start.3
  9.2 2.5 %second.1 = (bf16[256,768]{1,0:T(8,128)(2,1)S(1)}, bf16[256,384]{1,0:T(8,128)(2,1)S(1)}) custom-call(bf16[272,768]{1,0:T(8,128)(2,1)S(1)} %first.1.first_ref, bf16[5,768,768]{2,1,0:T(8,128)(2,1)S(1)} %bitcast.1, bf16[768,1536]{1,0:T(8,128)(2,1)S(1)} %copy-done.1, f32[4]{0:T(128)S(1)} %copy-done.4), custom_call_target="tpu_custom_call" | custom-call | tf_op jit(solution)/shard_map/second/pallas_call | solution.py:178
  11.7 5.5 %collective-permute-start.2 = (bf16[256,384]{1,0:T(8,128)(2,1)S(1)}, bf16[256,384]{1,0:T(8,128)(2,1)S(1)}, u32[]{:S(2)}, u32[]{:S(2)}) collective-permute-start(bf16[256,384]{1,0:T(8,128)(2,1)S(1)} %get-tuple-element.28), channel_id=1, source_target_pairs={{0,16},{1,24},{2,18},{3,26},{4,20},{5,28},{6,22},{7,30},{8,17},{9,... | collective-permute-start | bytes 589832 | tf_op jit(solution)/shard_map/ppermute | solution.py:330
  17.2 1.4 %third.1 = (bf16[256,384]{1,0:T(8,128)(2,1)S(1)}, bf16[256,384]{1,0:T(8,128)(2,1)S(1)}, bf16[256,384]{1,0:T(8,128)(2,1)S(1)}) custom-call(bf16[256,768]{1,0:T(8,128)(2,1)S(1)} %get-tuple-element.27.hidden_ref, bf16[768,1536]{1,0:T(8,128)(2,1)S(1)} %copy-done.1, f32[4]{0:T(128)S(1)} %copy-done.4), custom_call_target="tpu_custom_call" | custom-call | tf_op jit(solution)/shard_map/third/pallas_call | solution.py:187
  18.6 0.1 collective-permute-start.5
  18.7 0.1 collective-permute-start.6
  18.8 1.8 %collective-permute-start.3 = (bf16[256,384]{1,0:T(8,128)(2,1)S(1)}, bf16[256,384]{1,0:T(8,128)(2,1)S(1)}, u32[]{:S(2)}, u32[]{:S(2)}) collective-permute-start(bf16[256,384]{1,0:T(8,128)(2,1)S(1)} %get-tuple-element.29), channel_id=1, source_target_pairs={{0,20},{1,28},{2,22},{3,30},{4,16},{5,24},{6,18},{7,26},{8,21},{9,... | collective-permute-start | bytes 589832 | tf_op jit(solution)/shard_map/ppermute | solution.py:330
  20.6 1.3 %collective-permute-done.2.refs_0_.refs_2_ = bf16[256,384]{1,0:T(8,128)(2,1)S(1)} collective-permute-done((bf16[256,384]{1,0:T(8,128)(2,1)S(1)}, bf16[256,384]{1,0:T(8,128)(2,1)S(1)}, u32[]{:S(2)}, u32[]{:S(2)}) %collective-permute-start.2) | collective-permute-done | bytes 196640 | tf_op jit(solution)/shard_map/ppermute | solution.py:330
  21.9 4.1 %collective-permute-start.7 = (bf16[256,384]{1,0:T(8,128)(2,1)S(1)}, bf16[256,384]{1,0:T(8,128)(2,1)S(1)}, u32[]{:S(2)}, u32[]{:S(2)}) collective-permute-start(bf16[256,384]{1,0:T(8,128)(2,1)S(1)} %collective-permute-done.2.refs_0_.refs_2_), channel_id=1, source_target_pairs={{0,1},{1,0},{2,3},{3,2},{4,5},{5,4},{6,7},{7,6},{8,9},{9,8},{10,11... | collective-permute-start | bytes 589832 | tf_op jit(solution)/shard_map/ppermute | solution.py:332
  26.0 0.0 collective-permute-start.8
  26.0 2.3 %collective-permute-done.6.refs_3_.refs_1_ = bf16[256,384]{1,0:T(8,128)(2,1)S(1)} collective-permute-done((bf16[256,384]{1,0:T(8,128)(2,1)S(1)}, bf16[256,384]{1,0:T(8,128)(2,1)S(1)}, u32[]{:S(2)}, u32[]{:S(2)}) %collective-permute-start.6) | collective-permute-done | bytes 196640 | tf_op jit(solution)/shard_map/ppermute | solution.py:330
  28.2 2.9 %collective-permute-start.9 = (bf16[256,384]{1,0:T(8,128)(2,1)S(1)}, bf16[256,384]{1,0:T(8,128)(2,1)S(1)}, u32[]{:S(2)}, u32[]{:S(2)}) collective-permute-start(bf16[256,384]{1,0:T(8,128)(2,1)S(1)} %collective-permute-done.6.refs_3_.refs_1_), channel_id=1, source_target_pairs={{0,1},{1,0},{2,3},{3,2},{4,5},{5,4},{6,7},{7,6},{8,9},{9,8},{10,11... | collective-permute-start | bytes 589832 | tf_op jit(solution)/shard_map/ppermute | solution.py:332
  31.1 0.0 collective-permute-done.3.refs_1_.refs_3_
  31.1 3.7 %collective-permute-start.4 = (bf16[256,384]{1,0:T(8,128)(2,1)S(1)}, bf16[256,384]{1,0:T(8,128)(2,1)S(1)}, u32[]{:S(2)}, u32[]{:S(2)}) collective-permute-start(bf16[256,384]{1,0:T(8,128)(2,1)S(1)} %collective-permute-done.3.refs_1_.refs_3_), channel_id=1, source_target_pairs={{0,1},{1,0},{2,3},{3,2},{4,5},{5,4},{6,7},{7,6},{8,9},{9,8},{10,11... | collective-permute-start | bytes 589832 | tf_op jit(solution)/shard_map/ppermute | solution.py:332
  34.8 1.7 %most.1 = (f32[512,128]{1,0:T(8,128)S(1)}, f32[512,128]{1,0:T(8,128)S(1)}, f32[512,128]{1,0:T(8,128)S(1)}) custom-call(bf16[256,384]{1,0:T(8,128)(2,1)S(1)} %collective-permute-done.2.refs_0_.refs_2_, bf16[256,384]{1,0:T(8,128)(2,1)S(1)} %collective-permute-done.3.refs_1_.refs_3_, bf16[256,384]{1,0:T(8,128)(2,1)S(1)} %collective-permute-done.5.refs_2_.refs_0_, ...), custom_call_target="tpu_custom_call" | custom-call | tf_op jit(solution)/shard_map/most/pallas_call | solution.py:253
  36.5 0.5 %last.1 = (bf16[256,128]{1,0:T(8,128)(2,1)S(1)}, bf16[256,128]{1,0:T(8,128)(2,1)S(1)}) custom-call(bf16[256,384]{1,0:T(8,128)(2,1)S(1)} %collective-permute-done.2.refs_0_.refs_2_, bf16[256,384]{1,0:T(8,128)(2,1)S(1)} %collective-permute-done.3.refs_1_.refs_3_, bf16[256,384]{1,0:T(8,128)(2,1)S(1)} %collective-permute-done.4.refs_2_.refs_5_, ...), custom_call_target="tpu_custom_call" | custom-call | tf_op jit(solution)/shard_map/last/pallas_call | solution.py:253
  37.0 1.3 %collective-permute-start.10 = (bf16[256,128]{1,0:T(8,128)(2,1)S(1)}, bf16[256,128]{1,0:T(8,128)(2,1)S(1)}, u32[]{:S(2)}, u32[]{:S(2)}) collective-permute-start(bf16[256,128]{1,0:T(8,128)(2,1)S(1)} %get-tuple-element.37), channel_id=1, source_target_pairs={{16,0},{24,1},{18,2},{26,3},{20,4},{28,5},{22,6},{30,7},{17,8},{25... | collective-permute-start | bytes 196616 | tf_op jit(solution)/shard_map/ppermute | solution.py:334
  38.4 2.1 %collective-permute-start.11 = (bf16[256,128]{1,0:T(8,128)(2,1)S(1)}, bf16[256,128]{1,0:T(8,128)(2,1)S(1)}, u32[]{:S(2)}, u32[]{:S(2)}) collective-permute-start(bf16[256,128]{1,0:T(8,128)(2,1)S(1)} %get-tuple-element.38), channel_id=1, source_target_pairs={{20,0},{28,1},{22,2},{30,3},{16,4},{24,5},{18,6},{26,7},{21,8},{29... | collective-permute-start | bytes 196616 | tf_op jit(solution)/shard_map/ppermute | solution.py:334
  40.4 1.7 %near.1 = (bf16[256,128]{1,0:T(8,128)(2,1)S(1)}, bf16[256,128]{1,0:T(8,128)(2,1)S(1)}) custom-call(bf16[256,384]{1,0:T(8,128)(2,1)S(1)} %collective-permute-done.5.refs_2_.refs_0_, bf16[256,384]{1,0:T(8,128)(2,1)S(1)} %collective-permute-done.6.refs_3_.refs_1_, bf16[256,384]{1,0:T(8,128)(2,1)S(1)} %collective-permute-done.2.refs_0_.refs_2_, ...), custom_call_target="tpu_custom_call" | custom-call | tf_op jit(solution)/shard_map/near/pallas_call | solution.py:253
  42.2 0.1 collective-permute-start.12
  42.3 0.7 %collective-permute-start.13 = (bf16[256,128]{1,0:T(8,128)(2,1)S(1)}, bf16[256,128]{1,0:T(8,128)(2,1)S(1)}, u32[]{:S(2)}, u32[]{:S(2)}) collective-permute-start(bf16[256,128]{1,0:T(8,128)(2,1)S(1)} %get-tuple-element.44), channel_id=1, source_target_pairs={{5,0},{13,1},{7,2},{15,3},{1,4},{9,5},{3,6},{11,7},{4,8},{12,9},{6... | collective-permute-start | bytes 196616 | tf_op jit(solution)/shard_map/ppermute | solution.py:334
  43.0 0.3 collective-permute-done.10.rest_0_
  43.3 2.1 %collective-permute-done.11.rest_1_ = bf16[256,128]{1,0:T(8,128)(2,1)S(1)} collective-permute-done((bf16[256,128]{1,0:T(8,128)(2,1)S(1)}, bf16[256,128]{1,0:T(8,128)(2,1)S(1)}, u32[]{:S(2)}, u32[]{:S(2)}) %collective-permute-start.11) | collective-permute-done | bytes 65568 | tf_op jit(solution)/shard_map/ppermute | solution.py:334
  45.4 0.7 %collective-permute-done.12.rest_2_ = bf16[256,128]{1,0:T(8,128)(2,1)S(1)} collective-permute-done((bf16[256,128]{1,0:T(8,128)(2,1)S(1)}, bf16[256,128]{1,0:T(8,128)(2,1)S(1)}, u32[]{:S(2)}, u32[]{:S(2)}) %collective-permute-start.12) | collective-permute-done | bytes 65568 | tf_op jit(solution)/shard_map/ppermute | solution.py:334
  46.1 1.1 %collective-permute-done.13.rest_3_ = bf16[256,128]{1,0:T(8,128)(2,1)S(1)} collective-permute-done((bf16[256,128]{1,0:T(8,128)(2,1)S(1)}, bf16[256,128]{1,0:T(8,128)(2,1)S(1)}, u32[]{:S(2)}, u32[]{:S(2)}) %collective-permute-start.13) | collective-permute-done | bytes 65568 | tf_op jit(solution)/shard_map/ppermute | solution.py:334
  47.2 1.1 %finish.1 = bf16[256,768]{1,0:T(8,128)(2,1)} custom-call(bf16[256,768]{1,0:T(8,128)(2,1)S(1)} %get-tuple-element.27.hidden_ref, bf16[512,768]{1,0:T(8,128)(2,1)S(1)} %copy-done.3, bf16[256,128]{1,0:T(8,128)(2,1)S(1)} %collective-permute-done.10.rest_0_, bf16[256,128]{1,0:T(8,128)(2,1)S(1)} %collective-permute-done.11.rest_1_, ...), custom_call_target="tpu_custom_call" | custom-call | tf_op jit(solution)/shard_map/finish/pallas_call | solution.py:295
  (19 shorter events, 0.0 us)
Async XLA Ops:
  0.0 5.6 %copy-start = (bf16[5,1536,768]{2,1,0:T(8,128)(2,1)S(1)}, bf16[5,1536,768]{2,1,0:T(8,128)(2,1)}, u32[]{:S(2)}) copy-start(bf16[5,1536,768]{2,1,0:T(8,128)(2,1)} %w1.1) | copy-start | bytes 35389444
  0.0 5.6 %copy-start.2 = (bf16[256,1536]{1,0:T(8,128)(2,1)S(1)}, bf16[256,1536]{1,0:T(8,128)(2,1)}, u32[]{:S(2)}) copy-start(bf16[256,1536]{1,0:T(8,128)(2,1)} %x_ref.1) | copy-start | bytes 2359300
  1.0 3.5 %collective-permute-start = (bf16[8,768]{1,0:T(8,128)(2,1)S(1)}, bf16[8,768]{1,0:T(8,128)(2,1)S(1)}, u32[]{:S(2)}, u32[]{:S(2)}) collective-permute-start(bf16[8,768]{1,0:T(8,128)(2,1)S(1)} %get-tuple-element.25), channel_id=1, source_target_pairs={{0,1},{1,0},{2,3},{3,2},{4,8},{5,9},{6,10},{7,11},{8,4},{9,5},{10,... | collective-permute-start | bytes 36872 | tf_op jit(solution)/shard_map/ppermute | solution.py:163
  1.1 8.0 %slice-start = ((s8[5898240]{0:T(1024)(128)(4,1)}), s8[4194304]{0:T(1024)(128)(4,1)S(1)}, s32[]{:S(2)}) async-start(s8[5898240]{0:T(1024)(128)(4,1)} %bitcast), calls=%async_computation | async-start | bytes 8388608
  1.1 8.0 %copy-start.1 = (bf16[768,1536]{1,0:T(8,128)(2,1)S(1)}, bf16[768,1536]{1,0:T(8,128)(2,1)}, u32[]{:S(2)}) copy-start(bf16[768,1536]{1,0:T(8,128)(2,1)} %wqkv.3) | copy-start | bytes 7077892
  1.1 8.0 %slice-start.1 = ((s8[5898240]{0:T(1024)(128)(4,1)}), s8[1703936]{0:T(1024)(128)(4,1)S(1)}, s32[]{:S(2)}) async-start(s8[5898240]{0:T(1024)(128)(4,1)} %bitcast), calls=%async_computation.1 | async-start | bytes 3407872
  1.1 8.1 %copy-start.4 = (f32[4]{0:T(128)S(1)}, f32[4]{0:T(128)}, u32[]{:S(2)}) copy-start(f32[4]{0:T(128)} %scale_hbm.3) | copy-start | bytes 52
  1.1 4.4 %collective-permute-start.1 = (bf16[8,768]{1,0:T(8,128)(2,1)S(1)}, bf16[8,768]{1,0:T(8,128)(2,1)S(1)}, u32[]{:S(2)}, u32[]{:S(2)}) collective-permute-start(bf16[8,768]{1,0:T(8,128)(2,1)S(1)} %get-tuple-element.26), channel_id=1, source_target_pairs={{0,4},{1,5},{2,6},{3,7},{4,0},{5,1},{6,2},{7,3},{8,12},{9,13},{10,... | collective-permute-start | bytes 36872 | tf_op jit(solution)/shard_map/ppermute | solution.py:164
  9.2 38.0 %copy-start.3 = (bf16[512,768]{1,0:T(8,128)(2,1)S(1)}, bf16[512,768]{1,0:T(8,128)(2,1)}, u32[]{:S(2)}) copy-start(bf16[512,768]{1,0:T(8,128)(2,1)} %weight_ref.1) | copy-start | bytes 2359300
  11.7 10.1 %collective-permute-start.2 = (bf16[256,384]{1,0:T(8,128)(2,1)S(1)}, bf16[256,384]{1,0:T(8,128)(2,1)S(1)}, u32[]{:S(2)}, u32[]{:S(2)}) collective-permute-start(bf16[256,384]{1,0:T(8,128)(2,1)S(1)} %get-tuple-element.28), channel_id=1, source_target_pairs={{0,16},{1,24},{2,18},{3,26},{4,20},{5,28},{6,22},{7,30},{8,17},{9,... | collective-permute-start | bytes 589832 | tf_op jit(solution)/shard_map/ppermute | solution.py:330
  18.6 7.4 %collective-permute-start.5 = (bf16[256,384]{1,0:T(8,128)(2,1)S(1)}, bf16[256,384]{1,0:T(8,128)(2,1)S(1)}, u32[]{:S(2)}, u32[]{:S(2)}) collective-permute-start(bf16[256,384]{1,0:T(8,128)(2,1)S(1)} %get-tuple-element.30), channel_id=1, source_target_pairs={{0,1},{1,9},{2,3},{3,11},{4,5},{5,13},{6,7},{7,15},{8,0},{9,8},{10... | collective-permute-start | bytes 589832 | tf_op jit(solution)/shard_map/ppermute | solution.py:330
  18.7 9.6 %collective-permute-start.6 = (bf16[256,384]{1,0:T(8,128)(2,1)S(1)}, bf16[256,384]{1,0:T(8,128)(2,1)S(1)}, u32[]{:S(2)}, u32[]{:S(2)}) collective-permute-start(bf16[256,384]{1,0:T(8,128)(2,1)S(1)} %get-tuple-element.31), channel_id=1, source_target_pairs={{0,5},{1,13},{2,7},{3,15},{4,1},{5,9},{6,3},{7,11},{8,4},{9,12},{1... | collective-permute-start | bytes 589832 | tf_op jit(solution)/shard_map/ppermute | solution.py:330
  18.8 12.4 %collective-permute-start.3 = (bf16[256,384]{1,0:T(8,128)(2,1)S(1)}, bf16[256,384]{1,0:T(8,128)(2,1)S(1)}, u32[]{:S(2)}, u32[]{:S(2)}) collective-permute-start(bf16[256,384]{1,0:T(8,128)(2,1)S(1)} %get-tuple-element.29), channel_id=1, source_target_pairs={{0,20},{1,28},{2,22},{3,30},{4,16},{5,24},{6,18},{7,26},{8,21},{9,... | collective-permute-start | bytes 589832 | tf_op jit(solution)/shard_map/ppermute | solution.py:330
  21.9 13.0 %collective-permute-start.7 = (bf16[256,384]{1,0:T(8,128)(2,1)S(1)}, bf16[256,384]{1,0:T(8,128)(2,1)S(1)}, u32[]{:S(2)}, u32[]{:S(2)}) collective-permute-start(bf16[256,384]{1,0:T(8,128)(2,1)S(1)} %collective-permute-done.2.refs_0_.refs_2_), channel_id=1, source_target_pairs={{0,1},{1,0},{2,3},{3,2},{4,5},{5,4},{6,7},{7,6},{8,9},{9,8},{10,11... | collective-permute-start | bytes 589832 | tf_op jit(solution)/shard_map/ppermute | solution.py:332
  26.0 8.9 %collective-permute-start.8 = (bf16[256,384]{1,0:T(8,128)(2,1)S(1)}, bf16[256,384]{1,0:T(8,128)(2,1)S(1)}, u32[]{:S(2)}, u32[]{:S(2)}) collective-permute-start(bf16[256,384]{1,0:T(8,128)(2,1)S(1)} %collective-permute-done.5.refs_2_.refs_0_), channel_id=1, source_target_pairs={{0,1},{1,0},{2,3},{3,2},{4,5},{5,4},{6,7},{7,6},{8,9},{9,8},{10,11... | collective-permute-start | bytes 589832 | tf_op jit(solution)/shard_map/ppermute | solution.py:332
  28.2 6.6 %collective-permute-start.9 = (bf16[256,384]{1,0:T(8,128)(2,1)S(1)}, bf16[256,384]{1,0:T(8,128)(2,1)S(1)}, u32[]{:S(2)}, u32[]{:S(2)}) collective-permute-start(bf16[256,384]{1,0:T(8,128)(2,1)S(1)} %collective-permute-done.6.refs_3_.refs_1_), channel_id=1, source_target_pairs={{0,1},{1,0},{2,3},{3,2},{4,5},{5,4},{6,7},{7,6},{8,9},{9,8},{10,11... | collective-permute-start | bytes 589832 | tf_op jit(solution)/shard_map/ppermute | solution.py:332
  31.1 5.4 %collective-permute-start.4 = (bf16[256,384]{1,0:T(8,128)(2,1)S(1)}, bf16[256,384]{1,0:T(8,128)(2,1)S(1)}, u32[]{:S(2)}, u32[]{:S(2)}) collective-permute-start(bf16[256,384]{1,0:T(8,128)(2,1)S(1)} %collective-permute-done.3.refs_1_.refs_3_), channel_id=1, source_target_pairs={{0,1},{1,0},{2,3},{3,2},{4,5},{5,4},{6,7},{7,6},{8,9},{9,8},{10,11... | collective-permute-start | bytes 589832 | tf_op jit(solution)/shard_map/ppermute | solution.py:332
  37.0 6.3 %collective-permute-start.10 = (bf16[256,128]{1,0:T(8,128)(2,1)S(1)}, bf16[256,128]{1,0:T(8,128)(2,1)S(1)}, u32[]{:S(2)}, u32[]{:S(2)}) collective-permute-start(bf16[256,128]{1,0:T(8,128)(2,1)S(1)} %get-tuple-element.37), channel_id=1, source_target_pairs={{16,0},{24,1},{18,2},{26,3},{20,4},{28,5},{22,6},{30,7},{17,8},{25... | collective-permute-start | bytes 196616 | tf_op jit(solution)/shard_map/ppermute | solution.py:334
  38.4 7.1 %collective-permute-start.11 = (bf16[256,128]{1,0:T(8,128)(2,1)S(1)}, bf16[256,128]{1,0:T(8,128)(2,1)S(1)}, u32[]{:S(2)}, u32[]{:S(2)}) collective-permute-start(bf16[256,128]{1,0:T(8,128)(2,1)S(1)} %get-tuple-element.38), channel_id=1, source_target_pairs={{20,0},{28,1},{22,2},{30,3},{16,4},{24,5},{18,6},{26,7},{21,8},{29... | collective-permute-start | bytes 196616 | tf_op jit(solution)/shard_map/ppermute | solution.py:334
  42.2 3.9 %collective-permute-start.12 = (bf16[256,128]{1,0:T(8,128)(2,1)S(1)}, bf16[256,128]{1,0:T(8,128)(2,1)S(1)}, u32[]{:S(2)}, u32[]{:S(2)}) collective-permute-start(bf16[256,128]{1,0:T(8,128)(2,1)S(1)} %get-tuple-element.43), channel_id=1, source_target_pairs={{1,0},{9,1},{3,2},{11,3},{5,4},{13,5},{7,6},{15,7},{0,8},{8,9},{2,... | collective-permute-start | bytes 196616 | tf_op jit(solution)/shard_map/ppermute | solution.py:334
  42.3 4.9 %collective-permute-start.13 = (bf16[256,128]{1,0:T(8,128)(2,1)S(1)}, bf16[256,128]{1,0:T(8,128)(2,1)S(1)}, u32[]{:S(2)}, u32[]{:S(2)}) collective-permute-start(bf16[256,128]{1,0:T(8,128)(2,1)S(1)} %get-tuple-element.44), channel_id=1, source_target_pairs={{5,0},{13,1},{7,2},{15,3},{1,4},{9,5},{3,6},{11,7},{4,8},{12,9},{6... | collective-permute-start | bytes 196616 | tf_op jit(solution)/shard_map/ppermute | solution.py:334

commit v7 on v6

--- a/solution.py
+++ b/solution.py
@@ -311,7 +311,8 @@
             for b in range(batch_count):
                 h = head_of(r, g, heads)
                 chip = heads * (h // half) + half * (b % 2) + h % half
-                core = (g // half + r // half) % 2
+                far = h // half != g // heads
+                core = (g // half + (h // half if far else 1)) % 2
                 target = chip * batch_count + b - b % 2 + core
                 pairs.append((g * batch_count + b, target))
         rounds.append(pairs)

time: 48.4 us -> 48.2 us (level)
  waiting for transfers between devices: 8.82 us -> 7.07 us
  starting transfers between devices: 25.8 us -> 27.2 us
    ppermute x4, starting transfers between devices: 10.7 us -> 12.3 us  [by_heads(): lax.ppermute(unit, 'batch', cores)]
    ppermute x4, waiting for transfers between devices: 3.54 us -> 2.26 us  [by_heads(): lax.ppermute(unit, both, pairs)]
  transfers between devices with their start and end apart: 14 -> 14, of which waited for: 7 -> 5; matrix products, arithmetic and copies ran while one was open for 0% -> 0% of each run, Pallas kernels for 10% -> 10%
where the time goes in v7:
time: 48.2 us; the launch traced here: 48 us
  starting transfers between devices  27.2 us (56%)
  Pallas kernels  13.5 us (28%)
  waiting for transfers between devices  7.07 us (15%)
    ppermute x4, starting transfers between devices, by_heads(): lax.ppermute(unit, 'batch', cores)  12.3 us
    ppermute x4, starting transfers between devices, by_heads(): lax.ppermute(unit, both, pairs)  7.16 us
    ppermute x4, starting transfers between devices, by_heads(): lax.ppermute(out, both, [(target, source) for source, target in rounds[r]])  4.39 us
    pallas_call x3, Pallas kernels, attend(): pl.pallas_call(functools.partial(kernel, head=head, count=count), out_sha...  3.9 us
    ppermute x4, waiting for transfers between devices, by_heads(): lax.ppermute(out, both, [(target, source) for source, target in rounds[r]])  3.72 us
    pallas_call x1, Pallas kernels, stem(): pl.pallas_call(functools.partial(first_kernel, count=lax.axis_size('seq')...  3.6 us
    ppermute x1, starting transfers between devices, stem(): pair = lax.ppermute(to_pair, ('seq', 'batch'), swaps(0))  3.32 us
    pallas_call x1, Pallas kernels, stem(): pl.pallas_call(functools.partial(second_kernel, **fixed), out_shape=[shap...  2.49 us
  transfers between devices with their start and end apart: 14, of which 5 were waited for; matrix products, arithmetic and copies ran while one was open for 0% of the time, Pallas kernels for 10%

profile of v7, /device:TPU:1, one launch (start us, length us, event | category | flops | bytes accessed | tf_op | source)
XLA Modules:
  0.0 48.0 jit_solution(8291354591974429149)
XLA Ops:
  0.0 1.0 %edges.1 = (bf16[8,768]{1,0:T(8,128)(2,1)S(1)}, bf16[8,768]{1,0:T(8,128)(2,1)S(1)}) custom-call(bf16[256,1536]{1,0:T(8,128)(2,1)} %x_ref.1, bf16[5,1536,768]{2,1,0:T(8,128)(2,1)} %w1.1), custom_call_target="tpu_custom_call" | custom-call | tf_op jit(solution)/shard_map/edges/pallas_call | solution.py:150
  1.0 0.1 collective-permute-start
  1.1 3.3 %collective-permute-start.1 = (bf16[8,768]{1,0:T(8,128)(2,1)S(1)}, bf16[8,768]{1,0:T(8,128)(2,1)S(1)}, u32[]{:S(2)}, u32[]{:S(2)}) collective-permute-start(bf16[8,768]{1,0:T(8,128)(2,1)S(1)} %get-tuple-element.26), channel_id=1, source_target_pairs={{0,4},{1,5},{2,6},{3,7},{4,0},{5,1},{6,2},{7,3},{8,12},{9,13},{10,... | collective-permute-start | bytes 36872 | tf_op jit(solution)/shard_map/ppermute | solution.py:164
  4.5 0.0 collective-permute-done.other_ref
  4.5 1.1 %collective-permute-done.1.pair_ref = bf16[8,768]{1,0:T(8,128)(2,1)S(1)} collective-permute-done((bf16[8,768]{1,0:T(8,128)(2,1)S(1)}, bf16[8,768]{1,0:T(8,128)(2,1)S(1)}, u32[]{:S(2)}, u32[]{:S(2)}) %collective-permute-start.1) | collective-permute-done | bytes 12320 | tf_op jit(solution)/shard_map/ppermute | solution.py:164
  5.6 3.6 %first.1.first_ref = bf16[272,768]{1,0:T(8,128)(2,1)S(1)} custom-call(bf16[256,1536]{1,0:T(8,128)(2,1)S(1)} %copy-done.2, bf16[8,768]{1,0:T(8,128)(2,1)S(1)} %collective-permute-done.other_ref, bf16[8,768]{1,0:T(8,128)(2,1)S(1)} %collective-permute-done.1.pair_ref, bf16[5,1536,768]{2,1,0:T(8,128)(2,1)S(1)} %copy-done), custom_call_target="tpu_custom_call" | custom-call | tf_op jit(solution)/shard_map/first/pallas_call | solution.py:165
  9.2 0.0 copy-start.3
  9.2 2.5 %second.1 = (bf16[256,768]{1,0:T(8,128)(2,1)S(1)}, bf16[256,384]{1,0:T(8,128)(2,1)S(1)}) custom-call(bf16[272,768]{1,0:T(8,128)(2,1)S(1)} %first.1.first_ref, bf16[5,768,768]{2,1,0:T(8,128)(2,1)S(1)} %bitcast.1, bf16[768,1536]{1,0:T(8,128)(2,1)S(1)} %copy-done.1, f32[4]{0:T(128)S(1)} %copy-done.4), custom_call_target="tpu_custom_call" | custom-call | tf_op jit(solution)/shard_map/second/pallas_call | solution.py:178
  11.7 3.5 %collective-permute-start.2 = (bf16[256,384]{1,0:T(8,128)(2,1)S(1)}, bf16[256,384]{1,0:T(8,128)(2,1)S(1)}, u32[]{:S(2)}, u32[]{:S(2)}) collective-permute-start(bf16[256,384]{1,0:T(8,128)(2,1)S(1)} %get-tuple-element.28), channel_id=1, source_target_pairs={{0,17},{1,25},{2,19},{3,27},{4,21},{5,29},{6,23},{7,31},{8,16},{9,... | collective-permute-start | bytes 589832 | tf_op jit(solution)/shard_map/ppermute | solution.py:331
  15.2 1.4 %third.1 = (bf16[256,384]{1,0:T(8,128)(2,1)S(1)}, bf16[256,384]{1,0:T(8,128)(2,1)S(1)}, bf16[256,384]{1,0:T(8,128)(2,1)S(1)}) custom-call(bf16[256,768]{1,0:T(8,128)(2,1)S(1)} %get-tuple-element.27.hidden_ref, bf16[768,1536]{1,0:T(8,128)(2,1)S(1)} %copy-done.1, f32[4]{0:T(128)S(1)} %copy-done.4), custom_call_target="tpu_custom_call" | custom-call | tf_op jit(solution)/shard_map/third/pallas_call | solution.py:187
  16.6 2.3 %collective-permute-start.5 = (bf16[256,384]{1,0:T(8,128)(2,1)S(1)}, bf16[256,384]{1,0:T(8,128)(2,1)S(1)}, u32[]{:S(2)}, u32[]{:S(2)}) collective-permute-start(bf16[256,384]{1,0:T(8,128)(2,1)S(1)} %get-tuple-element.30), channel_id=1, source_target_pairs={{0,1},{1,9},{2,3},{3,11},{4,5},{5,13},{6,7},{7,15},{8,0},{9,8},{10... | collective-permute-start | bytes 589832 | tf_op jit(solution)/shard_map/ppermute | solution.py:331
  18.9 0.5 %collective-permute-start.6 = (bf16[256,384]{1,0:T(8,128)(2,1)S(1)}, bf16[256,384]{1,0:T(8,128)(2,1)S(1)}, u32[]{:S(2)}, u32[]{:S(2)}) collective-permute-start(bf16[256,384]{1,0:T(8,128)(2,1)S(1)} %get-tuple-element.31), channel_id=1, source_target_pairs={{0,5},{1,13},{2,7},{3,15},{4,1},{5,9},{6,3},{7,11},{8,4},{9,12},{1... | collective-permute-start | bytes 589832 | tf_op jit(solution)/shard_map/ppermute | solution.py:331
  19.4 0.9 %collective-permute-start.3 = (bf16[256,384]{1,0:T(8,128)(2,1)S(1)}, bf16[256,384]{1,0:T(8,128)(2,1)S(1)}, u32[]{:S(2)}, u32[]{:S(2)}) collective-permute-start(bf16[256,384]{1,0:T(8,128)(2,1)S(1)} %get-tuple-element.29), channel_id=1, source_target_pairs={{0,21},{1,29},{2,23},{3,31},{4,17},{5,25},{6,19},{7,27},{8,20},{9,... | collective-permute-start | bytes 589832 | tf_op jit(solution)/shard_map/ppermute | solution.py:331
  20.3 0.3 collective-permute-done.2.refs_0_.refs_2_
  20.6 6.7 %collective-permute-start.7 = (bf16[256,384]{1,0:T(8,128)(2,1)S(1)}, bf16[256,384]{1,0:T(8,128)(2,1)S(1)}, u32[]{:S(2)}, u32[]{:S(2)}) collective-permute-start(bf16[256,384]{1,0:T(8,128)(2,1)S(1)} %collective-permute-done.2.refs_0_.refs_2_), channel_id=1, source_target_pairs={{0,1},{1,0},{2,3},{3,2},{4,5},{5,4},{6,7},{7,6},{8,9},{9,8},{10,11... | collective-permute-start | bytes 589832 | tf_op jit(solution)/shard_map/ppermute | solution.py:333
  27.3 0.0 collective-permute-done.5.refs_2_.refs_0_
  27.3 0.0 collective-permute-start.8
  27.4 0.0 collective-permute-done.6.refs_3_.refs_1_
  27.4 1.0 %collective-permute-start.9 = (bf16[256,384]{1,0:T(8,128)(2,1)S(1)}, bf16[256,384]{1,0:T(8,128)(2,1)S(1)}, u32[]{:S(2)}, u32[]{:S(2)}) collective-permute-start(bf16[256,384]{1,0:T(8,128)(2,1)S(1)} %collective-permute-done.6.refs_3_.refs_1_), channel_id=1, source_target_pairs={{0,1},{1,0},{2,3},{3,2},{4,5},{5,4},{6,7},{7,6},{8,9},{9,8},{10,11... | collective-permute-start | bytes 589832 | tf_op jit(solution)/shard_map/ppermute | solution.py:333
  28.4 1.9 %collective-permute-done.3.refs_1_.refs_3_ = bf16[256,384]{1,0:T(8,128)(2,1)S(1)} collective-permute-done((bf16[256,384]{1,0:T(8,128)(2,1)S(1)}, bf16[256,384]{1,0:T(8,128)(2,1)S(1)}, u32[]{:S(2)}, u32[]{:S(2)}) %collective-permute-start.3) | collective-permute-done | bytes 196640 | tf_op jit(solution)/shard_map/ppermute | solution.py:331
  30.3 4.5 %collective-permute-start.4 = (bf16[256,384]{1,0:T(8,128)(2,1)S(1)}, bf16[256,384]{1,0:T(8,128)(2,1)S(1)}, u32[]{:S(2)}, u32[]{:S(2)}) collective-permute-start(bf16[256,384]{1,0:T(8,128)(2,1)S(1)} %collective-permute-done.3.refs_1_.refs_3_), channel_id=1, source_target_pairs={{0,1},{1,0},{2,3},{3,2},{4,5},{5,4},{6,7},{7,6},{8,9},{9,8},{10,11... | collective-permute-start | bytes 589832 | tf_op jit(solution)/shard_map/ppermute | solution.py:333
  34.8 0.0 collective-permute-done.9.refs_6_.refs_7_
  34.8 1.7 %most.1 = (f32[512,128]{1,0:T(8,128)S(1)}, f32[512,128]{1,0:T(8,128)S(1)}, f32[512,128]{1,0:T(8,128)S(1)}) custom-call(bf16[256,384]{1,0:T(8,128)(2,1)S(1)} %collective-permute-done.2.refs_0_.refs_2_, bf16[256,384]{1,0:T(8,128)(2,1)S(1)} %collective-permute-done.3.refs_1_.refs_3_, bf16[256,384]{1,0:T(8,128)(2,1)S(1)} %collective-permute-done.5.refs_2_.refs_0_, ...), custom_call_target="tpu_custom_call" | custom-call | tf_op jit(solution)/shard_map/most/pallas_call | solution.py:253
  36.5 0.0 collective-permute-done.4.refs_2_.refs_5_
  36.5 0.5 %last.1 = (bf16[256,128]{1,0:T(8,128)(2,1)S(1)}, bf16[256,128]{1,0:T(8,128)(2,1)S(1)}) custom-call(bf16[256,384]{1,0:T(8,128)(2,1)S(1)} %collective-permute-done.2.refs_0_.refs_2_, bf16[256,384]{1,0:T(8,128)(2,1)S(1)} %collective-permute-done.3.refs_1_.refs_3_, bf16[256,384]{1,0:T(8,128)(2,1)S(1)} %collective-permute-done.4.refs_2_.refs_5_, ...), custom_call_target="tpu_custom_call" | custom-call | tf_op jit(solution)/shard_map/last/pallas_call | solution.py:253
  37.0 2.6 %collective-permute-start.10 = (bf16[256,128]{1,0:T(8,128)(2,1)S(1)}, bf16[256,128]{1,0:T(8,128)(2,1)S(1)}, u32[]{:S(2)}, u32[]{:S(2)}) collective-permute-start(bf16[256,128]{1,0:T(8,128)(2,1)S(1)} %get-tuple-element.37), channel_id=1, source_target_pairs={{17,0},{25,1},{19,2},{27,3},{21,4},{29,5},{23,6},{31,7},{16,8},{24... | collective-permute-start | bytes 196616 | tf_op jit(solution)/shard_map/ppermute | solution.py:335
  39.6 1.8 %near.1 = (bf16[256,128]{1,0:T(8,128)(2,1)S(1)}, bf16[256,128]{1,0:T(8,128)(2,1)S(1)}) custom-call(bf16[256,384]{1,0:T(8,128)(2,1)S(1)} %collective-permute-done.5.refs_2_.refs_0_, bf16[256,384]{1,0:T(8,128)(2,1)S(1)} %collective-permute-done.6.refs_3_.refs_1_, bf16[256,384]{1,0:T(8,128)(2,1)S(1)} %collective-permute-done.2.refs_0_.refs_2_, ...), custom_call_target="tpu_custom_call" | custom-call | tf_op jit(solution)/shard_map/near/pallas_call | solution.py:253
  41.4 0.1 collective-permute-start.12
  41.5 1.7 %collective-permute-start.13 = (bf16[256,128]{1,0:T(8,128)(2,1)S(1)}, bf16[256,128]{1,0:T(8,128)(2,1)S(1)}, u32[]{:S(2)}, u32[]{:S(2)}) collective-permute-start(bf16[256,128]{1,0:T(8,128)(2,1)S(1)} %get-tuple-element.44), channel_id=1, source_target_pairs={{5,0},{13,1},{7,2},{15,3},{1,4},{9,5},{3,6},{11,7},{4,8},{12,9},{6... | collective-permute-start | bytes 196616 | tf_op jit(solution)/shard_map/ppermute | solution.py:335
  43.2 2.9 %collective-permute-done.11.rest_1_ = bf16[256,128]{1,0:T(8,128)(2,1)S(1)} collective-permute-done((bf16[256,128]{1,0:T(8,128)(2,1)S(1)}, bf16[256,128]{1,0:T(8,128)(2,1)S(1)}, u32[]{:S(2)}, u32[]{:S(2)}) %collective-permute-start.11) | collective-permute-done | bytes 65568 | tf_op jit(solution)/shard_map/ppermute | solution.py:335
  46.0 0.9 %collective-permute-done.13.rest_3_ = bf16[256,128]{1,0:T(8,128)(2,1)S(1)} collective-permute-done((bf16[256,128]{1,0:T(8,128)(2,1)S(1)}, bf16[256,128]{1,0:T(8,128)(2,1)S(1)}, u32[]{:S(2)}, u32[]{:S(2)}) %collective-permute-start.13) | collective-permute-done | bytes 65568 | tf_op jit(solution)/shard_map/ppermute | solution.py:335
  46.9 1.1 %finish.1 = bf16[256,768]{1,0:T(8,128)(2,1)} custom-call(bf16[256,768]{1,0:T(8,128)(2,1)S(1)} %get-tuple-element.27.hidden_ref, bf16[512,768]{1,0:T(8,128)(2,1)S(1)} %copy-done.3, bf16[256,128]{1,0:T(8,128)(2,1)S(1)} %collective-permute-done.10.rest_0_, bf16[256,128]{1,0:T(8,128)(2,1)S(1)} %collective-permute-done.11.rest_1_, ...), custom_call_target="tpu_custom_call" | custom-call | tf_op jit(solution)/shard_map/finish/pallas_call | solution.py:295
  (19 shorter events, 0.0 us)
Async XLA Ops:
  0.0 5.6 %copy-start = (bf16[5,1536,768]{2,1,0:T(8,128)(2,1)S(1)}, bf16[5,1536,768]{2,1,0:T(8,128)(2,1)}, u32[]{:S(2)}) copy-start(bf16[5,1536,768]{2,1,0:T(8,128)(2,1)} %w1.1) | copy-start | bytes 35389444
  0.0 5.6 %copy-start.2 = (bf16[256,1536]{1,0:T(8,128)(2,1)S(1)}, bf16[256,1536]{1,0:T(8,128)(2,1)}, u32[]{:S(2)}) copy-start(bf16[256,1536]{1,0:T(8,128)(2,1)} %x_ref.1) | copy-start | bytes 2359300
  1.0 3.5 %collective-permute-start = (bf16[8,768]{1,0:T(8,128)(2,1)S(1)}, bf16[8,768]{1,0:T(8,128)(2,1)S(1)}, u32[]{:S(2)}, u32[]{:S(2)}) collective-permute-start(bf16[8,768]{1,0:T(8,128)(2,1)S(1)} %get-tuple-element.25), channel_id=1, source_target_pairs={{0,1},{1,0},{2,3},{3,2},{4,8},{5,9},{6,10},{7,11},{8,4},{9,5},{10,... | collective-permute-start | bytes 36872 | tf_op jit(solution)/shard_map/ppermute | solution.py:163
  1.1 8.0 %slice-start = ((s8[5898240]{0:T(1024)(128)(4,1)}), s8[4194304]{0:T(1024)(128)(4,1)S(1)}, s32[]{:S(2)}) async-start(s8[5898240]{0:T(1024)(128)(4,1)} %bitcast), calls=%async_computation | async-start | bytes 8388608
  1.1 8.0 %copy-start.1 = (bf16[768,1536]{1,0:T(8,128)(2,1)S(1)}, bf16[768,1536]{1,0:T(8,128)(2,1)}, u32[]{:S(2)}) copy-start(bf16[768,1536]{1,0:T(8,128)(2,1)} %wqkv.3) | copy-start | bytes 7077892
  1.1 8.0 %slice-start.1 = ((s8[5898240]{0:T(1024)(128)(4,1)}), s8[1703936]{0:T(1024)(128)(4,1)S(1)}, s32[]{:S(2)}) async-start(s8[5898240]{0:T(1024)(128)(4,1)} %bitcast), calls=%async_computation.1 | async-start | bytes 3407872
  1.1 8.1 %copy-start.4 = (f32[4]{0:T(128)S(1)}, f32[4]{0:T(128)}, u32[]{:S(2)}) copy-start(f32[4]{0:T(128)} %scale_hbm.3) | copy-start | bytes 52
  1.1 4.4 %collective-permute-start.1 = (bf16[8,768]{1,0:T(8,128)(2,1)S(1)}, bf16[8,768]{1,0:T(8,128)(2,1)S(1)}, u32[]{:S(2)}, u32[]{:S(2)}) collective-permute-start(bf16[8,768]{1,0:T(8,128)(2,1)S(1)} %get-tuple-element.26), channel_id=1, source_target_pairs={{0,4},{1,5},{2,6},{3,7},{4,0},{5,1},{6,2},{7,3},{8,12},{9,13},{10,... | collective-permute-start | bytes 36872 | tf_op jit(solution)/shard_map/ppermute | solution.py:164
  9.2 37.7 %copy-start.3 = (bf16[512,768]{1,0:T(8,128)(2,1)S(1)}, bf16[512,768]{1,0:T(8,128)(2,1)}, u32[]{:S(2)}) copy-start(bf16[512,768]{1,0:T(8,128)(2,1)} %weight_ref.1) | copy-start | bytes 2359300
  11.7 8.9 %collective-permute-start.2 = (bf16[256,384]{1,0:T(8,128)(2,1)S(1)}, bf16[256,384]{1,0:T(8,128)(2,1)S(1)}, u32[]{:S(2)}, u32[]{:S(2)}) collective-permute-start(bf16[256,384]{1,0:T(8,128)(2,1)S(1)} %get-tuple-element.28), channel_id=1, source_target_pairs={{0,17},{1,25},{2,19},{3,27},{4,21},{5,29},{6,23},{7,31},{8,16},{9,... | collective-permute-start | bytes 589832 | tf_op jit(solution)/shard_map/ppermute | solution.py:331
  16.6 10.7 %collective-permute-start.5 = (bf16[256,384]{1,0:T(8,128)(2,1)S(1)}, bf16[256,384]{1,0:T(8,128)(2,1)S(1)}, u32[]{:S(2)}, u32[]{:S(2)}) collective-permute-start(bf16[256,384]{1,0:T(8,128)(2,1)S(1)} %get-tuple-element.30), channel_id=1, source_target_pairs={{0,1},{1,9},{2,3},{3,11},{4,5},{5,13},{6,7},{7,15},{8,0},{9,8},{10... | collective-permute-start | bytes 589832 | tf_op jit(solution)/shard_map/ppermute | solution.py:331
  18.9 8.4 %collective-permute-start.6 = (bf16[256,384]{1,0:T(8,128)(2,1)S(1)}, bf16[256,384]{1,0:T(8,128)(2,1)S(1)}, u32[]{:S(2)}, u32[]{:S(2)}) collective-permute-start(bf16[256,384]{1,0:T(8,128)(2,1)S(1)} %get-tuple-element.31), channel_id=1, source_target_pairs={{0,5},{1,13},{2,7},{3,15},{4,1},{5,9},{6,3},{7,11},{8,4},{9,12},{1... | collective-permute-start | bytes 589832 | tf_op jit(solution)/shard_map/ppermute | solution.py:331
  19.4 10.9 %collective-permute-start.3 = (bf16[256,384]{1,0:T(8,128)(2,1)S(1)}, bf16[256,384]{1,0:T(8,128)(2,1)S(1)}, u32[]{:S(2)}, u32[]{:S(2)}) collective-permute-start(bf16[256,384]{1,0:T(8,128)(2,1)S(1)} %get-tuple-element.29), channel_id=1, source_target_pairs={{0,21},{1,29},{2,23},{3,31},{4,17},{5,25},{6,19},{7,27},{8,20},{9,... | collective-permute-start | bytes 589832 | tf_op jit(solution)/shard_map/ppermute | solution.py:331
  20.6 14.2 %collective-permute-start.7 = (bf16[256,384]{1,0:T(8,128)(2,1)S(1)}, bf16[256,384]{1,0:T(8,128)(2,1)S(1)}, u32[]{:S(2)}, u32[]{:S(2)}) collective-permute-start(bf16[256,384]{1,0:T(8,128)(2,1)S(1)} %collective-permute-done.2.refs_0_.refs_2_), channel_id=1, source_target_pairs={{0,1},{1,0},{2,3},{3,2},{4,5},{5,4},{6,7},{7,6},{8,9},{9,8},{10,11... | collective-permute-start | bytes 589832 | tf_op jit(solution)/shard_map/ppermute | solution.py:333
  27.3 7.5 %collective-permute-start.8 = (bf16[256,384]{1,0:T(8,128)(2,1)S(1)}, bf16[256,384]{1,0:T(8,128)(2,1)S(1)}, u32[]{:S(2)}, u32[]{:S(2)}) collective-permute-start(bf16[256,384]{1,0:T(8,128)(2,1)S(1)} %collective-permute-done.5.refs_2_.refs_0_), channel_id=1, source_target_pairs={{0,1},{1,0},{2,3},{3,2},{4,5},{5,4},{6,7},{7,6},{8,9},{9,8},{10,11... | collective-permute-start | bytes 589832 | tf_op jit(solution)/shard_map/ppermute | solution.py:333
  27.4 7.5 %collective-permute-start.9 = (bf16[256,384]{1,0:T(8,128)(2,1)S(1)}, bf16[256,384]{1,0:T(8,128)(2,1)S(1)}, u32[]{:S(2)}, u32[]{:S(2)}) collective-permute-start(bf16[256,384]{1,0:T(8,128)(2,1)S(1)} %collective-permute-done.6.refs_3_.refs_1_), channel_id=1, source_target_pairs={{0,1},{1,0},{2,3},{3,2},{4,5},{5,4},{6,7},{7,6},{8,9},{9,8},{10,11... | collective-permute-start | bytes 589832 | tf_op jit(solution)/shard_map/ppermute | solution.py:333
  30.3 6.2 %collective-permute-start.4 = (bf16[256,384]{1,0:T(8,128)(2,1)S(1)}, bf16[256,384]{1,0:T(8,128)(2,1)S(1)}, u32[]{:S(2)}, u32[]{:S(2)}) collective-permute-start(bf16[256,384]{1,0:T(8,128)(2,1)S(1)} %collective-permute-done.3.refs_1_.refs_3_), channel_id=1, source_target_pairs={{0,1},{1,0},{2,3},{3,2},{4,5},{5,4},{6,7},{7,6},{8,9},{9,8},{10,11... | collective-permute-start | bytes 589832 | tf_op jit(solution)/shard_map/ppermute | solution.py:333
  37.0 6.2 %collective-permute-start.10 = (bf16[256,128]{1,0:T(8,128)(2,1)S(1)}, bf16[256,128]{1,0:T(8,128)(2,1)S(1)}, u32[]{:S(2)}, u32[]{:S(2)}) collective-permute-start(bf16[256,128]{1,0:T(8,128)(2,1)S(1)} %get-tuple-element.37), channel_id=1, source_target_pairs={{17,0},{25,1},{19,2},{27,3},{21,4},{29,5},{23,6},{31,7},{16,8},{24... | collective-permute-start | bytes 196616 | tf_op jit(solution)/shard_map/ppermute | solution.py:335
  39.6 6.4 %collective-permute-start.11 = (bf16[256,128]{1,0:T(8,128)(2,1)S(1)}, bf16[256,128]{1,0:T(8,128)(2,1)S(1)}, u32[]{:S(2)}, u32[]{:S(2)}) collective-permute-start(bf16[256,128]{1,0:T(8,128)(2,1)S(1)} %get-tuple-element.38), channel_id=1, source_target_pairs={{21,0},{29,1},{23,2},{31,3},{17,4},{25,5},{19,6},{27,7},{20,8},{28... | collective-permute-start | bytes 196616 | tf_op jit(solution)/shard_map/ppermute | solution.py:335
  41.4 4.6 %collective-permute-start.12 = (bf16[256,128]{1,0:T(8,128)(2,1)S(1)}, bf16[256,128]{1,0:T(8,128)(2,1)S(1)}, u32[]{:S(2)}, u32[]{:S(2)}) collective-permute-start(bf16[256,128]{1,0:T(8,128)(2,1)S(1)} %get-tuple-element.43), channel_id=1, source_target_pairs={{1,0},{9,1},{3,2},{11,3},{5,4},{13,5},{7,6},{15,7},{0,8},{8,9},{2,... | collective-permute-start | bytes 196616 | tf_op jit(solution)/shard_map/ppermute | solution.py:335
  41.5 5.4 %collective-permute-start.13 = (bf16[256,128]{1,0:T(8,128)(2,1)S(1)}, bf16[256,128]{1,0:T(8,128)(2,1)S(1)}, u32[]{:S(2)}, u32[]{:S(2)}) collective-permute-start(bf16[256,128]{1,0:T(8,128)(2,1)S(1)} %get-tuple-element.44), channel_id=1, source_target_pairs={{5,0},{13,1},{7,2},{15,3},{1,4},{9,5},{3,6},{11,7},{4,8},{12,9},{6... | collective-permute-start | bytes 196616 | tf_op jit(solution)/shard_map/ppermute | solution.py:335

commit v8 on v7

--- a/solution.py
+++ b/solution.py
@@ -64,13 +64,16 @@
     before = unfolded(jnp.where(even, other, pair)) * has_before
     x[0:rows] = x_ref[...]
     x[rows:] = jnp.concatenate([after, rest, rest, before], axis=0).astype(BF16)
-    for j in range(TAPS):
-        product = rolled(jnp.dot(x[...], w1[j], preferred_element_type=F32), j)
-        if j == 0:
-            total[...] = product
-        else:
-            total[...] += product
-    first_ref[0:rows] = jax.nn.gelu(total[0:rows]).astype(BF16)
+    width = total.shape[1]
+    for n in range(0, width, width // 3):
+        part = slice(n, n + width // 3)
+        for j in range(TAPS):
+            product = rolled(jnp.dot(x[...], w1[j, :, part], preferred_element_type=F32), j)
+            if j == 0:
+                total[:, part] = product
+            else:
+                total[:, part] += product
+        first_ref[0:rows, part] = jax.nn.gelu(total[0:rows, part]).astype(BF16)
     after = jax.nn.gelu(total[rows : rows + EDGE]) * has_after
     before = jax.nn.gelu(total[rows + EDGE :]) * has_before
     first_ref[rows:] = jnp.concatenate([after, before], axis=0).astype(BF16)
@@ -263,7 +266,7 @@
 def attention(own, swap):
     rows, wide = own[0].shape
     shape = jax.ShapeDtypeStruct
-    steps = [0, 1], [2, 3]
+    steps = [0, 1], [3, 2]
     result = [shape((rows, wide // 3), BF16)] * len(steps[0])
     partial = [shape((len(steps[0]) * rows, wide // 3), F32)] * 3
     other = [swap(unit) for unit in own]
@@ -310,9 +313,9 @@
         for g in range(seq_count):
             for b in range(batch_count):
                 h = head_of(r, g, heads)
-                chip = heads * (h // half) + half * (b % 2) + h % half
+                chip = heads * (h // half) + half * (b % 2 ^ h // half) + h % half
                 far = h // half != g // heads
-                core = (g // half + (h // half if far else 1)) % 2
+                core = (g // half + (h // half if far else 1 + g // heads)) % 2
                 target = chip * batch_count + b - b % 2 + core
                 pairs.append((g * batch_count + b, target))
         rounds.append(pairs)

time: 48.2 us -> 47.9 us (level)
  waiting for transfers between devices: 7.07 us -> 4.96 us
  starting transfers between devices: 27.2 us -> 29.2 us
    ppermute x4, starting transfers between devices: 12.3 us -> 14.3 us  [by_heads(): lax.ppermute(unit, 'batch', cores)]
    ppermute x4, waiting for transfers between devices: 2.26 us -> 0.27 us  [by_heads(): lax.ppermute(unit, both, pairs)]
  transfers between devices with their start and end apart: 14 -> 14, of which waited for: 5 -> 6; matrix products, arithmetic and copies ran while one was open for 0% -> 0% of each run, Pallas kernels for 10% -> 10%
where the time goes in v8:
time: 47.9 us; the launch traced here: 47.8 us
  starting transfers between devices  29.2 us (61%)
  Pallas kernels  13.4 us (28%)
  waiting for transfers between devices  4.96 us (10%)
    ppermute x4, starting transfers between devices, by_heads(): lax.ppermute(unit, 'batch', cores)  14.3 us
    ppermute x4, starting transfers between devices, by_heads(): lax.ppermute(unit, both, pairs)  7.11 us
    ppermute x4, starting transfers between devices, by_heads(): lax.ppermute(out, both, [(target, source) for source, target in rounds[r]])  4.35 us
    pallas_call x3, Pallas kernels, attend(): pl.pallas_call(functools.partial(kernel, head=head, count=count), out_sha...  3.9 us
    ppermute x4, waiting for transfers between devices, by_heads(): lax.ppermute(out, both, [(target, source) for source, target in rounds[r]])  3.59 us
    pallas_call x1, Pallas kernels, stem(): pl.pallas_call(functools.partial(first_kernel, count=lax.axis_size('seq')...  3.51 us
    ppermute x1, starting transfers between devices, stem(): pair = lax.ppermute(to_pair, ('seq', 'batch'), swaps(0))  3.32 us
    pallas_call x1, Pallas kernels, stem(): pl.pallas_call(functools.partial(second_kernel, **fixed), out_shape=[shap...  2.49 us
  transfers between devices with their start and end apart: 14, of which 6 were waited for; matrix products, arithmetic and copies ran while one was open for 0% of the time, Pallas kernels for 10%

profile of v8, /device:TPU:1, one launch (start us, length us, event | category | flops | bytes accessed | tf_op | source)
XLA Modules:
  0.0 47.8 jit_solution(3708133159810905412)
XLA Ops:
  0.0 1.0 %edges.1 = (bf16[8,768]{1,0:T(8,128)(2,1)S(1)}, bf16[8,768]{1,0:T(8,128)(2,1)S(1)}) custom-call(bf16[256,1536]{1,0:T(8,128)(2,1)} %x_ref.1, bf16[5,1536,768]{2,1,0:T(8,128)(2,1)} %w1.1), custom_call_target="tpu_custom_call" | custom-call | tf_op jit(solution)/shard_map/edges/pallas_call | solution.py:153
  1.0 0.1 collective-permute-start
  1.1 3.3 %collective-permute-start.1 = (bf16[8,768]{1,0:T(8,128)(2,1)S(1)}, bf16[8,768]{1,0:T(8,128)(2,1)S(1)}, u32[]{:S(2)}, u32[]{:S(2)}) collective-permute-start(bf16[8,768]{1,0:T(8,128)(2,1)S(1)} %get-tuple-element.26), channel_id=1, source_target_pairs={{0,4},{1,5},{2,6},{3,7},{4,0},{5,1},{6,2},{7,3},{8,12},{9,13},{10,... | collective-permute-start | bytes 36872 | tf_op jit(solution)/shard_map/ppermute | solution.py:167
  4.5 1.1 %collective-permute-done.1.pair_ref = bf16[8,768]{1,0:T(8,128)(2,1)S(1)} collective-permute-done((bf16[8,768]{1,0:T(8,128)(2,1)S(1)}, bf16[8,768]{1,0:T(8,128)(2,1)S(1)}, u32[]{:S(2)}, u32[]{:S(2)}) %collective-permute-start.1) | collective-permute-done | bytes 12320 | tf_op jit(solution)/shard_map/ppermute | solution.py:167
  5.6 3.5 %first.1.first_ref = bf16[272,768]{1,0:T(8,128)(2,1)S(1)} custom-call(bf16[256,1536]{1,0:T(8,128)(2,1)S(1)} %copy-done.2, bf16[8,768]{1,0:T(8,128)(2,1)S(1)} %collective-permute-done.other_ref, bf16[8,768]{1,0:T(8,128)(2,1)S(1)} %collective-permute-done.1.pair_ref, bf16[5,1536,768]{2,1,0:T(8,128)(2,1)S(1)} %copy-done), custom_call_target="tpu_custom_call" | custom-call | tf_op jit(solution)/shard_map/first/pallas_call | solution.py:168
  9.1 0.0 copy-start.3
  9.1 2.5 %second.1 = (bf16[256,768]{1,0:T(8,128)(2,1)S(1)}, bf16[256,384]{1,0:T(8,128)(2,1)S(1)}) custom-call(bf16[272,768]{1,0:T(8,128)(2,1)S(1)} %first.1.first_ref, bf16[5,768,768]{2,1,0:T(8,128)(2,1)S(1)} %bitcast.1, bf16[768,1536]{1,0:T(8,128)(2,1)S(1)} %copy-done.1, f32[4]{0:T(128)S(1)} %copy-done.4), custom_call_target="tpu_custom_call" | custom-call | tf_op jit(solution)/shard_map/second/pallas_call | solution.py:181
  11.6 2.4 %collective-permute-start.2 = (bf16[256,384]{1,0:T(8,128)(2,1)S(1)}, bf16[256,384]{1,0:T(8,128)(2,1)S(1)}, u32[]{:S(2)}, u32[]{:S(2)}) collective-permute-start(bf16[256,384]{1,0:T(8,128)(2,1)S(1)} %get-tuple-element.28), channel_id=1, source_target_pairs={{0,25},{1,17},{2,27},{3,19},{4,29},{5,21},{6,31},{7,23},{8,24},{9,... | collective-permute-start | bytes 589832 | tf_op jit(solution)/shard_map/ppermute | solution.py:334
  14.1 1.4 %third.1 = (bf16[256,384]{1,0:T(8,128)(2,1)S(1)}, bf16[256,384]{1,0:T(8,128)(2,1)S(1)}, bf16[256,384]{1,0:T(8,128)(2,1)S(1)}) custom-call(bf16[256,768]{1,0:T(8,128)(2,1)S(1)} %get-tuple-element.27.hidden_ref, bf16[768,1536]{1,0:T(8,128)(2,1)S(1)} %copy-done.1, f32[4]{0:T(128)S(1)} %copy-done.4), custom_call_target="tpu_custom_call" | custom-call | tf_op jit(solution)/shard_map/third/pallas_call | solution.py:190
  15.5 3.4 %collective-permute-start.5 = (bf16[256,384]{1,0:T(8,128)(2,1)S(1)}, bf16[256,384]{1,0:T(8,128)(2,1)S(1)}, u32[]{:S(2)}, u32[]{:S(2)}) collective-permute-start(bf16[256,384]{1,0:T(8,128)(2,1)S(1)} %get-tuple-element.30), channel_id=1, source_target_pairs={{0,5},{1,13},{2,7},{3,15},{4,1},{5,9},{6,3},{7,11},{8,4},{9,12},{1... | collective-permute-start | bytes 589832 | tf_op jit(solution)/shard_map/ppermute | solution.py:334
  19.0 0.1 collective-permute-start.6
  19.0 1.1 %collective-permute-start.3 = (bf16[256,384]{1,0:T(8,128)(2,1)S(1)}, bf16[256,384]{1,0:T(8,128)(2,1)S(1)}, u32[]{:S(2)}, u32[]{:S(2)}) collective-permute-start(bf16[256,384]{1,0:T(8,128)(2,1)S(1)} %get-tuple-element.29), channel_id=1, source_target_pairs={{0,29},{1,21},{2,31},{3,23},{4,25},{5,17},{6,27},{7,19},{8,28},{9,... | collective-permute-start | bytes 589832 | tf_op jit(solution)/shard_map/ppermute | solution.py:334
  20.2 0.3 collective-permute-done.2.refs_0_.refs_2_
  20.4 4.8 %collective-permute-start.7 = (bf16[256,384]{1,0:T(8,128)(2,1)S(1)}, bf16[256,384]{1,0:T(8,128)(2,1)S(1)}, u32[]{:S(2)}, u32[]{:S(2)}) collective-permute-start(bf16[256,384]{1,0:T(8,128)(2,1)S(1)} %collective-permute-done.2.refs_0_.refs_2_), channel_id=1, source_target_pairs={{0,1},{1,0},{2,3},{3,2},{4,5},{5,4},{6,7},{7,6},{8,9},{9,8},{10,11... | collective-permute-start | bytes 589832 | tf_op jit(solution)/shard_map/ppermute | solution.py:336
  25.2 2.0 %collective-permute-start.9 = (bf16[256,384]{1,0:T(8,128)(2,1)S(1)}, bf16[256,384]{1,0:T(8,128)(2,1)S(1)}, u32[]{:S(2)}, u32[]{:S(2)}) collective-permute-start(bf16[256,384]{1,0:T(8,128)(2,1)S(1)} %collective-permute-done.5.refs_2_.refs_0_), channel_id=1, source_target_pairs={{0,1},{1,0},{2,3},{3,2},{4,5},{5,4},{6,7},{7,6},{8,9},{9,8},{10,11... | collective-permute-start | bytes 589832 | tf_op jit(solution)/shard_map/ppermute | solution.py:336
  27.2 0.0 collective-permute-done.6.refs_3_.refs_1_
  27.2 2.4 %collective-permute-start.8 = (bf16[256,384]{1,0:T(8,128)(2,1)S(1)}, bf16[256,384]{1,0:T(8,128)(2,1)S(1)}, u32[]{:S(2)}, u32[]{:S(2)}) collective-permute-start(bf16[256,384]{1,0:T(8,128)(2,1)S(1)} %collective-permute-done.6.refs_3_.refs_1_), channel_id=1, source_target_pairs={{0,1},{1,0},{2,3},{3,2},{4,5},{5,4},{6,7},{7,6},{8,9},{9,8},{10,11... | collective-permute-start | bytes 589832 | tf_op jit(solution)/shard_map/ppermute | solution.py:336
  29.7 5.1 %collective-permute-start.4 = (bf16[256,384]{1,0:T(8,128)(2,1)S(1)}, bf16[256,384]{1,0:T(8,128)(2,1)S(1)}, u32[]{:S(2)}, u32[]{:S(2)}) collective-permute-start(bf16[256,384]{1,0:T(8,128)(2,1)S(1)} %collective-permute-done.3.refs_1_.refs_3_), channel_id=1, source_target_pairs={{0,1},{1,0},{2,3},{3,2},{4,5},{5,4},{6,7},{7,6},{8,9},{9,8},{10,11... | collective-permute-start | bytes 589832 | tf_op jit(solution)/shard_map/ppermute | solution.py:336
  34.8 0.0 collective-permute-done.8.refs_5_.refs_6_
  34.8 1.7 %most.1 = (f32[512,128]{1,0:T(8,128)S(1)}, f32[512,128]{1,0:T(8,128)S(1)}, f32[512,128]{1,0:T(8,128)S(1)}) custom-call(bf16[256,384]{1,0:T(8,128)(2,1)S(1)} %collective-permute-done.2.refs_0_.refs_2_, bf16[256,384]{1,0:T(8,128)(2,1)S(1)} %collective-permute-done.3.refs_1_.refs_3_, bf16[256,384]{1,0:T(8,128)(2,1)S(1)} %collective-permute-done.5.refs_2_.refs_0_, ...), custom_call_target="tpu_custom_call" | custom-call | tf_op jit(solution)/shard_map/most/pallas_call | solution.py:256
  36.4 0.0 collective-permute-done.4.refs_2_.refs_5_
  36.4 0.5 %last.1 = (bf16[256,128]{1,0:T(8,128)(2,1)S(1)}, bf16[256,128]{1,0:T(8,128)(2,1)S(1)}) custom-call(bf16[256,384]{1,0:T(8,128)(2,1)S(1)} %collective-permute-done.2.refs_0_.refs_2_, bf16[256,384]{1,0:T(8,128)(2,1)S(1)} %collective-permute-done.3.refs_1_.refs_3_, bf16[256,384]{1,0:T(8,128)(2,1)S(1)} %collective-permute-done.4.refs_2_.refs_5_, ...), custom_call_target="tpu_custom_call" | custom-call | tf_op jit(solution)/shard_map/last/pallas_call | solution.py:256
  36.9 2.2 %collective-permute-start.10 = (bf16[256,128]{1,0:T(8,128)(2,1)S(1)}, bf16[256,128]{1,0:T(8,128)(2,1)S(1)}, u32[]{:S(2)}, u32[]{:S(2)}) collective-permute-start(bf16[256,128]{1,0:T(8,128)(2,1)S(1)} %get-tuple-element.37), channel_id=1, source_target_pairs={{25,0},{17,1},{27,2},{19,3},{29,4},{21,5},{31,6},{23,7},{24,8},{16... | collective-permute-start | bytes 196616 | tf_op jit(solution)/shard_map/ppermute | solution.py:338
  39.1 0.2 collective-permute-start.11
  39.3 1.7 %near.1 = (bf16[256,128]{1,0:T(8,128)(2,1)S(1)}, bf16[256,128]{1,0:T(8,128)(2,1)S(1)}) custom-call(bf16[256,384]{1,0:T(8,128)(2,1)S(1)} %collective-permute-done.5.refs_2_.refs_0_, bf16[256,384]{1,0:T(8,128)(2,1)S(1)} %collective-permute-done.6.refs_3_.refs_1_, bf16[256,384]{1,0:T(8,128)(2,1)S(1)} %collective-permute-done.2.refs_0_.refs_2_, ...), custom_call_target="tpu_custom_call" | custom-call | tf_op jit(solution)/shard_map/near/pallas_call | solution.py:256
  41.1 0.9 %collective-permute-start.12 = (bf16[256,128]{1,0:T(8,128)(2,1)S(1)}, bf16[256,128]{1,0:T(8,128)(2,1)S(1)}, u32[]{:S(2)}, u32[]{:S(2)}) collective-permute-start(bf16[256,128]{1,0:T(8,128)(2,1)S(1)} %get-tuple-element.43), channel_id=1, source_target_pairs={{5,0},{13,1},{7,2},{15,3},{1,4},{9,5},{3,6},{11,7},{4,8},{12,9},{6... | collective-permute-start | bytes 196616 | tf_op jit(solution)/shard_map/ppermute | solution.py:338
  42.0 1.1 %collective-permute-start.13 = (bf16[256,128]{1,0:T(8,128)(2,1)S(1)}, bf16[256,128]{1,0:T(8,128)(2,1)S(1)}, u32[]{:S(2)}, u32[]{:S(2)}) collective-permute-start(bf16[256,128]{1,0:T(8,128)(2,1)S(1)} %get-tuple-element.44), channel_id=1, source_target_pairs={{1,0},{9,1},{3,2},{11,3},{5,4},{13,5},{7,6},{15,7},{0,8},{8,9},{2,... | collective-permute-start | bytes 196616 | tf_op jit(solution)/shard_map/ppermute | solution.py:338
  43.0 1.7 %collective-permute-done.10.rest_0_ = bf16[256,128]{1,0:T(8,128)(2,1)S(1)} collective-permute-done((bf16[256,128]{1,0:T(8,128)(2,1)S(1)}, bf16[256,128]{1,0:T(8,128)(2,1)S(1)}, u32[]{:S(2)}, u32[]{:S(2)}) %collective-permute-start.10) | collective-permute-done | bytes 65568 | tf_op jit(solution)/shard_map/ppermute | solution.py:338
  44.7 1.2 %collective-permute-done.11.rest_1_ = bf16[256,128]{1,0:T(8,128)(2,1)S(1)} collective-permute-done((bf16[256,128]{1,0:T(8,128)(2,1)S(1)}, bf16[256,128]{1,0:T(8,128)(2,1)S(1)}, u32[]{:S(2)}, u32[]{:S(2)}) %collective-permute-start.11) | collective-permute-done | bytes 65568 | tf_op jit(solution)/shard_map/ppermute | solution.py:338
  45.9 0.2 collective-permute-done.12.rest_2_
  46.2 0.4 collective-permute-done.13.rest_3_
  46.6 1.1 %finish.1 = bf16[256,768]{1,0:T(8,128)(2,1)} custom-call(bf16[256,768]{1,0:T(8,128)(2,1)S(1)} %get-tuple-element.27.hidden_ref, bf16[512,768]{1,0:T(8,128)(2,1)S(1)} %copy-done.3, bf16[256,128]{1,0:T(8,128)(2,1)S(1)} %collective-permute-done.10.rest_0_, bf16[256,128]{1,0:T(8,128)(2,1)S(1)} %collective-permute-done.11.rest_1_, ...), custom_call_target="tpu_custom_call" | custom-call | tf_op jit(solution)/shard_map/finish/pallas_call | solution.py:298
  (19 shorter events, 0.0 us)
Async XLA Ops:
  0.0 5.6 %copy-start = (bf16[5,1536,768]{2,1,0:T(8,128)(2,1)S(1)}, bf16[5,1536,768]{2,1,0:T(8,128)(2,1)}, u32[]{:S(2)}) copy-start(bf16[5,1536,768]{2,1,0:T(8,128)(2,1)} %w1.1) | copy-start | bytes 35389444
  0.0 5.6 %copy-start.2 = (bf16[256,1536]{1,0:T(8,128)(2,1)S(1)}, bf16[256,1536]{1,0:T(8,128)(2,1)}, u32[]{:S(2)}) copy-start(bf16[256,1536]{1,0:T(8,128)(2,1)} %x_ref.1) | copy-start | bytes 2359300
  1.0 3.5 %collective-permute-start = (bf16[8,768]{1,0:T(8,128)(2,1)S(1)}, bf16[8,768]{1,0:T(8,128)(2,1)S(1)}, u32[]{:S(2)}, u32[]{:S(2)}) collective-permute-start(bf16[8,768]{1,0:T(8,128)(2,1)S(1)} %get-tuple-element.25), channel_id=1, source_target_pairs={{0,1},{1,0},{2,3},{3,2},{4,8},{5,9},{6,10},{7,11},{8,4},{9,5},{10,... | collective-permute-start | bytes 36872 | tf_op jit(solution)/shard_map/ppermute | solution.py:166
  1.1 7.9 %slice-start = ((s8[5898240]{0:T(1024)(128)(4,1)}), s8[4194304]{0:T(1024)(128)(4,1)S(1)}, s32[]{:S(2)}) async-start(s8[5898240]{0:T(1024)(128)(4,1)} %bitcast), calls=%async_computation | async-start | bytes 8388608
  1.1 7.9 %copy-start.1 = (bf16[768,1536]{1,0:T(8,128)(2,1)S(1)}, bf16[768,1536]{1,0:T(8,128)(2,1)}, u32[]{:S(2)}) copy-start(bf16[768,1536]{1,0:T(8,128)(2,1)} %wqkv.3) | copy-start | bytes 7077892
  1.1 8.0 %slice-start.1 = ((s8[5898240]{0:T(1024)(128)(4,1)}), s8[1703936]{0:T(1024)(128)(4,1)S(1)}, s32[]{:S(2)}) async-start(s8[5898240]{0:T(1024)(128)(4,1)} %bitcast), calls=%async_computation.1 | async-start | bytes 3407872
  1.1 8.0 %copy-start.4 = (f32[4]{0:T(128)S(1)}, f32[4]{0:T(128)}, u32[]{:S(2)}) copy-start(f32[4]{0:T(128)} %scale_hbm.3) | copy-start | bytes 52
  1.1 4.4 %collective-permute-start.1 = (bf16[8,768]{1,0:T(8,128)(2,1)S(1)}, bf16[8,768]{1,0:T(8,128)(2,1)S(1)}, u32[]{:S(2)}, u32[]{:S(2)}) collective-permute-start(bf16[8,768]{1,0:T(8,128)(2,1)S(1)} %get-tuple-element.26), channel_id=1, source_target_pairs={{0,4},{1,5},{2,6},{3,7},{4,0},{5,1},{6,2},{7,3},{8,12},{9,13},{10,... | collective-permute-start | bytes 36872 | tf_op jit(solution)/shard_map/ppermute | solution.py:167
  9.1 37.5 %copy-start.3 = (bf16[512,768]{1,0:T(8,128)(2,1)S(1)}, bf16[512,768]{1,0:T(8,128)(2,1)}, u32[]{:S(2)}) copy-start(bf16[512,768]{1,0:T(8,128)(2,1)} %weight_ref.1) | copy-start | bytes 2359300
  11.6 8.8 %collective-permute-start.2 = (bf16[256,384]{1,0:T(8,128)(2,1)S(1)}, bf16[256,384]{1,0:T(8,128)(2,1)S(1)}, u32[]{:S(2)}, u32[]{:S(2)}) collective-permute-start(bf16[256,384]{1,0:T(8,128)(2,1)S(1)} %get-tuple-element.28), channel_id=1, source_target_pairs={{0,25},{1,17},{2,27},{3,19},{4,29},{5,21},{6,31},{7,23},{8,24},{9,... | collective-permute-start | bytes 589832 | tf_op jit(solution)/shard_map/ppermute | solution.py:334
  15.5 9.7 %collective-permute-start.5 = (bf16[256,384]{1,0:T(8,128)(2,1)S(1)}, bf16[256,384]{1,0:T(8,128)(2,1)S(1)}, u32[]{:S(2)}, u32[]{:S(2)}) collective-permute-start(bf16[256,384]{1,0:T(8,128)(2,1)S(1)} %get-tuple-element.30), channel_id=1, source_target_pairs={{0,5},{1,13},{2,7},{3,15},{4,1},{5,9},{6,3},{7,11},{8,4},{9,12},{1... | collective-permute-start | bytes 589832 | tf_op jit(solution)/shard_map/ppermute | solution.py:334
  19.0 8.3 %collective-permute-start.6 = (bf16[256,384]{1,0:T(8,128)(2,1)S(1)}, bf16[256,384]{1,0:T(8,128)(2,1)S(1)}, u32[]{:S(2)}, u32[]{:S(2)}) collective-permute-start(bf16[256,384]{1,0:T(8,128)(2,1)S(1)} %get-tuple-element.31), channel_id=1, source_target_pairs={{0,1},{1,9},{2,3},{3,11},{4,5},{5,13},{6,7},{7,15},{8,0},{9,8},{10... | collective-permute-start | bytes 589832 | tf_op jit(solution)/shard_map/ppermute | solution.py:334
  19.0 10.6 %collective-permute-start.3 = (bf16[256,384]{1,0:T(8,128)(2,1)S(1)}, bf16[256,384]{1,0:T(8,128)(2,1)S(1)}, u32[]{:S(2)}, u32[]{:S(2)}) collective-permute-start(bf16[256,384]{1,0:T(8,128)(2,1)S(1)} %get-tuple-element.29), channel_id=1, source_target_pairs={{0,29},{1,21},{2,31},{3,23},{4,25},{5,17},{6,27},{7,19},{8,28},{9,... | collective-permute-start | bytes 589832 | tf_op jit(solution)/shard_map/ppermute | solution.py:334
  20.4 14.3 %collective-permute-start.7 = (bf16[256,384]{1,0:T(8,128)(2,1)S(1)}, bf16[256,384]{1,0:T(8,128)(2,1)S(1)}, u32[]{:S(2)}, u32[]{:S(2)}) collective-permute-start(bf16[256,384]{1,0:T(8,128)(2,1)S(1)} %collective-permute-done.2.refs_0_.refs_2_), channel_id=1, source_target_pairs={{0,1},{1,0},{2,3},{3,2},{4,5},{5,4},{6,7},{7,6},{8,9},{9,8},{10,11... | collective-permute-start | bytes 589832 | tf_op jit(solution)/shard_map/ppermute | solution.py:336
  25.2 9.5 %collective-permute-start.9 = (bf16[256,384]{1,0:T(8,128)(2,1)S(1)}, bf16[256,384]{1,0:T(8,128)(2,1)S(1)}, u32[]{:S(2)}, u32[]{:S(2)}) collective-permute-start(bf16[256,384]{1,0:T(8,128)(2,1)S(1)} %collective-permute-done.5.refs_2_.refs_0_), channel_id=1, source_target_pairs={{0,1},{1,0},{2,3},{3,2},{4,5},{5,4},{6,7},{7,6},{8,9},{9,8},{10,11... | collective-permute-start | bytes 589832 | tf_op jit(solution)/shard_map/ppermute | solution.py:336
  27.2 7.5 %collective-permute-start.8 = (bf16[256,384]{1,0:T(8,128)(2,1)S(1)}, bf16[256,384]{1,0:T(8,128)(2,1)S(1)}, u32[]{:S(2)}, u32[]{:S(2)}) collective-permute-start(bf16[256,384]{1,0:T(8,128)(2,1)S(1)} %collective-permute-done.6.refs_3_.refs_1_), channel_id=1, source_target_pairs={{0,1},{1,0},{2,3},{3,2},{4,5},{5,4},{6,7},{7,6},{8,9},{9,8},{10,11... | collective-permute-start | bytes 589832 | tf_op jit(solution)/shard_map/ppermute | solution.py:336
  29.7 6.7 %collective-permute-start.4 = (bf16[256,384]{1,0:T(8,128)(2,1)S(1)}, bf16[256,384]{1,0:T(8,128)(2,1)S(1)}, u32[]{:S(2)}, u32[]{:S(2)}) collective-permute-start(bf16[256,384]{1,0:T(8,128)(2,1)S(1)} %collective-permute-done.3.refs_1_.refs_3_), channel_id=1, source_target_pairs={{0,1},{1,0},{2,3},{3,2},{4,5},{5,4},{6,7},{7,6},{8,9},{9,8},{10,11... | collective-permute-start | bytes 589832 | tf_op jit(solution)/shard_map/ppermute | solution.py:336
  36.9 7.8 %collective-permute-start.10 = (bf16[256,128]{1,0:T(8,128)(2,1)S(1)}, bf16[256,128]{1,0:T(8,128)(2,1)S(1)}, u32[]{:S(2)}, u32[]{:S(2)}) collective-permute-start(bf16[256,128]{1,0:T(8,128)(2,1)S(1)} %get-tuple-element.37), channel_id=1, source_target_pairs={{25,0},{17,1},{27,2},{19,3},{29,4},{21,5},{31,6},{23,7},{24,8},{16... | collective-permute-start | bytes 196616 | tf_op jit(solution)/shard_map/ppermute | solution.py:338
  39.1 6.9 %collective-permute-start.11 = (bf16[256,128]{1,0:T(8,128)(2,1)S(1)}, bf16[256,128]{1,0:T(8,128)(2,1)S(1)}, u32[]{:S(2)}, u32[]{:S(2)}) collective-permute-start(bf16[256,128]{1,0:T(8,128)(2,1)S(1)} %get-tuple-element.38), channel_id=1, source_target_pairs={{29,0},{21,1},{31,2},{23,3},{25,4},{17,5},{27,6},{19,7},{28,8},{20... | collective-permute-start | bytes 196616 | tf_op jit(solution)/shard_map/ppermute | solution.py:338
  41.1 5.1 %collective-permute-start.12 = (bf16[256,128]{1,0:T(8,128)(2,1)S(1)}, bf16[256,128]{1,0:T(8,128)(2,1)S(1)}, u32[]{:S(2)}, u32[]{:S(2)}) collective-permute-start(bf16[256,128]{1,0:T(8,128)(2,1)S(1)} %get-tuple-element.43), channel_id=1, source_target_pairs={{5,0},{13,1},{7,2},{15,3},{1,4},{9,5},{3,6},{11,7},{4,8},{12,9},{6... | collective-permute-start | bytes 196616 | tf_op jit(solution)/shard_map/ppermute | solution.py:338
  42.0 4.6 %collective-permute-start.13 = (bf16[256,128]{1,0:T(8,128)(2,1)S(1)}, bf16[256,128]{1,0:T(8,128)(2,1)S(1)}, u32[]{:S(2)}, u32[]{:S(2)}) collective-permute-start(bf16[256,128]{1,0:T(8,128)(2,1)S(1)} %get-tuple-element.44), channel_id=1, source_target_pairs={{1,0},{9,1},{3,2},{11,3},{5,4},{13,5},{7,6},{15,7},{0,8},{8,9},{2,... | collective-permute-start | bytes 196616 | tf_op jit(solution)/shard_map/ppermute | solution.py:338

commit v9 on v8

--- a/solution.py
+++ b/solution.py
@@ -84,13 +84,17 @@
     scale_copy = pltpu.make_async_copy(scale_hbm, scale_ref, sem)
     scale_copy.start()
     rows = hidden_ref.shape[0]
-    for j in range(TAPS):
-        product = rolled(jnp.dot(first_ref[...], w2[j], preferred_element_type=F32), j)
-        if j == 0:
-            total[...] = product
-        else:
-            total[...] += product
-    hidden_ref[...] = (first_ref[0:rows].astype(F32) + total[0:rows]).astype(BF16)
+    width = total.shape[1]
+    for n in range(0, width, width // 3):
+        part = slice(n, n + width // 3)
+        for j in range(TAPS):
+            product = jnp.dot(first_ref[...], w2[j, :, part], preferred_element_type=F32)
+            if j == 0:
+                total[:, part] = rolled(product, j)
+            else:
+                total[:, part] += rolled(product, j)
+        hidden = first_ref[0:rows, part].astype(F32) + total[0:rows, part]
+        hidden_ref[:, part] = hidden.astype(BF16)
     scale_copy.wait()
     g = lax.axis_index("seq")
     project(hidden_ref, wqkv, scale_ref, units, g, range(len(units)), heads, head, spread)

time: 47.9 us -> 48.1 us (level)
  no operation moved by 1% of the time
where the time goes in v9:
time: 48.1 us; the launch traced here: 47.7 us
  starting transfers between devices  29.2 us (61%)
  Pallas kernels  13.4 us (28%)
  waiting for transfers between devices  4.97 us (10%)
    ppermute x4, starting transfers between devices, by_heads(): lax.ppermute(unit, 'batch', cores)  14.3 us
    ppermute x4, starting transfers between devices, by_heads(): lax.ppermute(unit, both, pairs)  7.11 us
    ppermute x4, starting transfers between devices, by_heads(): lax.ppermute(out, both, [(target, source) for source, target in rounds[r]])  4.34 us
    pallas_call x3, Pallas kernels, attend(): pl.pallas_call(functools.partial(kernel, head=head, count=count), out_sha...  3.91 us
    ppermute x4, waiting for transfers between devices, by_heads(): lax.ppermute(out, both, [(target, source) for source, target in rounds[r]])  3.6 us
    pallas_call x1, Pallas kernels, stem(): pl.pallas_call(functools.partial(first_kernel, count=lax.axis_size('seq')...  3.51 us
    ppermute x1, starting transfers between devices, stem(): pair = lax.ppermute(to_pair, ('seq', 'batch'), swaps(0))  3.32 us
    pallas_call x1, Pallas kernels, stem(): pl.pallas_call(functools.partial(second_kernel, **fixed), out_shape=[shap...  2.45 us
  transfers between devices with their start and end apart: 14, of which 6 were waited for; matrix products, arithmetic and copies ran while one was open for 0% of the time, Pallas kernels for 10%

profile of v9, /device:TPU:1, one launch (start us, length us, event | category | flops | bytes accessed | tf_op | source)
XLA Modules:
  0.0 47.7 jit_solution(510997046523990568)
XLA Ops:
  0.0 1.0 %edges.1 = (bf16[8,768]{1,0:T(8,128)(2,1)S(1)}, bf16[8,768]{1,0:T(8,128)(2,1)S(1)}) custom-call(bf16[256,1536]{1,0:T(8,128)(2,1)} %x_ref.1, bf16[5,1536,768]{2,1,0:T(8,128)(2,1)} %w1.1), custom_call_target="tpu_custom_call" | custom-call | tf_op jit(solution)/shard_map/edges/pallas_call | solution.py:157
  1.0 0.1 collective-permute-start
  1.1 3.3 %collective-permute-start.1 = (bf16[8,768]{1,0:T(8,128)(2,1)S(1)}, bf16[8,768]{1,0:T(8,128)(2,1)S(1)}, u32[]{:S(2)}, u32[]{:S(2)}) collective-permute-start(bf16[8,768]{1,0:T(8,128)(2,1)S(1)} %get-tuple-element.26), channel_id=1, source_target_pairs={{0,4},{1,5},{2,6},{3,7},{4,0},{5,1},{6,2},{7,3},{8,12},{9,13},{10,... | collective-permute-start | bytes 36872 | tf_op jit(solution)/shard_map/ppermute | solution.py:171
  4.5 1.1 %collective-permute-done.1.pair_ref = bf16[8,768]{1,0:T(8,128)(2,1)S(1)} collective-permute-done((bf16[8,768]{1,0:T(8,128)(2,1)S(1)}, bf16[8,768]{1,0:T(8,128)(2,1)S(1)}, u32[]{:S(2)}, u32[]{:S(2)}) %collective-permute-start.1) | collective-permute-done | bytes 12320 | tf_op jit(solution)/shard_map/ppermute | solution.py:171
  5.6 3.5 %first.1.first_ref = bf16[272,768]{1,0:T(8,128)(2,1)S(1)} custom-call(bf16[256,1536]{1,0:T(8,128)(2,1)S(1)} %copy-done.2, bf16[8,768]{1,0:T(8,128)(2,1)S(1)} %collective-permute-done.other_ref, bf16[8,768]{1,0:T(8,128)(2,1)S(1)} %collective-permute-done.1.pair_ref, bf16[5,1536,768]{2,1,0:T(8,128)(2,1)S(1)} %copy-done), custom_call_target="tpu_custom_call" | custom-call | tf_op jit(solution)/shard_map/first/pallas_call | solution.py:172
  9.1 0.0 copy-start.3
  9.1 2.5 %second.1 = (bf16[256,768]{1,0:T(8,128)(2,1)S(1)}, bf16[256,384]{1,0:T(8,128)(2,1)S(1)}) custom-call(bf16[272,768]{1,0:T(8,128)(2,1)S(1)} %first.1.first_ref, bf16[5,768,768]{2,1,0:T(8,128)(2,1)S(1)} %bitcast.1, bf16[768,1536]{1,0:T(8,128)(2,1)S(1)} %copy-done.1, f32[4]{0:T(128)S(1)} %copy-done.4), custom_call_target="tpu_custom_call" | custom-call | tf_op jit(solution)/shard_map/second/pallas_call | solution.py:185
  11.6 2.4 %collective-permute-start.2 = (bf16[256,384]{1,0:T(8,128)(2,1)S(1)}, bf16[256,384]{1,0:T(8,128)(2,1)S(1)}, u32[]{:S(2)}, u32[]{:S(2)}) collective-permute-start(bf16[256,384]{1,0:T(8,128)(2,1)S(1)} %get-tuple-element.28), channel_id=1, source_target_pairs={{0,25},{1,17},{2,27},{3,19},{4,29},{5,21},{6,31},{7,23},{8,24},{9,... | collective-permute-start | bytes 589832 | tf_op jit(solution)/shard_map/ppermute | solution.py:338
  14.0 1.4 %third.1 = (bf16[256,384]{1,0:T(8,128)(2,1)S(1)}, bf16[256,384]{1,0:T(8,128)(2,1)S(1)}, bf16[256,384]{1,0:T(8,128)(2,1)S(1)}) custom-call(bf16[256,768]{1,0:T(8,128)(2,1)S(1)} %get-tuple-element.27.hidden_ref, bf16[768,1536]{1,0:T(8,128)(2,1)S(1)} %copy-done.1, f32[4]{0:T(128)S(1)} %copy-done.4), custom_call_target="tpu_custom_call" | custom-call | tf_op jit(solution)/shard_map/third/pallas_call | solution.py:194
  15.5 3.4 %collective-permute-start.5 = (bf16[256,384]{1,0:T(8,128)(2,1)S(1)}, bf16[256,384]{1,0:T(8,128)(2,1)S(1)}, u32[]{:S(2)}, u32[]{:S(2)}) collective-permute-start(bf16[256,384]{1,0:T(8,128)(2,1)S(1)} %get-tuple-element.30), channel_id=1, source_target_pairs={{0,5},{1,13},{2,7},{3,15},{4,1},{5,9},{6,3},{7,11},{8,4},{9,12},{1... | collective-permute-start | bytes 589832 | tf_op jit(solution)/shard_map/ppermute | solution.py:338
  18.9 0.1 collective-permute-start.6
  19.0 1.1 %collective-permute-start.3 = (bf16[256,384]{1,0:T(8,128)(2,1)S(1)}, bf16[256,384]{1,0:T(8,128)(2,1)S(1)}, u32[]{:S(2)}, u32[]{:S(2)}) collective-permute-start(bf16[256,384]{1,0:T(8,128)(2,1)S(1)} %get-tuple-element.29), channel_id=1, source_target_pairs={{0,29},{1,21},{2,31},{3,23},{4,25},{5,17},{6,27},{7,19},{8,28},{9,... | collective-permute-start | bytes 589832 | tf_op jit(solution)/shard_map/ppermute | solution.py:338
  20.1 0.3 collective-permute-done.2.refs_0_.refs_2_
  20.4 4.8 %collective-permute-start.7 = (bf16[256,384]{1,0:T(8,128)(2,1)S(1)}, bf16[256,384]{1,0:T(8,128)(2,1)S(1)}, u32[]{:S(2)}, u32[]{:S(2)}) collective-permute-start(bf16[256,384]{1,0:T(8,128)(2,1)S(1)} %collective-permute-done.2.refs_0_.refs_2_), channel_id=1, source_target_pairs={{0,1},{1,0},{2,3},{3,2},{4,5},{5,4},{6,7},{7,6},{8,9},{9,8},{10,11... | collective-permute-start | bytes 589832 | tf_op jit(solution)/shard_map/ppermute | solution.py:340
  25.2 0.0 collective-permute-done.5.refs_2_.refs_0_
  25.2 2.0 %collective-permute-start.9 = (bf16[256,384]{1,0:T(8,128)(2,1)S(1)}, bf16[256,384]{1,0:T(8,128)(2,1)S(1)}, u32[]{:S(2)}, u32[]{:S(2)}) collective-permute-start(bf16[256,384]{1,0:T(8,128)(2,1)S(1)} %collective-permute-done.5.refs_2_.refs_0_), channel_id=1, source_target_pairs={{0,1},{1,0},{2,3},{3,2},{4,5},{5,4},{6,7},{7,6},{8,9},{9,8},{10,11... | collective-permute-start | bytes 589832 | tf_op jit(solution)/shard_map/ppermute | solution.py:340
  27.2 0.0 collective-permute-done.6.refs_3_.refs_1_
  27.2 2.4 %collective-permute-start.8 = (bf16[256,384]{1,0:T(8,128)(2,1)S(1)}, bf16[256,384]{1,0:T(8,128)(2,1)S(1)}, u32[]{:S(2)}, u32[]{:S(2)}) collective-permute-start(bf16[256,384]{1,0:T(8,128)(2,1)S(1)} %collective-permute-done.6.refs_3_.refs_1_), channel_id=1, source_target_pairs={{0,1},{1,0},{2,3},{3,2},{4,5},{5,4},{6,7},{7,6},{8,9},{9,8},{10,11... | collective-permute-start | bytes 589832 | tf_op jit(solution)/shard_map/ppermute | solution.py:340
  29.6 0.0 collective-permute-done.3.refs_1_.refs_3_
  29.7 5.1 %collective-permute-start.4 = (bf16[256,384]{1,0:T(8,128)(2,1)S(1)}, bf16[256,384]{1,0:T(8,128)(2,1)S(1)}, u32[]{:S(2)}, u32[]{:S(2)}) collective-permute-start(bf16[256,384]{1,0:T(8,128)(2,1)S(1)} %collective-permute-done.3.refs_1_.refs_3_), channel_id=1, source_target_pairs={{0,1},{1,0},{2,3},{3,2},{4,5},{5,4},{6,7},{7,6},{8,9},{9,8},{10,11... | collective-permute-start | bytes 589832 | tf_op jit(solution)/shard_map/ppermute | solution.py:340
  34.7 1.7 %most.1 = (f32[512,128]{1,0:T(8,128)S(1)}, f32[512,128]{1,0:T(8,128)S(1)}, f32[512,128]{1,0:T(8,128)S(1)}) custom-call(bf16[256,384]{1,0:T(8,128)(2,1)S(1)} %collective-permute-done.2.refs_0_.refs_2_, bf16[256,384]{1,0:T(8,128)(2,1)S(1)} %collective-permute-done.3.refs_1_.refs_3_, bf16[256,384]{1,0:T(8,128)(2,1)S(1)} %collective-permute-done.5.refs_2_.refs_0_, ...), custom_call_target="tpu_custom_call" | custom-call | tf_op jit(solution)/shard_map/most/pallas_call | solution.py:260
  36.4 0.5 %last.1 = (bf16[256,128]{1,0:T(8,128)(2,1)S(1)}, bf16[256,128]{1,0:T(8,128)(2,1)S(1)}) custom-call(bf16[256,384]{1,0:T(8,128)(2,1)S(1)} %collective-permute-done.2.refs_0_.refs_2_, bf16[256,384]{1,0:T(8,128)(2,1)S(1)} %collective-permute-done.3.refs_1_.refs_3_, bf16[256,384]{1,0:T(8,128)(2,1)S(1)} %collective-permute-done.4.refs_2_.refs_5_, ...), custom_call_target="tpu_custom_call" | custom-call | tf_op jit(solution)/shard_map/last/pallas_call | solution.py:260
  36.9 2.1 %collective-permute-start.10 = (bf16[256,128]{1,0:T(8,128)(2,1)S(1)}, bf16[256,128]{1,0:T(8,128)(2,1)S(1)}, u32[]{:S(2)}, u32[]{:S(2)}) collective-permute-start(bf16[256,128]{1,0:T(8,128)(2,1)S(1)} %get-tuple-element.37), channel_id=1, source_target_pairs={{25,0},{17,1},{27,2},{19,3},{29,4},{21,5},{31,6},{23,7},{24,8},{16... | collective-permute-start | bytes 196616 | tf_op jit(solution)/shard_map/ppermute | solution.py:342
  39.1 0.2 collective-permute-start.11
  39.3 1.7 %near.1 = (bf16[256,128]{1,0:T(8,128)(2,1)S(1)}, bf16[256,128]{1,0:T(8,128)(2,1)S(1)}) custom-call(bf16[256,384]{1,0:T(8,128)(2,1)S(1)} %collective-permute-done.5.refs_2_.refs_0_, bf16[256,384]{1,0:T(8,128)(2,1)S(1)} %collective-permute-done.6.refs_3_.refs_1_, bf16[256,384]{1,0:T(8,128)(2,1)S(1)} %collective-permute-done.2.refs_0_.refs_2_, ...), custom_call_target="tpu_custom_call" | custom-call | tf_op jit(solution)/shard_map/near/pallas_call | solution.py:260
  41.0 0.9 %collective-permute-start.12 = (bf16[256,128]{1,0:T(8,128)(2,1)S(1)}, bf16[256,128]{1,0:T(8,128)(2,1)S(1)}, u32[]{:S(2)}, u32[]{:S(2)}) collective-permute-start(bf16[256,128]{1,0:T(8,128)(2,1)S(1)} %get-tuple-element.43), channel_id=1, source_target_pairs={{5,0},{13,1},{7,2},{15,3},{1,4},{9,5},{3,6},{11,7},{4,8},{12,9},{6... | collective-permute-start | bytes 196616 | tf_op jit(solution)/shard_map/ppermute | solution.py:342
  42.0 1.1 %collective-permute-start.13 = (bf16[256,128]{1,0:T(8,128)(2,1)S(1)}, bf16[256,128]{1,0:T(8,128)(2,1)S(1)}, u32[]{:S(2)}, u32[]{:S(2)}) collective-permute-start(bf16[256,128]{1,0:T(8,128)(2,1)S(1)} %get-tuple-element.44), channel_id=1, source_target_pairs={{1,0},{9,1},{3,2},{11,3},{5,4},{13,5},{7,6},{15,7},{0,8},{8,9},{2,... | collective-permute-start | bytes 196616 | tf_op jit(solution)/shard_map/ppermute | solution.py:342
  43.0 1.7 %collective-permute-done.10.rest_0_ = bf16[256,128]{1,0:T(8,128)(2,1)S(1)} collective-permute-done((bf16[256,128]{1,0:T(8,128)(2,1)S(1)}, bf16[256,128]{1,0:T(8,128)(2,1)S(1)}, u32[]{:S(2)}, u32[]{:S(2)}) %collective-permute-start.10) | collective-permute-done | bytes 65568 | tf_op jit(solution)/shard_map/ppermute | solution.py:342
  44.7 1.2 %collective-permute-done.11.rest_1_ = bf16[256,128]{1,0:T(8,128)(2,1)S(1)} collective-permute-done((bf16[256,128]{1,0:T(8,128)(2,1)S(1)}, bf16[256,128]{1,0:T(8,128)(2,1)S(1)}, u32[]{:S(2)}, u32[]{:S(2)}) %collective-permute-start.11) | collective-permute-done | bytes 65568 | tf_op jit(solution)/shard_map/ppermute | solution.py:342
  45.9 0.2 collective-permute-done.12.rest_2_
  46.2 0.5 collective-permute-done.13.rest_3_
  46.6 1.1 %finish.1 = bf16[256,768]{1,0:T(8,128)(2,1)} custom-call(bf16[256,768]{1,0:T(8,128)(2,1)S(1)} %get-tuple-element.27.hidden_ref, bf16[512,768]{1,0:T(8,128)(2,1)S(1)} %copy-done.3, bf16[256,128]{1,0:T(8,128)(2,1)S(1)} %collective-permute-done.10.rest_0_, bf16[256,128]{1,0:T(8,128)(2,1)S(1)} %collective-permute-done.11.rest_1_, ...), custom_call_target="tpu_custom_call" | custom-call | tf_op jit(solution)/shard_map/finish/pallas_call | solution.py:302
  (19 shorter events, 0.0 us)
Async XLA Ops:
  0.0 5.6 %copy-start = (bf16[5,1536,768]{2,1,0:T(8,128)(2,1)S(1)}, bf16[5,1536,768]{2,1,0:T(8,128)(2,1)}, u32[]{:S(2)}) copy-start(bf16[5,1536,768]{2,1,0:T(8,128)(2,1)} %w1.1) | copy-start | bytes 35389444
  0.0 5.6 %copy-start.2 = (bf16[256,1536]{1,0:T(8,128)(2,1)S(1)}, bf16[256,1536]{1,0:T(8,128)(2,1)}, u32[]{:S(2)}) copy-start(bf16[256,1536]{1,0:T(8,128)(2,1)} %x_ref.1) | copy-start | bytes 2359300
  1.0 3.5 %collective-permute-start = (bf16[8,768]{1,0:T(8,128)(2,1)S(1)}, bf16[8,768]{1,0:T(8,128)(2,1)S(1)}, u32[]{:S(2)}, u32[]{:S(2)}) collective-permute-start(bf16[8,768]{1,0:T(8,128)(2,1)S(1)} %get-tuple-element.25), channel_id=1, source_target_pairs={{0,1},{1,0},{2,3},{3,2},{4,8},{5,9},{6,10},{7,11},{8,4},{9,5},{10,... | collective-permute-start | bytes 36872 | tf_op jit(solution)/shard_map/ppermute | solution.py:170
  1.1 7.9 %slice-start = ((s8[5898240]{0:T(1024)(128)(4,1)}), s8[4194304]{0:T(1024)(128)(4,1)S(1)}, s32[]{:S(2)}) async-start(s8[5898240]{0:T(1024)(128)(4,1)} %bitcast), calls=%async_computation | async-start | bytes 8388608
  1.1 7.9 %copy-start.1 = (bf16[768,1536]{1,0:T(8,128)(2,1)S(1)}, bf16[768,1536]{1,0:T(8,128)(2,1)}, u32[]{:S(2)}) copy-start(bf16[768,1536]{1,0:T(8,128)(2,1)} %wqkv.3) | copy-start | bytes 7077892
  1.1 8.0 %slice-start.1 = ((s8[5898240]{0:T(1024)(128)(4,1)}), s8[1703936]{0:T(1024)(128)(4,1)S(1)}, s32[]{:S(2)}) async-start(s8[5898240]{0:T(1024)(128)(4,1)} %bitcast), calls=%async_computation.1 | async-start | bytes 3407872
  1.1 8.0 %copy-start.4 = (f32[4]{0:T(128)S(1)}, f32[4]{0:T(128)}, u32[]{:S(2)}) copy-start(f32[4]{0:T(128)} %scale_hbm.3) | copy-start | bytes 52
  1.1 4.4 %collective-permute-start.1 = (bf16[8,768]{1,0:T(8,128)(2,1)S(1)}, bf16[8,768]{1,0:T(8,128)(2,1)S(1)}, u32[]{:S(2)}, u32[]{:S(2)}) collective-permute-start(bf16[8,768]{1,0:T(8,128)(2,1)S(1)} %get-tuple-element.26), channel_id=1, source_target_pairs={{0,4},{1,5},{2,6},{3,7},{4,0},{5,1},{6,2},{7,3},{8,12},{9,13},{10,... | collective-permute-start | bytes 36872 | tf_op jit(solution)/shard_map/ppermute | solution.py:171
  9.1 37.5 %copy-start.3 = (bf16[512,768]{1,0:T(8,128)(2,1)S(1)}, bf16[512,768]{1,0:T(8,128)(2,1)}, u32[]{:S(2)}) copy-start(bf16[512,768]{1,0:T(8,128)(2,1)} %weight_ref.1) | copy-start | bytes 2359300
  11.6 8.8 %collective-permute-start.2 = (bf16[256,384]{1,0:T(8,128)(2,1)S(1)}, bf16[256,384]{1,0:T(8,128)(2,1)S(1)}, u32[]{:S(2)}, u32[]{:S(2)}) collective-permute-start(bf16[256,384]{1,0:T(8,128)(2,1)S(1)} %get-tuple-element.28), channel_id=1, source_target_pairs={{0,25},{1,17},{2,27},{3,19},{4,29},{5,21},{6,31},{7,23},{8,24},{9,... | collective-permute-start | bytes 589832 | tf_op jit(solution)/shard_map/ppermute | solution.py:338
  15.5 9.7 %collective-permute-start.5 = (bf16[256,384]{1,0:T(8,128)(2,1)S(1)}, bf16[256,384]{1,0:T(8,128)(2,1)S(1)}, u32[]{:S(2)}, u32[]{:S(2)}) collective-permute-start(bf16[256,384]{1,0:T(8,128)(2,1)S(1)} %get-tuple-element.30), channel_id=1, source_target_pairs={{0,5},{1,13},{2,7},{3,15},{4,1},{5,9},{6,3},{7,11},{8,4},{9,12},{1... | collective-permute-start | bytes 589832 | tf_op jit(solution)/shard_map/ppermute | solution.py:338
  18.9 8.3 %collective-permute-start.6 = (bf16[256,384]{1,0:T(8,128)(2,1)S(1)}, bf16[256,384]{1,0:T(8,128)(2,1)S(1)}, u32[]{:S(2)}, u32[]{:S(2)}) collective-permute-start(bf16[256,384]{1,0:T(8,128)(2,1)S(1)} %get-tuple-element.31), channel_id=1, source_target_pairs={{0,1},{1,9},{2,3},{3,11},{4,5},{5,13},{6,7},{7,15},{8,0},{9,8},{10... | collective-permute-start | bytes 589832 | tf_op jit(solution)/shard_map/ppermute | solution.py:338
  19.0 10.7 %collective-permute-start.3 = (bf16[256,384]{1,0:T(8,128)(2,1)S(1)}, bf16[256,384]{1,0:T(8,128)(2,1)S(1)}, u32[]{:S(2)}, u32[]{:S(2)}) collective-permute-start(bf16[256,384]{1,0:T(8,128)(2,1)S(1)} %get-tuple-element.29), channel_id=1, source_target_pairs={{0,29},{1,21},{2,31},{3,23},{4,25},{5,17},{6,27},{7,19},{8,28},{9,... | collective-permute-start | bytes 589832 | tf_op jit(solution)/shard_map/ppermute | solution.py:338
  20.4 14.3 %collective-permute-start.7 = (bf16[256,384]{1,0:T(8,128)(2,1)S(1)}, bf16[256,384]{1,0:T(8,128)(2,1)S(1)}, u32[]{:S(2)}, u32[]{:S(2)}) collective-permute-start(bf16[256,384]{1,0:T(8,128)(2,1)S(1)} %collective-permute-done.2.refs_0_.refs_2_), channel_id=1, source_target_pairs={{0,1},{1,0},{2,3},{3,2},{4,5},{5,4},{6,7},{7,6},{8,9},{9,8},{10,11... | collective-permute-start | bytes 589832 | tf_op jit(solution)/shard_map/ppermute | solution.py:340
  25.2 9.5 %collective-permute-start.9 = (bf16[256,384]{1,0:T(8,128)(2,1)S(1)}, bf16[256,384]{1,0:T(8,128)(2,1)S(1)}, u32[]{:S(2)}, u32[]{:S(2)}) collective-permute-start(bf16[256,384]{1,0:T(8,128)(2,1)S(1)} %collective-permute-done.5.refs_2_.refs_0_), channel_id=1, source_target_pairs={{0,1},{1,0},{2,3},{3,2},{4,5},{5,4},{6,7},{7,6},{8,9},{9,8},{10,11... | collective-permute-start | bytes 589832 | tf_op jit(solution)/shard_map/ppermute | solution.py:340
  27.2 7.5 %collective-permute-start.8 = (bf16[256,384]{1,0:T(8,128)(2,1)S(1)}, bf16[256,384]{1,0:T(8,128)(2,1)S(1)}, u32[]{:S(2)}, u32[]{:S(2)}) collective-permute-start(bf16[256,384]{1,0:T(8,128)(2,1)S(1)} %collective-permute-done.6.refs_3_.refs_1_), channel_id=1, source_target_pairs={{0,1},{1,0},{2,3},{3,2},{4,5},{5,4},{6,7},{7,6},{8,9},{9,8},{10,11... | collective-permute-start | bytes 589832 | tf_op jit(solution)/shard_map/ppermute | solution.py:340
  29.7 6.7 %collective-permute-start.4 = (bf16[256,384]{1,0:T(8,128)(2,1)S(1)}, bf16[256,384]{1,0:T(8,128)(2,1)S(1)}, u32[]{:S(2)}, u32[]{:S(2)}) collective-permute-start(bf16[256,384]{1,0:T(8,128)(2,1)S(1)} %collective-permute-done.3.refs_1_.refs_3_), channel_id=1, source_target_pairs={{0,1},{1,0},{2,3},{3,2},{4,5},{5,4},{6,7},{7,6},{8,9},{9,8},{10,11... | collective-permute-start | bytes 589832 | tf_op jit(solution)/shard_map/ppermute | solution.py:340
  36.9 7.8 %collective-permute-start.10 = (bf16[256,128]{1,0:T(8,128)(2,1)S(1)}, bf16[256,128]{1,0:T(8,128)(2,1)S(1)}, u32[]{:S(2)}, u32[]{:S(2)}) collective-permute-start(bf16[256,128]{1,0:T(8,128)(2,1)S(1)} %get-tuple-element.37), channel_id=1, source_target_pairs={{25,0},{17,1},{27,2},{19,3},{29,4},{21,5},{31,6},{23,7},{24,8},{16... | collective-permute-start | bytes 196616 | tf_op jit(solution)/shard_map/ppermute | solution.py:342
  39.1 6.9 %collective-permute-start.11 = (bf16[256,128]{1,0:T(8,128)(2,1)S(1)}, bf16[256,128]{1,0:T(8,128)(2,1)S(1)}, u32[]{:S(2)}, u32[]{:S(2)}) collective-permute-start(bf16[256,128]{1,0:T(8,128)(2,1)S(1)} %get-tuple-element.38), channel_id=1, source_target_pairs={{29,0},{21,1},{31,2},{23,3},{25,4},{17,5},{27,6},{19,7},{28,8},{20... | collective-permute-start | bytes 196616 | tf_op jit(solution)/shard_map/ppermute | solution.py:342
  41.0 5.1 %collective-permute-start.12 = (bf16[256,128]{1,0:T(8,128)(2,1)S(1)}, bf16[256,128]{1,0:T(8,128)(2,1)S(1)}, u32[]{:S(2)}, u32[]{:S(2)}) collective-permute-start(bf16[256,128]{1,0:T(8,128)(2,1)S(1)} %get-tuple-element.43), channel_id=1, source_target_pairs={{5,0},{13,1},{7,2},{15,3},{1,4},{9,5},{3,6},{11,7},{4,8},{12,9},{6... | collective-permute-start | bytes 196616 | tf_op jit(solution)/shard_map/ppermute | solution.py:342
  42.0 4.7 %collective-permute-start.13 = (bf16[256,128]{1,0:T(8,128)(2,1)S(1)}, bf16[256,128]{1,0:T(8,128)(2,1)S(1)}, u32[]{:S(2)}, u32[]{:S(2)}) collective-permute-start(bf16[256,128]{1,0:T(8,128)(2,1)S(1)} %get-tuple-element.44), channel_id=1, source_target_pairs={{1,0},{9,1},{3,2},{11,3},{5,4},{13,5},{7,6},{15,7},{0,8},{8,9},{2,... | collective-permute-start | bytes 196616 | tf_op jit(solution)/shard_map/ppermute | solution.py:342
